TPU v7x, 256 devices: a whole 4x4x8 slice. The times are simulated.
256 devices in a mesh: expert: 4 (over y), tensor: 16 (over x, z_lo, core), dp: 4 (over z_hi).
Axes of the slice: x: 4, y: 4, z: 8 (z_hi: 4, z_lo: 2; z = z_hi * 2 + z_lo), core: 2. Of those that a mesh axis runs over, the one named last changes fastest.
Arguments:
- tokens: bfloat16 [32768, 3072], P(('dp', 'expert', 'tensor')), parts along dimension 0, may hold values from -6 to 6
- routes: int32 [32768, 2], P(('dp', 'expert', 'tensor')), parts along dimension 0, may hold values from 0 to 7, as said below
- language: int32 [32768], P(('dp', 'expert', 'tensor')), parts along dimension 0, may hold values from 0 to 100
- teacher: bfloat16 [32768, 3072], P(('dp', 'expert', 'tensor')), parts along dimension 0, may hold values from -33 to 33
- router_weight: bfloat16 [3072, 8], replicated, may hold values from -0.109375 to 0.109375
- gate_weight: bfloat16 [3072, 8192], P(None, 'tensor'), may hold values from -0.109375 to 0.109375
- up_weight: bfloat16 [3072, 8192], P(None, 'tensor'), may hold values from -0.109375 to 0.109375
- down_weight: bfloat16 [8192, 3072], P('tensor'), may hold values from -0.0625 to 0.0625
Outputs:
- layer_out: bfloat16 [32768, 3072], P(('dp', 'expert', 'tensor')), parts along dimension 0
- grad_tokens: bfloat16 [32768, 3072], P(('dp', 'expert', 'tensor')), parts along dimension 0
- grad_router: float32 [12288, 8], P('dp'), parts along dimension 0
- lang_loss: float32 [404], P('dp'), parts along dimension 0
There are 4 independent parts, one for each index of `dp`. A program takes and returns all parts, laid end to end along the dimension named above; an argument that names none is the same for every part. Nothing has to cross between parts.
Inputs may be any that keep to these rules, and one draw needn't show every extreme that they name: `routes`: each row names two different experts. Among the rows of one device (aligned blocks of 128 rows) at most 32 name expert 0; in every draw each block of some run of 2048 rows starting at a multiple of it has exactly 32 such rows.
All inputs are finite; a program needn't handle non-finite values.
Results may differ from a plain program's by a relative error of at most 0.015.
Values may be sent and summed in bfloat16 or wider, within the bound.
No kernel may reach another device: no remote copies, remote signals or barrier semaphores. Data moves between devices by JAX's collectives and lax.ppermute only.
A program may use at most 128 MiB of HBM per device.

v0:
```python
import jax
import jax.numpy as jnp
from jax import lax
from jax.sharding import PartitionSpec as P

LANGS = 101


highest = lax.Precision.HIGHEST
CONTRACT_LAST = (((1,), (1,)), ((), ()))


def routing(tokens, routes, router_weight):
    logits = jnp.dot(tokens, router_weight, preferred_element_type=jnp.float32)
    first_id = routes[:, 0]
    second_id = routes[:, 1]
    chosen = jnp.logical_or(first_id == 0, second_id == 0)
    other_id = jnp.where(first_id == 0, second_id, first_id)
    columns = lax.broadcasted_iota(jnp.int32, logits.shape, 1)
    other_hot = (columns == other_id[:, None]).astype(jnp.float32)
    own_hot = (columns == 0).astype(jnp.float32)
    margin = logits[:, 0] - jnp.sum(logits * other_hot, axis=1)
    squash = jax.nn.sigmoid(margin)
    chosen_mask = chosen.astype(jnp.float32)
    return (
        chosen,
        chosen_mask * squash,
        chosen_mask * squash * (1.0 - squash),
        own_hot - other_hot,
    )


def placing_matrix(chosen, capacity):
    slot_rank = jnp.cumsum(chosen.astype(jnp.int32)) - 1
    slot_ids = lax.broadcasted_iota(jnp.int32, (chosen.shape[0], capacity), 1)
    return jnp.logical_and(slot_rank[:, None] == slot_ids, chosen[:, None]).astype(jnp.float32)


def project_rows(rows_in, gate_weight, up_weight):
    gate_part = jnp.dot(rows_in, gate_weight, preferred_element_type=jnp.float32)
    up_part = jnp.dot(rows_in, up_weight, preferred_element_type=jnp.float32)
    return jnp.stack([gate_part, up_part], 0)


def input_grads(rows_grad, rows_pre, down_weight):
    back_hidden = lax.dot_general(
        rows_grad, down_weight, CONTRACT_LAST, preferred_element_type=jnp.float32
    )
    squash = jax.nn.sigmoid(rows_pre[0])
    gate_grad = (back_hidden * rows_pre[1] * squash * (1.0 + rows_pre[0] * (1.0 - squash))).astype(
        jnp.bfloat16
    )
    up_grad = (back_hidden * rows_pre[0] * squash).astype(jnp.bfloat16)
    return jnp.stack([gate_grad, up_grad], 0)


def local(tokens, routes, language, teacher, router_weight, gate_weight, up_weight, down_weight):
    tok_rows = tokens.shape[0]
    capacity = tok_rows // 4
    all_tokens = tok_rows * lax.axis_size("expert") * lax.axis_size("tensor")
    chosen, gate_value, gate_slope, direction = routing(tokens, routes, router_weight)
    placing = placing_matrix(chosen, capacity)
    placing_half = placing.astype(jnp.bfloat16)
    token_slots = jnp.einsum(
        "tc,td->cd", placing_half, tokens, preferred_element_type=jnp.float32
    ).astype(jnp.bfloat16)
    projected_pair = project_rows(
        lax.all_gather(token_slots, "tensor", axis=0, tiled=True), gate_weight, up_weight
    )
    hidden = (jax.nn.silu(projected_pair[0]) * projected_pair[1]).astype(jnp.bfloat16)
    own_out = lax.psum_scatter(
        jnp.dot(hidden, down_weight, preferred_element_type=jnp.float32).astype(jnp.bfloat16),
        "tensor",
        scatter_dimension=0,
        tiled=True,
    ).astype(jnp.float32)
    expert_rows = jnp.einsum("tc,cd->td", placing, own_out, precision=highest)
    combined = tokens.astype(jnp.float32) + gate_value[:, None] * expert_rows
    layer_out = combined.astype(jnp.bfloat16)
    deviation = combined - teacher.astype(jnp.float32)
    loss_tok = 0.5 * jnp.mean(deviation * deviation, axis=1)
    lang_hot = (language[:, None] == lax.broadcasted_iota(jnp.int32, (tok_rows, LANGS), 1)).astype(
        jnp.float32
    )
    lang_terms = jnp.stack(
        [jnp.dot(loss_tok, lang_hot, precision=highest), jnp.sum(lang_hot, axis=0)], 0
    )
    lang_totals = lax.psum(lang_terms, ("expert", "tensor"))
    gate_dot = jnp.sum(deviation * expert_rows, axis=1)
    dlogits = (gate_dot * gate_slope)[:, None] * direction
    router_part = (
        jnp.einsum("td,te->de", tokens.astype(jnp.float32), dlogits, precision=highest) / all_tokens
    )
    expert_grad = (gate_value[:, None] * deviation).astype(jnp.bfloat16)
    grad_slots = jnp.einsum(
        "tc,td->cd", placing_half, expert_grad, preferred_element_type=jnp.float32
    ).astype(jnp.bfloat16)
    pre_grads = input_grads(
        lax.all_gather(grad_slots, "tensor", axis=0, tiled=True), projected_pair, down_weight
    )
    gate_rows = pre_grads[0]
    up_rows = pre_grads[1]
    summed = lax.dot_general(
        gate_rows, gate_weight, CONTRACT_LAST, preferred_element_type=jnp.float32
    )
    own_back = lax.psum_scatter(
        (
            summed
            + lax.dot_general(up_rows, up_weight, CONTRACT_LAST, preferred_element_type=jnp.float32)
        ).astype(jnp.bfloat16),
        "tensor",
        scatter_dimension=0,
        tiled=True,
    ).astype(jnp.float32)
    back_rows = jnp.einsum("tc,cd->td", placing, own_back, precision=highest)
    router_back = jnp.einsum(
        "te,de->td", dlogits, router_weight.astype(jnp.float32), precision=highest
    )
    grad_tokens = (deviation + back_rows + router_back).astype(jnp.bfloat16)
    grad_router = lax.psum(router_part, ("expert", "tensor"))
    lang_loss = lang_totals[0] / jnp.maximum(lang_totals[1], 1.0)
    return (layer_out, grad_tokens, grad_router, lang_loss)


def solution(mesh):
    return jax.shard_map(
        local,
        mesh=mesh,
        in_specs=(
            P(("dp", "expert", "tensor"), None),
            P(("dp", "expert", "tensor"), None),
            P(("dp", "expert", "tensor")),
            P(("dp", "expert", "tensor"), None),
            P(),
            P(None, "tensor"),
            P(None, "tensor"),
            P("tensor", None),
        ),
        out_specs=(
            P(("dp", "expert", "tensor"), None),
            P(("dp", "expert", "tensor"), None),
            P("dp", None),
            P("dp"),
        ),
        check_vma=False,
    )
```

profile of v0, /device:TPU:64, one launch (start us, length us, event | category | flops | bytes accessed | tf_op | source)
XLA Modules:
  0.0 817.9 jit_solution(11641941166505160650)
XLA Ops:
  7.2 0.9 fusion.28
  8.1 1.5 select_reduce_fusion
  9.6 0.8 fusion.34
  10.4 0.1 copy.14
  10.5 0.2 reduce-window.8
  10.7 0.1 add_reduce_fusion
  10.8 2.2 convolution_convert_fusion.2
  13.0 0.0 reduce-scatter.3.cloned.1.call-start
  13.0 40.7 %all-gather.3.cloned.1.call-done = bf16[512,3072]{1,0:T(8,128)(2,1)} async-done(((bf16[32,3072]{1,0:T(8,128)(2,1)}), bf16[512,3072]{1,0:T(8,128)(2,1)}) %all-gather.3.cloned.1.call-update) | async-done | bytes 3145744 | tf_op jit(solution)/shard_map/all_gather | solution.py:68
  53.7 4.8 fusion.39
  58.5 1.8 fusion.40
  60.3 1.0 copy-done.7
  61.3 3.5 convolution_convert_fusion
  64.8 69.7 %reduce-scatter.3.cloned.1.call-done = bf16[32,3072]{1,0:T(8,128)(2,1)} async-done(((bf16[512,3072]{1,0:T(8,128)(2,1)}), bf16[32,3072]{1,0:T(8,128)(2,1)}) %reduce-scatter.3.cloned.1.call-update) | async-done | bytes 196624 | tf_op jit(solution)/shard_map/reduce_scatter | solution.py:71
  134.6 3.0 multiply_reduce_fusion
  137.6 1.2 copy-done.1
  138.8 1.0 convolution_convert_fusion.1
  139.9 36.8 %all-gather.5.cloned.1.call-done = bf16[512,3072]{1,0:T(8,128)(2,1)} async-done(((bf16[32,3072]{1,0:T(8,128)(2,1)}), bf16[512,3072]{1,0:T(8,128)(2,1)}) %all-gather.5.cloned.1.call-update) | async-done | bytes 3145744 | tf_op jit(solution)/shard_map/all_gather | solution.py:99
  176.7 3.9 fusion.41
  180.6 2.1 fusion.4
  182.7 3.5 add_convert_fusion
  186.3 0.6 copy-done.11
  186.9 0.1 convert_reduce_fusion
  187.0 0.1 fusion.12
  187.1 0.1 pad_maximum_fusion
  187.2 142.6 %psum.15 = f32[2,101]{1,0:T(2,128)S(1)} all-reduce(f32[2,101]{1,0:T(2,128)S(1)} %pad_maximum_fusion), channel_id=1, replica_groups=mesh['expert'=4,'tensor'=16,'dp'=4] {'expert','tensor'}, use_global_device_ids=true, to_apply=%region_8.9 | all-reduce | flops 202 | bytes 1616 | tf_op jit(solution)/shard_map/psum | solution.py:88
  329.8 0.5 fusion.32
  330.4 2.2 fusion.1
  332.7 1.9 convolution_add_fusion.1
  334.6 1.8 fusion
  336.4 473.5 %all-reduce.2.cloned.1.call-done = f32[3072,8]{0,1:T(8,128)} async-done(((f32[3072,8]{0,1:T(8,128)}), f32[3072,8]{0,1:T(8,128)}) %all-reduce.2.cloned.1.call-update) | async-done | bytes 98320 | tf_op jit(solution)/shard_map/psum | solution.py:120
  809.9 1.5 copy.16
  (34 shorter events, 0.3 us)
Async XLA Ops:
  7.2 54.1 %copy-start = (bf16[512,3072]{1,0:T(8,128)(2,1)S(1)}, bf16[512,3072]{1,0:T(8,128)(2,1)}, u32[]{:S(2)}) copy-start(bf16[512,3072]{1,0:T(8,128)(2,1)} %param.15) | copy-start | bytes 9437188
  7.2 46.5 %all-gather.3.cloned.1.call-start = ((), (), s32[]{:S(2)}) async-start(), calls=%async_computation.2 | async-start | bytes 3342336 | tf_op jit(solution)/shard_map/all_gather | solution.py:68
  13.0 121.6 %reduce-scatter.3.cloned.1.call-start = ((), (), s32[]{:S(2)}) async-start(), calls=%async_computation.3 | async-start | bytes 3342336 | tf_op jit(solution)/shard_map/reduce_scatter | solution.py:71
  53.7 4.8 copy-start.4
  53.7 4.8 copy-start.10
  58.5 1.8 copy-start.2
  60.3 1.0 copy-start.7
  64.8 111.9 %all-gather.5.cloned.1.call-start = ((), (), s32[]{:S(2)}) async-start(), calls=%async_computation.4 | async-start | bytes 3342336 | tf_op jit(solution)/shard_map/all_gather | solution.py:99
  137.6 1.2 copy-start.1
  139.8 192.8 %reduce-scatter.5.cloned.1.call-start = ((), (), s32[]{:S(2)}) async-start(), calls=%async_computation.5 | async-start | bytes 3342336 | tf_op jit(solution)/shard_map/reduce_scatter | solution.py:106
  176.7 3.9 copy-start.3
  176.7 3.9 copy-start.6
  176.7 3.9 copy-start.8
  180.6 2.1 copy-start.5
  186.2 0.7 copy-start.11
  186.2 148.4 %copy-start.9 = (bf16[3072,8]{0,1:T(8,128)(2,1)S(1)}, bf16[3072,8]{0,1:T(8,128)(2,1)}, u32[]{:S(2)}) copy-start(bf16[3072,8]{0,1:T(8,128)(2,1)} %param.12) | copy-start | bytes 147460
  186.3 623.6 %all-reduce.2.cloned.1.call-start = ((), (), s32[]{:S(2)}) async-start(), calls=%async_computation.6 | async-start | bytes 196608 | tf_op jit(solution)/shard_map/psum | solution.py:120
Sparse Core Ops, SparseCore 0:
  13.1 40.5 all-gather.2
  64.9 69.6 reduce-scatter.2
  140.0 36.6 all-gather.4
  186.4 69.9 reduce-scatter.4
  332.8 477.0 all-reduce.1
where the time goes:
time: 818 us
  waiting for transfers between devices  621 us (76%)
  blocking collectives  143 us (17%)
  matrix products  33.4 us (4%)
  between operations  13.9 us (2%)
    psum x1, waiting for transfers between devices, local(): grad_router = lax.psum(router_part, ('expert', 'tensor'))  473 us
    psum x1, blocking collectives, local(): lang_totals = lax.psum(lang_terms, ('expert', 'tensor'))  143 us
    reduce_scatter x1, waiting for transfers between devices, local(): lax.psum_scatter(jnp.dot(hidden, down_weight, preferred_element_type=jnp....  69.7 us
    all_gather x1, waiting for transfers between devices, local(): lax.all_gather(token_slots, 'tensor', axis=0, tiled=True)  40.7 us
    all_gather x1, waiting for transfers between devices, local(): lax.all_gather(grad_slots, 'tensor', axis=0, tiled=True)  36.8 us
  transfers between devices with their start and end apart: 5, of which 4 were waited for; matrix products, arithmetic and copies ran while one was open for 1% of the time, Pallas kernels for 0%

commit v1 on v0

v1 whole, which is shorter than its diff:
```python
import functools

import jax
import jax.numpy as jnp
from jax import lax
from jax.experimental import pallas as pl
from jax.experimental.pallas import tpu as pltpu
from jax.sharding import Mesh
from jax.sharding import PartitionSpec as P

LANGS = 101
LANES = 128
TILE = 256
BLOCKS = 8
PLANE = 4
NT = (((1,), (1,)), ((), ()))
TN = (((0,), (0,)), ((), ()))
f32 = jnp.float32
bf16 = jnp.bfloat16
GROUP = ("x", "z", "core", "dp")


def move(value, target):
    pairs = []
    for x in range(4):
        for z in range(8):
            for c in range(2):
                tx, tz, tc = target(x, z, c)
                spots = [((px % 4 * 2 + pz % 2) * 2 + pc) * 4 + pz % 8 // 2 for px, pz, pc in ((x, z, c), (tx, tz, tc))]
                pairs.append(tuple(spots))
    return lax.ppermute(value, GROUP, pairs)


def facing(z, c):
    return z + 1 - 2 * ((z + c) % 2)


def ahead(value):
    return move(value, lambda x, z, c: (x + 1 - 2 * c, z, c))


def behind(value):
    return move(value, lambda x, z, c: (x - 1 + 2 * c, z, c))


def across(value):
    return move(value, lambda x, z, c: (x, facing(z, c), c))


def ahead_across(value):
    return move(value, lambda x, z, c: (x + 1 - 2 * c, facing(z, c), c))


def behind_across(value):
    return move(value, lambda x, z, c: (x - 1 + 2 * c, facing(z, c), c))


def twin(value):
    return move(value, lambda x, z, c: (x, z, 1 - c))


def pair(value):
    return move(value, lambda x, z, c: (x, z + 1 - 2 * (z % 2), c))


def after(value, *others):
    return lax.optimization_barrier((value, *others))[0]


def gather(own):
    f1 = ahead(own)
    zb1 = behind_across(own)
    b1 = behind(own)
    z0 = across(own)
    zf1 = ahead_across(own)
    x2 = ahead(f1)
    zx2 = behind(zb1)
    return [own, f1, b1, x2, z0, zf1, zb1, zx2]


def add(*parts):
    return sum(p.astype(f32) for p in parts).astype(bf16)


def scatter(terms):
    own, f1, b1, x2, z0, zf1, zb1, zx2 = terms
    got_zx2 = ahead_across(zx2)
    got_x2 = behind(x2)
    got_zf1 = across(zf1)
    got_zb1 = across(zb1)
    got_z0 = across(z0)
    got_f1 = behind(add(f1, got_x2, got_zf1))
    got_b1 = ahead(add(b1, got_zb1, got_zx2))
    return [own, got_z0, got_f1, got_b1]


def stack_rows(blocks, rows):
    each, width = blocks[0].shape[0], rows.shape[1]
    for b, block in enumerate(blocks):
        rows[b * each : (b + 1) * each] = block[:, :width]


VMEM = pl.BlockSpec(memory_space=pltpu.VMEM)


def hidden_kernel(*refs):
    blocks, gates, ups = refs[:BLOCKS], refs[BLOCKS : BLOCKS + 2], refs[BLOCKS + 2 : BLOCKS + 4]
    hidden, pre_gate, pre_up, rows = refs[BLOCKS + 4 :]
    half = gates[0].shape[1]
    stack_rows(blocks, rows)
    for t in range(2 * half // TILE):
        which, col = t * TILE // half, t * TILE % half
        gate = jnp.dot(rows[...], gates[which][:, col : col + TILE], preferred_element_type=f32)
        up = jnp.dot(rows[...], ups[which][:, col : col + TILE], preferred_element_type=f32)
        pre_gate[:, t * TILE : (t + 1) * TILE] = gate
        pre_up[:, t * TILE : (t + 1) * TILE] = up
        hidden[:, t * TILE : (t + 1) * TILE] = (gate * jax.nn.sigmoid(gate) * up).astype(bf16)


def hidden_units(blocks, gates, ups):
    width, half = gates[0].shape
    rows = BLOCKS * blocks[0].shape[0]
    return pl.pallas_call(
        hidden_kernel,
        name="hidden_units",
        out_shape=[jax.ShapeDtypeStruct((rows, 2 * half), kind) for kind in (bf16, f32, f32)],
        in_specs=[VMEM] * (BLOCKS + 4),
        out_specs=[VMEM] * 3,
        scratch_shapes=[pltpu.VMEM((rows, width), bf16)],
        compiler_params=pltpu.CompilerParams(vmem_limit_bytes=20 << 20),
        cost_estimate=pl.CostEstimate(flops=8 * rows * width * half, bytes_accessed=8 * width * half, transcendentals=2 * rows * half),
    )(*blocks, *gates, *ups)


def slot_term_kernel(*refs):
    hidden, downs, outs = refs[0], refs[1:3], refs[3:]
    each, width = outs[0].shape
    half = downs[0].shape[0]
    for n in range(width // TILE):
        cols = pl.ds(n * TILE, TILE)
        total = jnp.dot(hidden[:, :half], downs[0][:, cols], preferred_element_type=f32)
        total = total + jnp.dot(hidden[:, half:], downs[1][:, cols], preferred_element_type=f32)
        part = total.astype(bf16)
        for b in range(BLOCKS):
            outs[b][:, cols] = part[b * each : (b + 1) * each]


def slot_terms(hidden, downs):
    rows = hidden.shape[0]
    half, width = downs[0].shape
    return pl.pallas_call(
        slot_term_kernel,
        name="slot_terms",
        out_shape=[jax.ShapeDtypeStruct((rows // BLOCKS, width), bf16)] * BLOCKS,
        in_specs=[VMEM] * 3,
        out_specs=[VMEM] * BLOCKS,
        compiler_params=pltpu.CompilerParams(vmem_limit_bytes=20 << 20),
        cost_estimate=pl.CostEstimate(flops=4 * rows * width * half, bytes_accessed=4 * width * half, transcendentals=0),
    )(hidden, *downs)


def hidden_grad_kernel(*refs):
    blocks, downs = refs[:BLOCKS], refs[BLOCKS : BLOCKS + 2]
    pre_gate, pre_up, gate_grad, up_grad, rows = refs[BLOCKS + 2 :]
    half = downs[0].shape[0]
    stack_rows(blocks, rows)
    for t in range(2 * half // TILE):
        which, row = t * TILE // half, t * TILE % half
        back = lax.dot_general(rows[...], downs[which][row : row + TILE, :], NT, preferred_element_type=f32)
        gate = pre_gate[:, t * TILE : (t + 1) * TILE]
        up = pre_up[:, t * TILE : (t + 1) * TILE]
        squash = jax.nn.sigmoid(gate)
        gate_grad[:, t * TILE : (t + 1) * TILE] = (back * up * squash * (1.0 + gate * (1.0 - squash))).astype(bf16)
        up_grad[:, t * TILE : (t + 1) * TILE] = (back * gate * squash).astype(bf16)


def hidden_grads(blocks, downs, pre_gate, pre_up):
    half, width = downs[0].shape
    rows = pre_gate.shape[0]
    return pl.pallas_call(
        hidden_grad_kernel,
        name="hidden_grads",
        out_shape=[jax.ShapeDtypeStruct((rows, 2 * half), bf16)] * 2,
        in_specs=[VMEM] * (BLOCKS + 4),
        out_specs=[VMEM] * 2,
        scratch_shapes=[pltpu.VMEM((rows, width), bf16)],
        compiler_params=pltpu.CompilerParams(vmem_limit_bytes=20 << 20),
        cost_estimate=pl.CostEstimate(flops=4 * rows * width * half, bytes_accessed=4 * width * half, transcendentals=2 * rows * half),
    )(*blocks, *downs, pre_gate, pre_up)


def slot_grad_kernel(*refs):
    gate_grad, up_grad = refs[:2]
    gates, ups, outs = refs[2:4], refs[4:6], refs[6:]
    each = outs[0].shape[0]
    width, half = gates[0].shape
    for n in range(width // TILE):
        cols = pl.ds(n * TILE, TILE)
        total = None
        for which in range(2):
            for grad, weights in ((gate_grad, gates), (up_grad, ups)):
                term = lax.dot_general(grad[:, which * half : (which + 1) * half], weights[which][cols, :], NT, preferred_element_type=f32)
                total = term if total is None else total + term
        part = total.astype(bf16)
        for b in range(BLOCKS):
            outs[b][:, cols] = part[b * each : (b + 1) * each]


def slot_grads(gate_grad, up_grad, gates, ups):
    width, half = gates[0].shape
    rows = gate_grad.shape[0]
    return pl.pallas_call(
        slot_grad_kernel,
        name="slot_grads",
        out_shape=[jax.ShapeDtypeStruct((rows // BLOCKS, width), bf16)] * BLOCKS,
        in_specs=[VMEM] * 6,
        out_specs=[VMEM] * BLOCKS,
        compiler_params=pltpu.CompilerParams(vmem_limit_bytes=20 << 20),
        cost_estimate=pl.CostEstimate(flops=8 * rows * width * half, bytes_accessed=8 * width * half, transcendentals=0),
    )(gate_grad, up_grad, *gates, *ups)


def three(value):
    high = value.astype(bf16).astype(f32)
    rest = value - high
    mid = rest.astype(bf16).astype(f32)
    return high, mid, rest - mid


SHIFT = 4


def slot_kernel(*refs):
    terms = refs[:4]
    tokens, teacher, aux, langs, base, router, combined_ref, grad_ref, so_far_ref = refs[4:]
    width = tokens.shape[1]
    aux = aux[...]
    gate_value, gate_slope, other = aux[:, 0:1], aux[:, 1:2], aux[:, 2:3]
    total = terms[0][...].astype(f32)
    for t in terms[1:]:
        total = total + t[...].astype(f32)
    combined = tokens[...].astype(f32) + gate_value * total
    combined_ref[...] = combined.astype(bf16)
    deviation = combined - teacher[...].astype(f32)
    grad_ref[:, :width] = (gate_value * deviation).astype(bf16)
    loss = jnp.sum(deviation * deviation, axis=1, keepdims=True) * (0.5 / width)
    dot = jnp.sum(deviation * total, axis=1, keepdims=True) * gate_slope
    lang_sums = base[0:1, :] + jnp.sum(loss * langs[...], axis=0, keepdims=True)
    rows = lax.broadcasted_iota(jnp.int32, langs.shape, 0)
    lanes = lax.broadcasted_iota(jnp.int32, langs.shape, 1)
    extra = jnp.zeros(langs.shape, f32)
    for i, (d, s) in enumerate(zip(three(dot) + (other,), three(lang_sums) + (base[1:2, :],))):
        extra = jnp.where(lanes == i, d, extra)
        extra = jnp.where(jnp.logical_and(rows == i, lanes >= SHIFT), s, extra)
    grad_ref[:, width:] = extra.astype(bf16)
    back = deviation
    columns = lax.broadcasted_iota(jnp.int32, (tokens.shape[0], router.shape[0]), 1)
    direction = (columns == 0).astype(f32) - (columns.astype(f32) == other).astype(f32)
    for part in three(dot):
        back = back + jnp.dot((part * direction).astype(bf16), router[...], preferred_element_type=f32)
    so_far_ref[...] = back


def slots(terms, tokens, teacher, aux, langs, base, router):
    each, width = tokens.shape
    return pl.pallas_call(
        slot_kernel,
        name="slot_step",
        out_shape=[
            jax.ShapeDtypeStruct((each, width), bf16),
            jax.ShapeDtypeStruct((each, width + LANES), bf16),
            jax.ShapeDtypeStruct((each, width), f32),
        ],
        in_specs=[VMEM] * 10,
        out_specs=[VMEM] * 3,
        compiler_params=pltpu.CompilerParams(vmem_limit_bytes=8 << 20),
        cost_estimate=pl.CostEstimate(flops=30 * each * width, bytes_accessed=24 * each * width, transcendentals=0),
    )(*terms, tokens, teacher, aux, langs, base, router)


def router_kernel(*refs):
    token_blocks, grad_blocks = refs[:PLANE], refs[PLANE : 2 * PLANE]
    out, rows = refs[2 * PLANE :]
    experts = out.shape[0]
    width = rows.shape[1]
    stack_rows(token_blocks, rows)
    each = token_blocks[0].shape[0]
    lanes = lax.broadcasted_iota(jnp.int32, (each, LANES), 1)
    expert = lanes % experts
    slopes, langs = [], jnp.zeros((each, LANES), f32)
    for b in range(PLANE):
        extra = grad_blocks[b][:, width:].astype(f32)
        langs = langs + extra
        other = extra[:, 3:4]
        direction = (expert == 0).astype(f32) - (expert.astype(f32) == other).astype(f32)
        part = jnp.where(lanes < experts, extra[:, 0:1], jnp.where(lanes < 2 * experts, extra[:, 1:2], extra[:, 2:3]))
        slopes.append(jnp.where(lanes < 3 * experts, part * direction, 0.0).astype(bf16))
    sums = lax.dot_general(jnp.concatenate(slopes, 0), rows[...], TN, preferred_element_type=f32)
    out[:, :width] = sums[:experts] + sums[experts : 2 * experts] + sums[2 * experts : 3 * experts]
    sub = lax.broadcasted_iota(jnp.int32, (experts, LANES), 0)
    out[:, width:] = jnp.where(sub == 0, langs[0:1] + langs[1:2] + langs[2:3], jnp.where(sub == 1, langs[3:4], 0.0))


def router_sum(token_blocks, grad_blocks, experts):
    each, width = token_blocks[0].shape
    return pl.pallas_call(
        router_kernel,
        name="router_sum",
        out_shape=jax.ShapeDtypeStruct((experts, width + LANES), f32),
        in_specs=[VMEM] * (2 * PLANE),
        out_specs=VMEM,
        scratch_shapes=[pltpu.VMEM((PLANE * each, width), bf16)],
        compiler_params=pltpu.CompilerParams(vmem_limit_bytes=12 << 20),
        cost_estimate=pl.CostEstimate(flops=2 * 128 * 128 * 3072, bytes_accessed=4 * 128 * 3072, transcendentals=0),
    )(*token_blocks, *grad_blocks)


def place_kernel(routes, tokens, placing_ref, slots_ref):
    rows = tokens.shape[0]
    capacity = slots_ref.shape[0]
    chosen = jnp.logical_or(routes[0:1, :] == 0, routes[1:2, :] == 0).astype(f32)
    upper = lax.broadcasted_iota(jnp.int32, (rows, rows), 0) <= lax.broadcasted_iota(jnp.int32, (rows, rows), 1)
    many = jnp.broadcast_to(chosen, (8, rows)).astype(bf16)
    rank = jnp.dot(many, upper.astype(bf16), preferred_element_type=f32)[0:1, :] - 1.0
    slot_ids = lax.broadcasted_iota(jnp.int32, (capacity, rows), 0).astype(f32)
    placing = jnp.where(rank == slot_ids, chosen, 0.0)
    placing_ref[...] = placing
    slots_ref[...] = jnp.dot(placing.astype(bf16), tokens[...], preferred_element_type=f32).astype(bf16)


def place(routes, tokens):
    rows, width = tokens.shape
    return pl.pallas_call(
        place_kernel,
        name="place_tokens",
        out_shape=[jax.ShapeDtypeStruct((rows // 4, rows), f32), jax.ShapeDtypeStruct((rows // 4, width), bf16)],
        in_specs=[VMEM] * 2,
        out_specs=[VMEM] * 2,
        compiler_params=pltpu.CompilerParams(vmem_limit_bytes=8 << 20),
        cost_estimate=pl.CostEstimate(flops=2 * 32 * rows * width, bytes_accessed=3 * rows * width, transcendentals=0),
    )(routes, tokens)


def local(tokens, routes, language, teacher, router_weight, gate_weight, up_weight, down_weight):
    tok_rows, width = tokens.shape
    capacity = tok_rows // 4
    experts = router_weight.shape[1]
    all_tokens = tok_rows * 64
    first_id = routes[:, 0]
    second_id = routes[:, 1]
    chosen = jnp.logical_or(first_id == 0, second_id == 0)
    other_id = jnp.where(first_id == 0, second_id, first_id).astype(f32)
    placing, token_slots = place(routes.T, tokens)
    placing_half = placing.astype(bf16)

    token_blocks = gather(token_slots)
    gates = [gate_weight, twin(after(gate_weight, token_slots))]
    ups = [up_weight, twin(after(up_weight, token_slots))]
    downs = [down_weight, twin(after(down_weight, gates[1], token_blocks[1], token_blocks[2]))]
    tokens, teacher = lax.optimization_barrier((tokens, teacher, token_slots))[:2]

    teacher_slots = jnp.dot(placing_half, teacher, preferred_element_type=f32).astype(bf16)
    logits = jnp.dot(token_slots, router_weight, preferred_element_type=f32)
    other_slots = jnp.sum(placing * other_id[None, :], axis=1)
    filled = jnp.sum(placing, axis=1)
    columns = lax.broadcasted_iota(jnp.int32, logits.shape, 1).astype(f32)
    other_hot = (columns == other_slots[:, None]).astype(f32)
    squash = jax.nn.sigmoid(logits[:, 0] - jnp.sum(logits * other_hot, axis=1))
    gate_value = filled * squash
    gate_slope = filled * squash * (1.0 - squash)
    aux_lane = lax.broadcasted_iota(jnp.int32, (capacity, LANES), 1)
    aux = jnp.where(aux_lane == 0, gate_value[:, None], jnp.where(aux_lane == 1, gate_slope[:, None], other_slots[:, None]))
    plain = tokens.astype(f32) - teacher.astype(f32)
    plain_grad = plain.astype(bf16)
    plain_loss = jnp.where(chosen, 0.0, 0.5 * jnp.mean(plain * plain, axis=1))
    lang_hot = (language[:, None] + SHIFT == lax.broadcasted_iota(jnp.int32, (tok_rows, LANES), 1)).astype(f32)
    slot_langs = jnp.dot(placing_half, lang_hot.astype(bf16), preferred_element_type=f32)
    sub = lax.broadcasted_iota(jnp.int32, (8, LANES), 0)
    base = jnp.where(sub == 0, jnp.sum(plain_loss[:, None] * lang_hot, axis=0)[None, :], jnp.sum(lang_hot, axis=0)[None, :])

    hidden, pre_gate, pre_up = hidden_units(token_blocks, gates, ups)
    terms = slot_terms(hidden, downs)
    combined, grad_slots, so_far = slots(scatter(terms), token_slots, teacher_slots, aux, slot_langs, base, router_weight.T)
    grad_blocks = gather(grad_slots)
    placed = lax.dot_general(placing_half, combined, TN, preferred_element_type=f32)
    layer_out = jnp.where(chosen[:, None], placed.astype(bf16), tokens)

    summed = router_sum(token_blocks[:PLANE], grad_blocks[:PLANE], experts)
    summed = summed + twin(summed)
    gate_grad, up_grad = hidden_grads(grad_blocks, downs, after(pre_gate, summed), pre_up)
    summed = summed + lax.ppermute(summed, "expert", [(i, i ^ 1) for i in range(4)])
    back_terms = slot_grads(after(gate_grad, summed), up_grad, gates, ups)
    summed = summed + lax.ppermute(summed, "expert", [(i, i ^ 2) for i in range(4)])
    summed = summed + pair(summed)
    grad_router = summed[:, :width].T / all_tokens
    lang_loss = (summed[0, width:] / jnp.maximum(summed[1, width:], 1.0))[SHIFT : SHIFT + LANGS]

    own_back = sum(t.astype(f32) for t in scatter(list(back_terms)))
    slot_grad = (so_far + own_back).astype(bf16)
    placed_grad = lax.dot_general(placing_half, slot_grad, TN, preferred_element_type=f32)
    grad_tokens = jnp.where(chosen[:, None], placed_grad.astype(bf16), plain_grad)
    return (layer_out, grad_tokens, grad_router, lang_loss)


def solution(mesh):
    wide = Mesh(mesh.devices.reshape(4, 4, 2, 2, 4), ("expert", "x", "z", "core", "dp"))
    rows = ("dp", "expert", "x", "z", "core")
    hidden = ("x", "z", "core")
    return jax.shard_map(
        local,
        mesh=wide,
        in_specs=(
            P(rows, None),
            P(rows, None),
            P(rows),
            P(rows, None),
            P(),
            P(None, hidden),
            P(None, hidden),
            P(hidden, None),
        ),
        out_specs=(P(rows, None), P(rows, None), P("dp", None), P("dp")),
        check_vma=False,
    )
```

time: 818 us -> 118 us (0.14)
  the two profiles are of different devices: /device:TPU:64 before, /device:TPU:1 now
where the time goes in v1:
time: 118 us
  starting transfers between devices  67.7 us (57%)
  waiting for transfers between devices  24.6 us (21%)
  Pallas kernels  12.2 us (10%)
  matrix products  5.13 us (4%)
  local copies, waits for them, and re-layouts  4.3 us (4%)
  other arithmetic  3.14 us (3%)
    ppermute x33, starting transfers between devices, move(): return lax.ppermute(value, GROUP, pairs)  63 us
    ppermute x33, waiting for transfers between devices, move(): return lax.ppermute(value, GROUP, pairs)  24.5 us
    unnamed x20, local copies, waits for them, and re-layouts  3.72 us
    pallas_call x1, Pallas kernels, slot_grads(): pl.pallas_call(slot_grad_kernel, name='slot_grads', out_shape=[jax.ShapeD...  3.44 us
    pallas_call x1, Pallas kernels, hidden_units(): pl.pallas_call(hidden_kernel, name='hidden_units', out_shape=[jax.ShapeDt...  3.41 us
    ppermute x1, starting transfers between devices, local(): lax.ppermute(summed, 'expert', [(i, i ^ 2) for i in range(4)])  3 us
  transfers between devices with their start and end apart: 35, of which 14 were waited for; matrix products, arithmetic and copies ran while one was open for 6% of the time, Pallas kernels for 8%

profile of v1, /device:TPU:1, one launch (start us, length us, event | category | flops | bytes accessed | tf_op | source)
XLA Modules:
  0.0 118.0 jit_solution(18149897010686072832)
XLA Ops:
  2.8 3.3 %collective-permute-start.7 = (bf16[3072,512]{1,0:T(8,128)(2,1)}, bf16[3072,512]{1,0:T(8,128)(2,1)S(1)}, u32[]{:S(2)}, u32[]{:S(2)}) collective-permute-start(bf16[3072,512]{1,0:T(8,128)(2,1)} %refs_2_.1), channel_id=1, source_target_pairs={{0,4},{4,0},{8,12},{12,8},{1,5},{5,1},{9,13},{13,9},{2,6},{6,2},{1... | collective-permute-start | bytes 9437192 | tf_op jit(solution)/shard_map/ppermute | solution.py:31
  6.3 2.7 %collective-permute-start = (bf16[32,3072]{1,0:T(8,128)(2,1)S(1)}, bf16[32,3072]{1,0:T(8,128)(2,1)S(1)}, u32[]{:S(2)}, u32[]{:S(2)}) collective-permute-start(bf16[32,3072]{1,0:T(8,128)(2,1)S(1)} %get-tuple-element.38.refs_0_.refs_4_), channel_id=1, source_target_pairs={{0,16},{4,52},{8,24},{12,60},{1,17},{5,53},{9,25},{13,61},{2,18},{... | collective-permute-start | bytes 589832 | tf_op jit(solution)/shard_map/ppermute | solution.py:31
  8.9 3.5 %collective-permute-done.1.refs_2_ = bf16[32,3072]{1,0:T(8,128)(2,1)S(1)} collective-permute-done((bf16[32,3072]{1,0:T(8,128)(2,1)S(1)}, bf16[32,3072]{1,0:T(8,128)(2,1)S(1)}, u32[]{:S(2)}, u32[]{:S(2)}) %collective-permute-start.1) | collective-permute-done | bytes 196640 | tf_op jit(solution)/shard_map/ppermute | solution.py:31
  12.6 2.2 %collective-permute-start.9 = (bf16[512,3072]{1,0:T(8,128)(2,1)}, bf16[512,3072]{1,0:T(8,128)(2,1)S(1)}, u32[]{:S(2)}, u32[]{:S(2)}) collective-permute-start(bf16[512,3072]{1,0:T(8,128)(2,1)} %refs_8_.3), channel_id=1, source_target_pairs={{0,4},{4,0},{8,12},{12,8},{1,5},{5,1},{9,13},{13,9},{2,6},{6,2},{1... | collective-permute-start | bytes 9437192 | tf_op jit(solution)/shard_map/ppermute | solution.py:31
  14.8 4.1 %collective-permute-start.5 = (bf16[32,3072]{1,0:T(8,128)(2,1)S(1)}, bf16[32,3072]{1,0:T(8,128)(2,1)S(1)}, u32[]{:S(2)}, u32[]{:S(2)}) collective-permute-start(bf16[32,3072]{1,0:T(8,128)(2,1)S(1)} %get-tuple-element.38.refs_0_.refs_4_), channel_id=1, source_target_pairs={{0,56},{4,31},{8,48},{12,21},{1,57},{5,28},{9,49},{13,22},{2,58},{... | collective-permute-start | bytes 589832 | tf_op jit(solution)/shard_map/ppermute | solution.py:31
  18.9 2.2 %collective-permute-start.4 = (bf16[32,3072]{1,0:T(8,128)(2,1)S(1)}, bf16[32,3072]{1,0:T(8,128)(2,1)S(1)}, u32[]{:S(2)}, u32[]{:S(2)}) collective-permute-start(bf16[32,3072]{1,0:T(8,128)(2,1)S(1)} %get-tuple-element.38.refs_0_.refs_4_), channel_id=1, source_target_pairs={{0,24},{4,63},{8,16},{12,53},{1,25},{5,60},{9,17},{13,54},{2,26},{... | collective-permute-start | bytes 589832 | tf_op jit(solution)/shard_map/ppermute | solution.py:31
  21.0 3.9 %collective-permute-start.3 = (bf16[32,3072]{1,0:T(8,128)(2,1)S(1)}, bf16[32,3072]{1,0:T(8,128)(2,1)S(1)}, u32[]{:S(2)}, u32[]{:S(2)}) collective-permute-start(bf16[32,3072]{1,0:T(8,128)(2,1)S(1)} %get-tuple-element.38.refs_0_.refs_4_), channel_id=1, source_target_pairs={{0,8},{4,15},{8,0},{12,5},{1,9},{5,12},{9,1},{13,6},{2,10},{6,13},... | collective-permute-start | bytes 589832 | tf_op jit(solution)/shard_map/ppermute | solution.py:31
  24.9 1.7 %multiply_reduce_fusion = f32[128]{0:T(128)S(1)} fusion(bf16[128,3072]{1,0:T(8,128)(2,1)} %param.11, bf16[128,3072]{1,0:T(8,128)(2,1)} %tokens.1), kind=kLoop, calls=%fused_computation.5 | loop fusion | flops 1965952 | bytes 1573376 | tf_op jit(solution)/shard_map/reduce_sum | solution.py:375
  31.1 4.4 %collective-permute-done.6.refs_7_ = bf16[32,3072]{1,0:T(8,128)(2,1)S(1)} collective-permute-done((bf16[32,3072]{1,0:T(8,128)(2,1)S(1)}, bf16[32,3072]{1,0:T(8,128)(2,1)S(1)}, u32[]{:S(2)}, u32[]{:S(2)}) %collective-permute-start.6) | collective-permute-done | bytes 196640 | tf_op jit(solution)/shard_map/ppermute | solution.py:31
  35.5 1.9 %copy-done.2 = bf16[3072,512]{1,0:T(8,128)(2,1)S(1)} copy-done((bf16[3072,512]{1,0:T(8,128)(2,1)S(1)}, bf16[3072,512]{1,0:T(8,128)(2,1)}, u32[]{:S(2)}) %copy-start.2) | copy-done | bytes 3145752
  37.3 3.4 %hidden_units.1 = (bf16[256,1024]{1,0:T(8,128)(2,1)S(1)}, f32[256,1024]{1,0:T(8,128)S(1)}, f32[256,1024]{1,0:T(8,128)S(1)}) custom-call(bf16[32,3072]{1,0:T(8,128)(2,1)S(1)} %get-tuple-element.38.refs_0_.refs_4_, bf16[32,3072]{1,0:T(8,128)(2,1)S(1)} %collective-permute-done.refs_1_, bf16[32,3072]{1,0:T(8,128)(2,1)S(1)} %collective-permute-done.1.refs_2_, ...), custom_call_target="tpu_custom_call" | custom-call | flops 3221225472 | bytes 12582912 | tf_op jit(solution)/shard_map/hidden_units/pallas_call | solution.py:123
  40.8 1.8 %slot_terms.1 = (bf16[32,3072]{1,0:T(8,128)(2,1)S(1)}, bf16[32,3072]{1,0:T(8,128)(2,1)S(1)}, bf16[32,3072]{1,0:T(8,128)(2,1)S(1)}, bf16[32,3072]{1,0:T(8,128)(2,...) custom-call(bf16[256,1024]{1,0:T(8,128)(2,1)S(1)} %get-tuple-element, ...), custom_call_target="tpu_custom_call" | custom-call | flops 1610612736 | bytes 6291456 | tf_op jit(solution)/shard_map/slot_terms/pallas_call | solution.py:151
  45.8 1.6 %collective-permute-start.14 = (bf16[32,3072]{1,0:T(8,128)(2,1)S(1)}, bf16[32,3072]{1,0:T(8,128)(2,1)S(1)}, u32[]{:S(2)}, u32[]{:S(2)}) collective-permute-start(bf16[32,3072]{1,0:T(8,128)(2,1)S(1)} %get-tuple-element.49), channel_id=1, source_target_pairs={{0,8},{4,15},{8,0},{12,5},{1,9},{5,12},{9,1},{13,6},{2,10},{6,13},... | collective-permute-start | bytes 589832 | tf_op jit(solution)/shard_map/ppermute | solution.py:31
  47.3 3.4 %collective-permute-start.15 = (bf16[32,3072]{1,0:T(8,128)(2,1)S(1)}, bf16[32,3072]{1,0:T(8,128)(2,1)S(1)}, u32[]{:S(2)}, u32[]{:S(2)}) collective-permute-start(bf16[32,3072]{1,0:T(8,128)(2,1)S(1)} %get-tuple-element.50), channel_id=1, source_target_pairs={{0,24},{4,63},{8,16},{12,53},{1,25},{5,60},{9,17},{13,54},{2,26},{... | collective-permute-start | bytes 589832 | tf_op jit(solution)/shard_map/ppermute | solution.py:31
  50.9 2.4 %collective-permute-done.14 = bf16[32,3072]{1,0:T(8,128)(2,1)S(1)} collective-permute-done((bf16[32,3072]{1,0:T(8,128)(2,1)S(1)}, bf16[32,3072]{1,0:T(8,128)(2,1)S(1)}, u32[]{:S(2)}, u32[]{:S(2)}) %collective-permute-start.14) | collective-permute-done | bytes 196640 | tf_op jit(solution)/shard_map/ppermute | solution.py:31
  53.2 1.6 %collective-permute-done.15 = bf16[32,3072]{1,0:T(8,128)(2,1)S(1)} collective-permute-done((bf16[32,3072]{1,0:T(8,128)(2,1)S(1)}, bf16[32,3072]{1,0:T(8,128)(2,1)S(1)}, u32[]{:S(2)}, u32[]{:S(2)}) %collective-permute-start.15) | collective-permute-done | bytes 196640 | tf_op jit(solution)/shard_map/ppermute | solution.py:31
  55.0 3.0 %collective-permute-start.16 = (bf16[32,3072]{1,0:T(8,128)(2,1)S(1)}, bf16[32,3072]{1,0:T(8,128)(2,1)S(1)}, u32[]{:S(2)}, u32[]{:S(2)}) collective-permute-start(bf16[32,3072]{1,0:T(8,128)(2,1)S(1)} %add_convert_fusion.3), channel_id=1, source_target_pairs={{0,16},{4,52},{8,24},{12,60},{1,17},{5,53},{9,25},{13,61},{2,18},{... | collective-permute-start | bytes 589832 | tf_op jit(solution)/shard_map/ppermute | solution.py:31
  58.0 2.5 %collective-permute-done.16.refs_3_ = bf16[32,3072]{1,0:T(8,128)(2,1)S(1)} collective-permute-done((bf16[32,3072]{1,0:T(8,128)(2,1)S(1)}, bf16[32,3072]{1,0:T(8,128)(2,1)S(1)}, u32[]{:S(2)}, u32[]{:S(2)}) %collective-permute-start.16) | collective-permute-done | bytes 196640 | tf_op jit(solution)/shard_map/ppermute | solution.py:31
  61.2 3.2 %collective-permute-start.17 = (bf16[32,3200]{1,0:T(8,128)(2,1)S(1)}, bf16[32,3200]{1,0:T(8,128)(2,1)S(1)}, u32[]{:S(2)}, u32[]{:S(2)}) collective-permute-start(bf16[32,3200]{1,0:T(8,128)(2,1)S(1)} %get-tuple-element.55.refs_4_.refs_0_), channel_id=1, source_target_pairs={{0,16},{4,52},{8,24},{12,60},{1,17},{5,53},{9,25},{13,61},{2,18},{... | collective-permute-start | bytes 614408 | tf_op jit(solution)/shard_map/ppermute | solution.py:31
  65.3 2.3 %collective-permute-done.17.refs_5_.refs_1_ = bf16[32,3200]{1,0:T(8,128)(2,1)S(1)} collective-permute-done((bf16[32,3200]{1,0:T(8,128)(2,1)S(1)}, bf16[32,3200]{1,0:T(8,128)(2,1)S(1)}, u32[]{:S(2)}, u32[]{:S(2)}) %collective-permute-start.17) | collective-permute-done | bytes 204832 | tf_op jit(solution)/shard_map/ppermute | solution.py:31
  67.6 5.7 %collective-permute-start.19 = (bf16[32,3200]{1,0:T(8,128)(2,1)S(1)}, bf16[32,3200]{1,0:T(8,128)(2,1)S(1)}, u32[]{:S(2)}, u32[]{:S(2)}) collective-permute-start(bf16[32,3200]{1,0:T(8,128)(2,1)S(1)} %collective-permute-done.17.refs_5_.refs_1_), channel_id=1, source_target_pairs={{0,16},{4,52},{8,24},{12,60},{1,17},{5,53},{9,25},{13,61},{2,18},{... | collective-permute-start | bytes 614408 | tf_op jit(solution)/shard_map/ppermute | solution.py:31
  73.3 2.4 %collective-permute-start.20 = (bf16[32,3200]{1,0:T(8,128)(2,1)S(1)}, bf16[32,3200]{1,0:T(8,128)(2,1)S(1)}, u32[]{:S(2)}, u32[]{:S(2)}) collective-permute-start(bf16[32,3200]{1,0:T(8,128)(2,1)S(1)} %get-tuple-element.55.refs_4_.refs_0_), channel_id=1, source_target_pairs={{0,8},{4,15},{8,0},{12,5},{1,9},{5,12},{9,1},{13,6},{2,10},{6,13},... | collective-permute-start | bytes 614408 | tf_op jit(solution)/shard_map/ppermute | solution.py:31
  79.1 1.6 %collective-permute-start.25 = (f32[8,3200]{1,0:T(8,128)S(1)}, f32[8,3200]{1,0:T(8,128)S(1)}, u32[]{:S(2)}, u32[]{:S(2)}) collective-permute-start(f32[8,3200]{1,0:T(8,128)S(1)} %add.67), channel_id=1, source_target_pairs={{0,64},{64,0},{128,192},{192,128},{1,65},{65,1},{129,193},{193,129... | collective-permute-start | bytes 307208 | tf_op jit(solution)/shard_map/ppermute | solution.py:391
  81.6 2.1 %hidden_grads.1 = (bf16[256,1024]{1,0:T(8,128)(2,1)S(1)}, bf16[256,1024]{1,0:T(8,128)(2,1)S(1)}) custom-call(bf16[32,3200]{1,0:T(8,128)(2,1)S(1)} %get-tuple-element.55.refs_4_.refs_0_, bf16[32,3200]{1,0:T(8,128)(2,1)S(1)} %collective-permute-done.17.refs_5_.refs_1_, bf16[32,3200]{1,0:T(8,128)(2,1)S(1)} %collective-permute-done.18.refs_6_.refs_2_, ...), custom_call_target="tpu_custom_call" | custom-call | flops 1610612736 | bytes 6291456 | tf_op jit(solution)/shard_map/hidden_grads/pallas_call | solution.py:180
  83.8 3.0 %collective-permute-start.33 = (f32[8,3200]{1,0:T(8,128)S(1)}, f32[8,3200]{1,0:T(8,128)S(1)}, u32[]{:S(2)}, u32[]{:S(2)}) collective-permute-start(f32[8,3200]{1,0:T(8,128)S(1)} %add.68), channel_id=1, source_target_pairs={{0,128},{64,192},{128,0},{192,64},{1,129},{65,193},{129,1},{193,65... | collective-permute-start | bytes 307208 | tf_op jit(solution)/shard_map/ppermute | solution.py:393
  86.8 3.4 %slot_grads.1 = (bf16[32,3072]{1,0:T(8,128)(2,1)S(1)}, bf16[32,3072]{1,0:T(8,128)(2,1)S(1)}, bf16[32,3072]{1,0:T(8,128)(2,1)S(1)}, bf16[32,3072]{1,0:T(8,128)(2,...) custom-call(bf16[256,1024]{1,0:T(8,128)(2,1)S(1)} %get-tuple-element, ...), custom_call_target="tpu_custom_call" | custom-call | flops 3221225472 | bytes 12582912 | tf_op jit(solution)/shard_map/slot_grads/pallas_call | solution.py:212
  91.2 8.3 %collective-permute-start.28 = (bf16[32,3072]{1,0:T(8,128)(2,1)S(1)}, bf16[32,3072]{1,0:T(8,128)(2,1)S(1)}, u32[]{:S(2)}, u32[]{:S(2)}) collective-permute-start(bf16[32,3072]{1,0:T(8,128)(2,1)S(1)} %get-tuple-element.66), channel_id=1, source_target_pairs={{0,8},{4,15},{8,0},{12,5},{1,9},{5,12},{9,1},{13,6},{2,10},{6,13},... | collective-permute-start | bytes 589832 | tf_op jit(solution)/shard_map/ppermute | solution.py:31
  100.8 2.7 %collective-permute-start.30 = (bf16[32,3072]{1,0:T(8,128)(2,1)S(1)}, bf16[32,3072]{1,0:T(8,128)(2,1)S(1)}, u32[]{:S(2)}, u32[]{:S(2)}) collective-permute-start(bf16[32,3072]{1,0:T(8,128)(2,1)S(1)} %get-tuple-element.68), channel_id=1, source_target_pairs={{0,8},{4,15},{8,0},{12,5},{1,9},{5,12},{9,1},{13,6},{2,10},{6,13},... | collective-permute-start | bytes 589832 | tf_op jit(solution)/shard_map/ppermute | solution.py:31
  103.5 2.3 %collective-permute-start.31 = (bf16[32,3072]{1,0:T(8,128)(2,1)S(1)}, bf16[32,3072]{1,0:T(8,128)(2,1)S(1)}, u32[]{:S(2)}, u32[]{:S(2)}) collective-permute-start(bf16[32,3072]{1,0:T(8,128)(2,1)S(1)} %get-tuple-element.69), channel_id=1, source_target_pairs={{0,24},{4,63},{8,16},{12,53},{1,25},{5,60},{9,17},{13,54},{2,26},{... | collective-permute-start | bytes 589832 | tf_op jit(solution)/shard_map/ppermute | solution.py:31
  106.1 2.5 %collective-permute-done.30 = bf16[32,3072]{1,0:T(8,128)(2,1)S(1)} collective-permute-done((bf16[32,3072]{1,0:T(8,128)(2,1)S(1)}, bf16[32,3072]{1,0:T(8,128)(2,1)S(1)}, u32[]{:S(2)}, u32[]{:S(2)}) %collective-permute-start.30) | collective-permute-done | bytes 196640 | tf_op jit(solution)/shard_map/ppermute | solution.py:31
  108.7 1.6 %collective-permute-done.31 = bf16[32,3072]{1,0:T(8,128)(2,1)S(1)} collective-permute-done((bf16[32,3072]{1,0:T(8,128)(2,1)S(1)}, bf16[32,3072]{1,0:T(8,128)(2,1)S(1)}, u32[]{:S(2)}, u32[]{:S(2)}) %collective-permute-start.31) | collective-permute-done | bytes 196640 | tf_op jit(solution)/shard_map/ppermute | solution.py:31
  110.3 3.7 %collective-permute-start.32 = (bf16[32,3072]{1,0:T(8,128)(2,1)S(1)}, bf16[32,3072]{1,0:T(8,128)(2,1)S(1)}, u32[]{:S(2)}, u32[]{:S(2)}) collective-permute-start(bf16[32,3072]{1,0:T(8,128)(2,1)S(1)} %add_convert_fusion.1), channel_id=1, source_target_pairs={{0,16},{4,52},{8,24},{12,60},{1,17},{5,53},{9,25},{13,61},{2,18},{... | collective-permute-start | bytes 589832 | tf_op jit(solution)/shard_map/ppermute | solution.py:31
  (94 shorter events, 22.8 us)
Async XLA Ops:
  2.8 9.8 %collective-permute-start.7 = (bf16[3072,512]{1,0:T(8,128)(2,1)}, bf16[3072,512]{1,0:T(8,128)(2,1)S(1)}, u32[]{:S(2)}, u32[]{:S(2)}) collective-permute-start(bf16[3072,512]{1,0:T(8,128)(2,1)} %refs_2_.1), channel_id=1, source_target_pairs={{0,4},{4,0},{8,12},{12,8},{1,5},{5,1},{9,13},{13,9},{2,6},{6,2},{1... | collective-permute-start | bytes 9437192 | tf_op jit(solution)/shard_map/ppermute | solution.py:31
  6.2 29.3 %collective-permute-start.8 = (bf16[3072,512]{1,0:T(8,128)(2,1)}, bf16[3072,512]{1,0:T(8,128)(2,1)S(1)}, u32[]{:S(2)}, u32[]{:S(2)}) collective-permute-start(bf16[3072,512]{1,0:T(8,128)(2,1)} %refs_4_.1), channel_id=1, source_target_pairs={{0,4},{4,0},{8,12},{12,8},{1,5},{5,1},{9,13},{13,9},{2,6},{6,2},{1... | collective-permute-start | bytes 9437192 | tf_op jit(solution)/shard_map/ppermute | solution.py:31
  6.3 6.2 %collective-permute-start.1 = (bf16[32,3072]{1,0:T(8,128)(2,1)S(1)}, bf16[32,3072]{1,0:T(8,128)(2,1)S(1)}, u32[]{:S(2)}, u32[]{:S(2)}) collective-permute-start(bf16[32,3072]{1,0:T(8,128)(2,1)S(1)} %get-tuple-element.38.refs_0_.refs_4_), channel_id=1, source_target_pairs={{0,48},{4,20},{8,56},{12,28},{1,49},{5,21},{9,57},{13,29},{2,50},{... | collective-permute-start | bytes 589832 | tf_op jit(solution)/shard_map/ppermute | solution.py:31
  6.3 6.3 %collective-permute-start = (bf16[32,3072]{1,0:T(8,128)(2,1)S(1)}, bf16[32,3072]{1,0:T(8,128)(2,1)S(1)}, u32[]{:S(2)}, u32[]{:S(2)}) collective-permute-start(bf16[32,3072]{1,0:T(8,128)(2,1)S(1)} %get-tuple-element.38.refs_0_.refs_4_), channel_id=1, source_target_pairs={{0,16},{4,52},{8,24},{12,60},{1,17},{5,53},{9,25},{13,61},{2,18},{... | collective-permute-start | bytes 589832 | tf_op jit(solution)/shard_map/ppermute | solution.py:31
  12.6 28.2 %collective-permute-start.9 = (bf16[512,3072]{1,0:T(8,128)(2,1)}, bf16[512,3072]{1,0:T(8,128)(2,1)S(1)}, u32[]{:S(2)}, u32[]{:S(2)}) collective-permute-start(bf16[512,3072]{1,0:T(8,128)(2,1)} %refs_8_.3), channel_id=1, source_target_pairs={{0,4},{4,0},{8,12},{12,8},{1,5},{5,1},{9,13},{13,9},{2,6},{6,2},{1... | collective-permute-start | bytes 9437192 | tf_op jit(solution)/shard_map/ppermute | solution.py:31
  14.8 14.7 %collective-permute-start.5 = (bf16[32,3072]{1,0:T(8,128)(2,1)S(1)}, bf16[32,3072]{1,0:T(8,128)(2,1)S(1)}, u32[]{:S(2)}, u32[]{:S(2)}) collective-permute-start(bf16[32,3072]{1,0:T(8,128)(2,1)S(1)} %get-tuple-element.38.refs_0_.refs_4_), channel_id=1, source_target_pairs={{0,56},{4,31},{8,48},{12,21},{1,57},{5,28},{9,49},{13,22},{2,58},{... | collective-permute-start | bytes 589832 | tf_op jit(solution)/shard_map/ppermute | solution.py:31
  18.9 10.7 %collective-permute-start.4 = (bf16[32,3072]{1,0:T(8,128)(2,1)S(1)}, bf16[32,3072]{1,0:T(8,128)(2,1)S(1)}, u32[]{:S(2)}, u32[]{:S(2)}) collective-permute-start(bf16[32,3072]{1,0:T(8,128)(2,1)S(1)} %get-tuple-element.38.refs_0_.refs_4_), channel_id=1, source_target_pairs={{0,24},{4,63},{8,16},{12,53},{1,25},{5,60},{9,17},{13,54},{2,26},{... | collective-permute-start | bytes 589832 | tf_op jit(solution)/shard_map/ppermute | solution.py:31
  21.0 10.1 %collective-permute-start.3 = (bf16[32,3072]{1,0:T(8,128)(2,1)S(1)}, bf16[32,3072]{1,0:T(8,128)(2,1)S(1)}, u32[]{:S(2)}, u32[]{:S(2)}) collective-permute-start(bf16[32,3072]{1,0:T(8,128)(2,1)S(1)} %get-tuple-element.38.refs_0_.refs_4_), channel_id=1, source_target_pairs={{0,8},{4,15},{8,0},{12,5},{1,9},{5,12},{9,1},{13,6},{2,10},{6,13},... | collective-permute-start | bytes 589832 | tf_op jit(solution)/shard_map/ppermute | solution.py:31
  29.5 5.9 %collective-permute-start.2 = (bf16[32,3072]{1,0:T(8,128)(2,1)S(1)}, bf16[32,3072]{1,0:T(8,128)(2,1)S(1)}, u32[]{:S(2)}, u32[]{:S(2)}) collective-permute-start(bf16[32,3072]{1,0:T(8,128)(2,1)S(1)} %collective-permute-done.refs_1_), channel_id=1, source_target_pairs={{0,16},{4,52},{8,24},{12,60},{1,17},{5,53},{9,25},{13,61},{2,18},{... | collective-permute-start | bytes 589832 | tf_op jit(solution)/shard_map/ppermute | solution.py:31
  29.6 5.8 %collective-permute-start.6 = (bf16[32,3072]{1,0:T(8,128)(2,1)S(1)}, bf16[32,3072]{1,0:T(8,128)(2,1)S(1)}, u32[]{:S(2)}, u32[]{:S(2)}) collective-permute-start(bf16[32,3072]{1,0:T(8,128)(2,1)S(1)} %collective-permute-done.5.refs_6_), channel_id=1, source_target_pairs={{0,48},{4,20},{8,56},{12,28},{1,49},{5,21},{9,57},{13,29},{2,50},{... | collective-permute-start | bytes 589832 | tf_op jit(solution)/shard_map/ppermute | solution.py:31
  42.6 8.1 %collective-permute-start.11 = (bf16[32,3072]{1,0:T(8,128)(2,1)S(1)}, bf16[32,3072]{1,0:T(8,128)(2,1)S(1)}, u32[]{:S(2)}, u32[]{:S(2)}) collective-permute-start(bf16[32,3072]{1,0:T(8,128)(2,1)S(1)} %get-tuple-element.46), channel_id=1, source_target_pairs={{0,48},{4,20},{8,56},{12,28},{1,49},{5,21},{9,57},{13,29},{2,50},{... | collective-permute-start | bytes 589832 | tf_op jit(solution)/shard_map/ppermute | solution.py:31
  43.0 7.7 %collective-permute-start.12 = (bf16[32,3072]{1,0:T(8,128)(2,1)S(1)}, bf16[32,3072]{1,0:T(8,128)(2,1)S(1)}, u32[]{:S(2)}, u32[]{:S(2)}) collective-permute-start(bf16[32,3072]{1,0:T(8,128)(2,1)S(1)} %get-tuple-element.47), channel_id=1, source_target_pairs={{0,8},{4,15},{8,0},{12,5},{1,9},{5,12},{9,1},{13,6},{2,10},{6,13},... | collective-permute-start | bytes 589832 | tf_op jit(solution)/shard_map/ppermute | solution.py:31
  44.6 13.4 %collective-permute-start.10 = (bf16[32,3072]{1,0:T(8,128)(2,1)S(1)}, bf16[32,3072]{1,0:T(8,128)(2,1)S(1)}, u32[]{:S(2)}, u32[]{:S(2)}) collective-permute-start(bf16[32,3072]{1,0:T(8,128)(2,1)S(1)} %get-tuple-element.44), channel_id=1, source_target_pairs={{0,8},{4,15},{8,0},{12,5},{1,9},{5,12},{9,1},{13,6},{2,10},{6,13},... | collective-permute-start | bytes 589832 | tf_op jit(solution)/shard_map/ppermute | solution.py:31
  45.8 7.5 %collective-permute-start.14 = (bf16[32,3072]{1,0:T(8,128)(2,1)S(1)}, bf16[32,3072]{1,0:T(8,128)(2,1)S(1)}, u32[]{:S(2)}, u32[]{:S(2)}) collective-permute-start(bf16[32,3072]{1,0:T(8,128)(2,1)S(1)} %get-tuple-element.49), channel_id=1, source_target_pairs={{0,8},{4,15},{8,0},{12,5},{1,9},{5,12},{9,1},{13,6},{2,10},{6,13},... | collective-permute-start | bytes 589832 | tf_op jit(solution)/shard_map/ppermute | solution.py:31
  47.3 7.5 %collective-permute-start.15 = (bf16[32,3072]{1,0:T(8,128)(2,1)S(1)}, bf16[32,3072]{1,0:T(8,128)(2,1)S(1)}, u32[]{:S(2)}, u32[]{:S(2)}) collective-permute-start(bf16[32,3072]{1,0:T(8,128)(2,1)S(1)} %get-tuple-element.50), channel_id=1, source_target_pairs={{0,24},{4,63},{8,16},{12,53},{1,25},{5,60},{9,17},{13,54},{2,26},{... | collective-permute-start | bytes 589832 | tf_op jit(solution)/shard_map/ppermute | solution.py:31
  50.8 7.2 %collective-permute-start.13 = (bf16[32,3072]{1,0:T(8,128)(2,1)S(1)}, bf16[32,3072]{1,0:T(8,128)(2,1)S(1)}, u32[]{:S(2)}, u32[]{:S(2)}) collective-permute-start(bf16[32,3072]{1,0:T(8,128)(2,1)S(1)} %add_convert_fusion.4), channel_id=1, source_target_pairs={{0,48},{4,20},{8,56},{12,28},{1,49},{5,21},{9,57},{13,29},{2,50},{... | collective-permute-start | bytes 589832 | tf_op jit(solution)/shard_map/ppermute | solution.py:31
  61.2 6.4 %collective-permute-start.17 = (bf16[32,3200]{1,0:T(8,128)(2,1)S(1)}, bf16[32,3200]{1,0:T(8,128)(2,1)S(1)}, u32[]{:S(2)}, u32[]{:S(2)}) collective-permute-start(bf16[32,3200]{1,0:T(8,128)(2,1)S(1)} %get-tuple-element.55.refs_4_.refs_0_), channel_id=1, source_target_pairs={{0,16},{4,52},{8,24},{12,60},{1,17},{5,53},{9,25},{13,61},{2,18},{... | collective-permute-start | bytes 614408 | tf_op jit(solution)/shard_map/ppermute | solution.py:31
  64.4 11.3 %collective-permute-start.22 = (bf16[32,3200]{1,0:T(8,128)(2,1)S(1)}, bf16[32,3200]{1,0:T(8,128)(2,1)S(1)}, u32[]{:S(2)}, u32[]{:S(2)}) collective-permute-start(bf16[32,3200]{1,0:T(8,128)(2,1)S(1)} %get-tuple-element.55.refs_4_.refs_0_), channel_id=1, source_target_pairs={{0,56},{4,31},{8,48},{12,21},{1,57},{5,28},{9,49},{13,22},{2,58},{... | collective-permute-start | bytes 614408 | tf_op jit(solution)/shard_map/ppermute | solution.py:31
  64.4 12.8 %collective-permute-start.18 = (bf16[32,3200]{1,0:T(8,128)(2,1)S(1)}, bf16[32,3200]{1,0:T(8,128)(2,1)S(1)}, u32[]{:S(2)}, u32[]{:S(2)}) collective-permute-start(bf16[32,3200]{1,0:T(8,128)(2,1)S(1)} %get-tuple-element.55.refs_4_.refs_0_), channel_id=1, source_target_pairs={{0,48},{4,20},{8,56},{12,28},{1,49},{5,21},{9,57},{13,29},{2,50},{... | collective-permute-start | bytes 614408 | tf_op jit(solution)/shard_map/ppermute | solution.py:31
  67.6 9.6 %collective-permute-start.19 = (bf16[32,3200]{1,0:T(8,128)(2,1)S(1)}, bf16[32,3200]{1,0:T(8,128)(2,1)S(1)}, u32[]{:S(2)}, u32[]{:S(2)}) collective-permute-start(bf16[32,3200]{1,0:T(8,128)(2,1)S(1)} %collective-permute-done.17.refs_5_.refs_1_), channel_id=1, source_target_pairs={{0,16},{4,52},{8,24},{12,60},{1,17},{5,53},{9,25},{13,61},{2,18},{... | collective-permute-start | bytes 614408 | tf_op jit(solution)/shard_map/ppermute | solution.py:31
  73.3 7.4 %collective-permute-start.21 = (bf16[32,3200]{1,0:T(8,128)(2,1)S(1)}, bf16[32,3200]{1,0:T(8,128)(2,1)S(1)}, u32[]{:S(2)}, u32[]{:S(2)}) collective-permute-start(bf16[32,3200]{1,0:T(8,128)(2,1)S(1)} %get-tuple-element.55.refs_4_.refs_0_), channel_id=1, source_target_pairs={{0,24},{4,63},{8,16},{12,53},{1,25},{5,60},{9,17},{13,54},{2,26},{... | collective-permute-start | bytes 614408 | tf_op jit(solution)/shard_map/ppermute | solution.py:31
  73.3 7.8 %collective-permute-start.20 = (bf16[32,3200]{1,0:T(8,128)(2,1)S(1)}, bf16[32,3200]{1,0:T(8,128)(2,1)S(1)}, u32[]{:S(2)}, u32[]{:S(2)}) collective-permute-start(bf16[32,3200]{1,0:T(8,128)(2,1)S(1)} %get-tuple-element.55.refs_4_.refs_0_), channel_id=1, source_target_pairs={{0,8},{4,15},{8,0},{12,5},{1,9},{5,12},{9,1},{13,6},{2,10},{6,13},... | collective-permute-start | bytes 614408 | tf_op jit(solution)/shard_map/ppermute | solution.py:31
  75.7 5.8 %collective-permute-start.23 = (bf16[32,3200]{1,0:T(8,128)(2,1)S(1)}, bf16[32,3200]{1,0:T(8,128)(2,1)S(1)}, u32[]{:S(2)}, u32[]{:S(2)}) collective-permute-start(bf16[32,3200]{1,0:T(8,128)(2,1)S(1)} %collective-permute-done.22.refs_6_), channel_id=1, source_target_pairs={{0,48},{4,20},{8,56},{12,28},{1,49},{5,21},{9,57},{13,29},{2,50},{... | collective-permute-start | bytes 614408 | tf_op jit(solution)/shard_map/ppermute | solution.py:31
  83.8 19.7 %collective-permute-start.33 = (f32[8,3200]{1,0:T(8,128)S(1)}, f32[8,3200]{1,0:T(8,128)S(1)}, u32[]{:S(2)}, u32[]{:S(2)}) collective-permute-start(f32[8,3200]{1,0:T(8,128)S(1)} %add.68), channel_id=1, source_target_pairs={{0,128},{64,192},{128,0},{192,64},{1,129},{65,193},{129,1},{193,65... | collective-permute-start | bytes 307208 | tf_op jit(solution)/shard_map/ppermute | solution.py:393
  90.2 15.6 %collective-permute-start.27 = (bf16[32,3072]{1,0:T(8,128)(2,1)S(1)}, bf16[32,3072]{1,0:T(8,128)(2,1)S(1)}, u32[]{:S(2)}, u32[]{:S(2)}) collective-permute-start(bf16[32,3072]{1,0:T(8,128)(2,1)S(1)} %get-tuple-element.65), channel_id=1, source_target_pairs={{0,48},{4,20},{8,56},{12,28},{1,49},{5,21},{9,57},{13,29},{2,50},{... | collective-permute-start | bytes 589832 | tf_op jit(solution)/shard_map/ppermute | solution.py:31
  91.2 14.7 %collective-permute-start.28 = (bf16[32,3072]{1,0:T(8,128)(2,1)S(1)}, bf16[32,3072]{1,0:T(8,128)(2,1)S(1)}, u32[]{:S(2)}, u32[]{:S(2)}) collective-permute-start(bf16[32,3072]{1,0:T(8,128)(2,1)S(1)} %get-tuple-element.66), channel_id=1, source_target_pairs={{0,8},{4,15},{8,0},{12,5},{1,9},{5,12},{9,1},{13,6},{2,10},{6,13},... | collective-permute-start | bytes 589832 | tf_op jit(solution)/shard_map/ppermute | solution.py:31
  100.8 14.5 %collective-permute-start.26 = (bf16[32,3072]{1,0:T(8,128)(2,1)S(1)}, bf16[32,3072]{1,0:T(8,128)(2,1)S(1)}, u32[]{:S(2)}, u32[]{:S(2)}) collective-permute-start(bf16[32,3072]{1,0:T(8,128)(2,1)S(1)} %get-tuple-element.63), channel_id=1, source_target_pairs={{0,8},{4,15},{8,0},{12,5},{1,9},{5,12},{9,1},{13,6},{2,10},{6,13},... | collective-permute-start | bytes 589832 | tf_op jit(solution)/shard_map/ppermute | solution.py:31
  100.8 7.8 %collective-permute-start.30 = (bf16[32,3072]{1,0:T(8,128)(2,1)S(1)}, bf16[32,3072]{1,0:T(8,128)(2,1)S(1)}, u32[]{:S(2)}, u32[]{:S(2)}) collective-permute-start(bf16[32,3072]{1,0:T(8,128)(2,1)S(1)} %get-tuple-element.68), channel_id=1, source_target_pairs={{0,8},{4,15},{8,0},{12,5},{1,9},{5,12},{9,1},{13,6},{2,10},{6,13},... | collective-permute-start | bytes 589832 | tf_op jit(solution)/shard_map/ppermute | solution.py:31
  103.5 6.8 %collective-permute-start.31 = (bf16[32,3072]{1,0:T(8,128)(2,1)S(1)}, bf16[32,3072]{1,0:T(8,128)(2,1)S(1)}, u32[]{:S(2)}, u32[]{:S(2)}) collective-permute-start(bf16[32,3072]{1,0:T(8,128)(2,1)S(1)} %get-tuple-element.69), channel_id=1, source_target_pairs={{0,24},{4,63},{8,16},{12,53},{1,25},{5,60},{9,17},{13,54},{2,26},{... | collective-permute-start | bytes 589832 | tf_op jit(solution)/shard_map/ppermute | solution.py:31
  105.8 8.2 %collective-permute-start.34 = (f32[8,3200]{1,0:T(8,128)S(1)}, f32[8,3200]{1,0:T(8,128)S(1)}, u32[]{:S(2)}, u32[]{:S(2)}) collective-permute-start(f32[8,3200]{1,0:T(8,128)S(1)} %add.77), channel_id=1, source_target_pairs={{0,8},{4,12},{8,0},{12,4},{1,9},{5,13},{9,1},{13,5},{2,10},{6,14},... | collective-permute-start | bytes 307208 | tf_op jit(solution)/shard_map/ppermute | solution.py:31
  106.0 9.3 %collective-permute-start.29 = (bf16[32,3072]{1,0:T(8,128)(2,1)S(1)}, bf16[32,3072]{1,0:T(8,128)(2,1)S(1)}, u32[]{:S(2)}, u32[]{:S(2)}) collective-permute-start(bf16[32,3072]{1,0:T(8,128)(2,1)S(1)} %add_convert_fusion.2), channel_id=1, source_target_pairs={{0,48},{4,20},{8,56},{12,28},{1,49},{5,21},{9,57},{13,29},{2,50},{... | collective-permute-start | bytes 589832 | tf_op jit(solution)/shard_map/ppermute | solution.py:31
  110.3 6.3 %collective-permute-start.32 = (bf16[32,3072]{1,0:T(8,128)(2,1)S(1)}, bf16[32,3072]{1,0:T(8,128)(2,1)S(1)}, u32[]{:S(2)}, u32[]{:S(2)}) collective-permute-start(bf16[32,3072]{1,0:T(8,128)(2,1)S(1)} %add_convert_fusion.1), channel_id=1, source_target_pairs={{0,16},{4,52},{8,24},{12,60},{1,17},{5,53},{9,25},{13,61},{2,18},{... | collective-permute-start | bytes 589832 | tf_op jit(solution)/shard_map/ppermute | solution.py:31
  (13 other events, 135.8 us)

commit v2 on v1

--- a/solution.py
+++ b/solution.py
@@ -67,14 +67,14 @@
     return lax.optimization_barrier((value, *others))[0]
 
 
-def gather(own):
+def gather(own, *others):
     f1 = ahead(own)
-    zb1 = behind_across(own)
     b1 = behind(own)
     z0 = across(own)
-    zf1 = ahead_across(own)
-    x2 = ahead(f1)
-    zx2 = behind(zb1)
+    x2 = ahead(after(f1, *others))
+    zf1 = across(f1)
+    zb1 = across(b1)
+    zx2 = behind_across(b1)
     return [own, f1, b1, x2, z0, zf1, zb1, zx2]
 
 
@@ -101,6 +101,7 @@
 
 
 VMEM = pl.BlockSpec(memory_space=pltpu.VMEM)
+HBM = pl.BlockSpec(memory_space=pltpu.HBM)
 
 
 def hidden_kernel(*refs):
@@ -315,6 +316,27 @@
     )(*token_blocks, *grad_blocks)
 
 
+def load_kernel(gate, up, gate_ref, up_ref, sems):
+    copies = [pltpu.make_async_copy(gate, gate_ref, sems.at[0]), pltpu.make_async_copy(up, up_ref, sems.at[1])]
+    for copy in copies:
+        copy.start()
+    for copy in copies:
+        copy.wait()
+
+
+def load(gate, up):
+    return pl.pallas_call(
+        load_kernel,
+        name="load_weights",
+        out_shape=[jax.ShapeDtypeStruct(w.shape, w.dtype) for w in (gate, up)],
+        in_specs=[HBM] * 2,
+        out_specs=[VMEM] * 2,
+        scratch_shapes=[pltpu.SemaphoreType.DMA((2,))],
+        compiler_params=pltpu.CompilerParams(vmem_limit_bytes=8 << 20),
+        cost_estimate=pl.CostEstimate(flops=0, bytes_accessed=4 * gate.size, transcendentals=0),
+    )(gate, up)
+
+
 def place_kernel(routes, tokens, placing_ref, slots_ref):
     rows = tokens.shape[0]
     capacity = slots_ref.shape[0]
@@ -346,19 +368,22 @@
     capacity = tok_rows // 4
     experts = router_weight.shape[1]
     all_tokens = tok_rows * 64
+    placing, token_slots = place(routes.T, tokens)
+
+    own_gate, own_up = load(after(gate_weight, token_slots), up_weight)
+    token_blocks = gather(token_slots, own_gate)
+    gates = [own_gate, twin(after(gate_weight, token_slots))]
+    ups = [own_up, twin(after(up_weight, token_slots))]
+    downs = [down_weight, twin(after(down_weight, *token_blocks[1:]))]
+    hidden, pre_gate, pre_up = hidden_units(token_blocks, gates, ups)
+    terms = slot_terms(hidden, downs)
+
+    tokens, teacher, routes, language = lax.optimization_barrier((tokens, teacher, routes, language, hidden))[:4]
     first_id = routes[:, 0]
     second_id = routes[:, 1]
     chosen = jnp.logical_or(first_id == 0, second_id == 0)
     other_id = jnp.where(first_id == 0, second_id, first_id).astype(f32)
-    placing, token_slots = place(routes.T, tokens)
     placing_half = placing.astype(bf16)
-
-    token_blocks = gather(token_slots)
-    gates = [gate_weight, twin(after(gate_weight, token_slots))]
-    ups = [up_weight, twin(after(up_weight, token_slots))]
-    downs = [down_weight, twin(after(down_weight, gates[1], token_blocks[1], token_blocks[2]))]
-    tokens, teacher = lax.optimization_barrier((tokens, teacher, token_slots))[:2]
-
     teacher_slots = jnp.dot(placing_half, teacher, preferred_element_type=f32).astype(bf16)
     logits = jnp.dot(token_slots, router_weight, preferred_element_type=f32)
     other_slots = jnp.sum(placing * other_id[None, :], axis=1)
@@ -378,8 +403,6 @@
     sub = lax.broadcasted_iota(jnp.int32, (8, LANES), 0)
     base = jnp.where(sub == 0, jnp.sum(plain_loss[:, None] * lang_hot, axis=0)[None, :], jnp.sum(lang_hot, axis=0)[None, :])
 
-    hidden, pre_gate, pre_up = hidden_units(token_blocks, gates, ups)
-    terms = slot_terms(hidden, downs)
     combined, grad_slots, so_far = slots(scatter(terms), token_slots, teacher_slots, aux, slot_langs, base, router_weight.T)
     grad_blocks = gather(grad_slots)
     placed = lax.dot_general(placing_half, combined, TN, preferred_element_type=f32)

time: 118 us -> 112 us (0.949)
  the two profiles are of different devices: /device:TPU:1 before, /device:TPU:64 now
where the time goes in v2:
time: 112 us; the launch traced here: 111 us
  starting transfers between devices  48.7 us (43%)
  waiting for transfers between devices  36.7 us (33%)
  Pallas kernels  12.7 us (11%)
  local copies, waits for them, and re-layouts  6.48 us (6%)
  matrix products  3.2 us (3%)
  other arithmetic  1.77 us (2%)
    ppermute x33, starting transfers between devices, move(): return lax.ppermute(value, GROUP, pairs)  43.6 us
    ppermute x33, waiting for transfers between devices, move(): return lax.ppermute(value, GROUP, pairs)  35.5 us
    unnamed x20, local copies, waits for them, and re-layouts  5.9 us
    pallas_call x1, Pallas kernels, slot_grads(): pl.pallas_call(slot_grad_kernel, name='slot_grads', out_shape=[jax.ShapeD...  3.44 us
    pallas_call x1, Pallas kernels, hidden_units(): pl.pallas_call(hidden_kernel, name='hidden_units', out_shape=[jax.ShapeDt...  3.42 us
    ppermute x1, starting transfers between devices, local(): lax.ppermute(summed, 'expert', [(i, i ^ 2) for i in range(4)])  3.26 us
  transfers between devices with their start and end apart: 35, of which 16 were waited for; matrix products, arithmetic and copies ran while one was open for 4% of the time, Pallas kernels for 9%

profile of v2, /device:TPU:64, one launch (start us, length us, event | category | flops | bytes accessed | tf_op | source)
XLA Modules:
  0.0 110.6 jit_solution(15881828718787537827)
XLA Ops:
  3.4 2.8 %collective-permute-start.1 = (bf16[32,3072]{1,0:T(8,128)(2,1)S(1)}, bf16[32,3072]{1,0:T(8,128)(2,1)S(1)}, u32[]{:S(2)}, u32[]{:S(2)}) collective-permute-start(bf16[32,3072]{1,0:T(8,128)(2,1)S(1)} %get-tuple-element.42.refs_0_.refs_4_), channel_id=1, source_target_pairs={{0,48},{4,20},{8,56},{12,28},{1,49},{5,21},{9,57},{13,29},{2,50},{... | collective-permute-start | bytes 589832 | tf_op jit(solution)/shard_map/ppermute | solution.py:31
  6.2 1.9 %collective-permute-start.3 = (bf16[32,3072]{1,0:T(8,128)(2,1)S(1)}, bf16[32,3072]{1,0:T(8,128)(2,1)S(1)}, u32[]{:S(2)}, u32[]{:S(2)}) collective-permute-start(bf16[32,3072]{1,0:T(8,128)(2,1)S(1)} %get-tuple-element.42.refs_0_.refs_4_), channel_id=1, source_target_pairs={{0,8},{4,15},{8,0},{12,5},{1,9},{5,12},{9,1},{13,6},{2,10},{6,13},... | collective-permute-start | bytes 589832 | tf_op jit(solution)/shard_map/ppermute | solution.py:31
  8.1 2.8 %collective-permute-done.1.refs_2_ = bf16[32,3072]{1,0:T(8,128)(2,1)S(1)} collective-permute-done((bf16[32,3072]{1,0:T(8,128)(2,1)S(1)}, bf16[32,3072]{1,0:T(8,128)(2,1)S(1)}, u32[]{:S(2)}, u32[]{:S(2)}) %collective-permute-start.1) | collective-permute-done | bytes 196640 | tf_op jit(solution)/shard_map/ppermute | solution.py:31
  10.8 5.0 %collective-permute-start.6 = (bf16[32,3072]{1,0:T(8,128)(2,1)S(1)}, bf16[32,3072]{1,0:T(8,128)(2,1)S(1)}, u32[]{:S(2)}, u32[]{:S(2)}) collective-permute-start(bf16[32,3072]{1,0:T(8,128)(2,1)S(1)} %collective-permute-done.1.refs_2_), channel_id=1, source_target_pairs={{0,56},{4,31},{8,48},{12,21},{1,57},{5,28},{9,49},{13,22},{2,58},{... | collective-permute-start | bytes 589832 | tf_op jit(solution)/shard_map/ppermute | solution.py:31
  15.8 1.9 %copy-done.3 = bf16[3072,512]{1,0:T(8,128)(2,1)S(1)} copy-done((bf16[3072,512]{1,0:T(8,128)(2,1)S(1)}, bf16[3072,512]{1,0:T(8,128)(2,1)}, u32[]{:S(2)}) %copy-start.3) | copy-done | bytes 3145752
  17.7 1.9 %copy-done.4 = bf16[3072,512]{1,0:T(8,128)(2,1)S(1)} copy-done((bf16[3072,512]{1,0:T(8,128)(2,1)S(1)}, bf16[3072,512]{1,0:T(8,128)(2,1)}, u32[]{:S(2)}) %copy-start.4) | copy-done | bytes 3145752
  20.3 1.9 %collective-permute-start.4 = (bf16[32,3072]{1,0:T(8,128)(2,1)S(1)}, bf16[32,3072]{1,0:T(8,128)(2,1)S(1)}, u32[]{:S(2)}, u32[]{:S(2)}) collective-permute-start(bf16[32,3072]{1,0:T(8,128)(2,1)S(1)} %collective-permute-done.refs_1_), channel_id=1, source_target_pairs={{0,8},{4,15},{8,0},{12,5},{1,9},{5,12},{9,1},{13,6},{2,10},{6,13},... | collective-permute-start | bytes 589832 | tf_op jit(solution)/shard_map/ppermute | solution.py:31
  22.2 3.6 %collective-permute-done.5.refs_6_ = bf16[32,3072]{1,0:T(8,128)(2,1)S(1)} collective-permute-done((bf16[32,3072]{1,0:T(8,128)(2,1)S(1)}, bf16[32,3072]{1,0:T(8,128)(2,1)S(1)}, u32[]{:S(2)}, u32[]{:S(2)}) %collective-permute-start.5) | collective-permute-done | bytes 196640 | tf_op jit(solution)/shard_map/ppermute | solution.py:31
  25.8 2.1 %collective-permute-done.4.refs_5_ = bf16[32,3072]{1,0:T(8,128)(2,1)S(1)} collective-permute-done((bf16[32,3072]{1,0:T(8,128)(2,1)S(1)}, bf16[32,3072]{1,0:T(8,128)(2,1)S(1)}, u32[]{:S(2)}, u32[]{:S(2)}) %collective-permute-start.4) | collective-permute-done | bytes 196640 | tf_op jit(solution)/shard_map/ppermute | solution.py:31
  29.2 3.4 %hidden_units.1 = (bf16[256,1024]{1,0:T(8,128)(2,1)S(1)}, f32[256,1024]{1,0:T(8,128)S(1)}, f32[256,1024]{1,0:T(8,128)S(1)}) custom-call(bf16[32,3072]{1,0:T(8,128)(2,1)S(1)} %get-tuple-element.42.refs_0_.refs_4_, bf16[32,3072]{1,0:T(8,128)(2,1)S(1)} %collective-permute-done.refs_1_, bf16[32,3072]{1,0:T(8,128)(2,1)S(1)} %collective-permute-done.1.refs_2_, ...), custom_call_target="tpu_custom_call" | custom-call | flops 3221225472 | bytes 12582912 | tf_op jit(solution)/shard_map/hidden_units/pallas_call | solution.py:124
  34.8 1.8 %slot_terms.1 = (bf16[32,3072]{1,0:T(8,128)(2,1)S(1)}, bf16[32,3072]{1,0:T(8,128)(2,1)S(1)}, bf16[32,3072]{1,0:T(8,128)(2,1)S(1)}, bf16[32,3072]{1,0:T(8,128)(2,...) custom-call(bf16[256,1024]{1,0:T(8,128)(2,1)S(1)} %get-tuple-element, ...), custom_call_target="tpu_custom_call" | custom-call | flops 1610612736 | bytes 6291456 | tf_op jit(solution)/shard_map/slot_terms/pallas_call | solution.py:152
  37.5 1.6 %collective-permute-start.10 = (bf16[32,3072]{1,0:T(8,128)(2,1)S(1)}, bf16[32,3072]{1,0:T(8,128)(2,1)S(1)}, u32[]{:S(2)}, u32[]{:S(2)}) collective-permute-start(bf16[32,3072]{1,0:T(8,128)(2,1)S(1)} %get-tuple-element.53), channel_id=1, source_target_pairs={{0,8},{4,15},{8,0},{12,5},{1,9},{5,12},{9,1},{13,6},{2,10},{6,13},... | collective-permute-start | bytes 589832 | tf_op jit(solution)/shard_map/ppermute | solution.py:31
  39.5 2.7 %collective-permute-start.15 = (bf16[32,3072]{1,0:T(8,128)(2,1)S(1)}, bf16[32,3072]{1,0:T(8,128)(2,1)S(1)}, u32[]{:S(2)}, u32[]{:S(2)}) collective-permute-start(bf16[32,3072]{1,0:T(8,128)(2,1)S(1)} %get-tuple-element.59), channel_id=1, source_target_pairs={{0,24},{4,63},{8,16},{12,53},{1,25},{5,60},{9,17},{13,54},{2,26},{... | collective-permute-start | bytes 589832 | tf_op jit(solution)/shard_map/ppermute | solution.py:31
  43.9 2.9 %collective-permute-done.14 = bf16[32,3072]{1,0:T(8,128)(2,1)S(1)} collective-permute-done((bf16[32,3072]{1,0:T(8,128)(2,1)S(1)}, bf16[32,3072]{1,0:T(8,128)(2,1)S(1)}, u32[]{:S(2)}, u32[]{:S(2)}) %collective-permute-start.14) | collective-permute-done | bytes 196640 | tf_op jit(solution)/shard_map/ppermute | solution.py:31
  48.1 2.5 %collective-permute-start.16 = (bf16[32,3072]{1,0:T(8,128)(2,1)S(1)}, bf16[32,3072]{1,0:T(8,128)(2,1)S(1)}, u32[]{:S(2)}, u32[]{:S(2)}) collective-permute-start(bf16[32,3072]{1,0:T(8,128)(2,1)S(1)} %add_convert_fusion.3), channel_id=1, source_target_pairs={{0,16},{4,52},{8,24},{12,60},{1,17},{5,53},{9,25},{13,61},{2,18},{... | collective-permute-start | bytes 589832 | tf_op jit(solution)/shard_map/ppermute | solution.py:31
  50.6 4.4 %collective-permute-done.16.refs_3_ = bf16[32,3072]{1,0:T(8,128)(2,1)S(1)} collective-permute-done((bf16[32,3072]{1,0:T(8,128)(2,1)S(1)}, bf16[32,3072]{1,0:T(8,128)(2,1)S(1)}, u32[]{:S(2)}, u32[]{:S(2)}) %collective-permute-start.16) | collective-permute-done | bytes 196640 | tf_op jit(solution)/shard_map/ppermute | solution.py:31
  56.9 2.1 %collective-permute-start.18 = (bf16[32,3200]{1,0:T(8,128)(2,1)S(1)}, bf16[32,3200]{1,0:T(8,128)(2,1)S(1)}, u32[]{:S(2)}, u32[]{:S(2)}) collective-permute-start(bf16[32,3200]{1,0:T(8,128)(2,1)S(1)} %get-tuple-element.65.refs_4_.refs_0_), channel_id=1, source_target_pairs={{0,48},{4,20},{8,56},{12,28},{1,49},{5,21},{9,57},{13,29},{2,50},{... | collective-permute-start | bytes 614408 | tf_op jit(solution)/shard_map/ppermute | solution.py:31
  59.0 5.6 %collective-permute-done.17.refs_5_.refs_1_ = bf16[32,3200]{1,0:T(8,128)(2,1)S(1)} collective-permute-done((bf16[32,3200]{1,0:T(8,128)(2,1)S(1)}, bf16[32,3200]{1,0:T(8,128)(2,1)S(1)}, u32[]{:S(2)}, u32[]{:S(2)}) %collective-permute-start.17) | collective-permute-done | bytes 204832 | tf_op jit(solution)/shard_map/ppermute | solution.py:31
  64.7 4.7 %collective-permute-start.23 = (bf16[32,3200]{1,0:T(8,128)(2,1)S(1)}, bf16[32,3200]{1,0:T(8,128)(2,1)S(1)}, u32[]{:S(2)}, u32[]{:S(2)}) collective-permute-start(bf16[32,3200]{1,0:T(8,128)(2,1)S(1)} %collective-permute-done.18.refs_6_.refs_2_), channel_id=1, source_target_pairs={{0,56},{4,31},{8,48},{12,21},{1,57},{5,28},{9,49},{13,22},{2,58},{... | collective-permute-start | bytes 614408 | tf_op jit(solution)/shard_map/ppermute | solution.py:31
  69.4 2.0 %collective-permute-start.21 = (bf16[32,3200]{1,0:T(8,128)(2,1)S(1)}, bf16[32,3200]{1,0:T(8,128)(2,1)S(1)}, u32[]{:S(2)}, u32[]{:S(2)}) collective-permute-start(bf16[32,3200]{1,0:T(8,128)(2,1)S(1)} %collective-permute-done.17.refs_5_.refs_1_), channel_id=1, source_target_pairs={{0,8},{4,15},{8,0},{12,5},{1,9},{5,12},{9,1},{13,6},{2,10},{6,13},... | collective-permute-start | bytes 614408 | tf_op jit(solution)/shard_map/ppermute | solution.py:31
  71.4 2.4 %collective-permute-done.19.refs_7_.refs_3_ = bf16[32,3200]{1,0:T(8,128)(2,1)S(1)} collective-permute-done((bf16[32,3200]{1,0:T(8,128)(2,1)S(1)}, bf16[32,3200]{1,0:T(8,128)(2,1)S(1)}, u32[]{:S(2)}, u32[]{:S(2)}) %collective-permute-start.19) | collective-permute-done | bytes 204832 | tf_op jit(solution)/shard_map/ppermute | solution.py:31
  75.7 1.9 %collective-permute-start.25 = (f32[8,3200]{1,0:T(8,128)S(1)}, f32[8,3200]{1,0:T(8,128)S(1)}, u32[]{:S(2)}, u32[]{:S(2)}) collective-permute-start(f32[8,3200]{1,0:T(8,128)S(1)} %add.67), channel_id=1, source_target_pairs={{0,64},{64,0},{128,192},{192,128},{1,65},{65,1},{129,193},{193,129... | collective-permute-start | bytes 307208 | tf_op jit(solution)/shard_map/ppermute | solution.py:414
  77.6 2.1 %hidden_grads.1 = (bf16[256,1024]{1,0:T(8,128)(2,1)S(1)}, bf16[256,1024]{1,0:T(8,128)(2,1)S(1)}) custom-call(bf16[32,3200]{1,0:T(8,128)(2,1)S(1)} %get-tuple-element.65.refs_4_.refs_0_, bf16[32,3200]{1,0:T(8,128)(2,1)S(1)} %collective-permute-done.17.refs_5_.refs_1_, bf16[32,3200]{1,0:T(8,128)(2,1)S(1)} %collective-permute-done.18.refs_6_.refs_2_, ...), custom_call_target="tpu_custom_call" | custom-call | flops 1610612736 | bytes 6291456 | tf_op jit(solution)/shard_map/hidden_grads/pallas_call | solution.py:181
  81.0 3.3 %collective-permute-start.33 = (f32[8,3200]{1,0:T(8,128)S(1)}, f32[8,3200]{1,0:T(8,128)S(1)}, u32[]{:S(2)}, u32[]{:S(2)}) collective-permute-start(f32[8,3200]{1,0:T(8,128)S(1)} %add.68), channel_id=1, source_target_pairs={{0,128},{64,192},{128,0},{192,64},{1,129},{65,193},{129,1},{193,65... | collective-permute-start | bytes 307208 | tf_op jit(solution)/shard_map/ppermute | solution.py:416
  84.3 3.4 %slot_grads.1 = (bf16[32,3072]{1,0:T(8,128)(2,1)S(1)}, bf16[32,3072]{1,0:T(8,128)(2,1)S(1)}, bf16[32,3072]{1,0:T(8,128)(2,1)S(1)}, bf16[32,3072]{1,0:T(8,128)(2,...) custom-call(bf16[256,1024]{1,0:T(8,128)(2,1)S(1)} %get-tuple-element, ...), custom_call_target="tpu_custom_call" | custom-call | flops 3221225472 | bytes 12582912 | tf_op jit(solution)/shard_map/slot_grads/pallas_call | solution.py:213
  87.7 1.5 %collective-permute-start.27 = (bf16[32,3072]{1,0:T(8,128)(2,1)S(1)}, bf16[32,3072]{1,0:T(8,128)(2,1)S(1)}, u32[]{:S(2)}, u32[]{:S(2)}) collective-permute-start(bf16[32,3072]{1,0:T(8,128)(2,1)S(1)} %get-tuple-element.75), channel_id=1, source_target_pairs={{0,48},{4,20},{8,56},{12,28},{1,49},{5,21},{9,57},{13,29},{2,50},{... | collective-permute-start | bytes 589832 | tf_op jit(solution)/shard_map/ppermute | solution.py:31
  89.2 1.3 %collective-permute-start.28 = (bf16[32,3072]{1,0:T(8,128)(2,1)S(1)}, bf16[32,3072]{1,0:T(8,128)(2,1)S(1)}, u32[]{:S(2)}, u32[]{:S(2)}) collective-permute-start(bf16[32,3072]{1,0:T(8,128)(2,1)S(1)} %get-tuple-element.76), channel_id=1, source_target_pairs={{0,8},{4,15},{8,0},{12,5},{1,9},{5,12},{9,1},{13,6},{2,10},{6,13},... | collective-permute-start | bytes 589832 | tf_op jit(solution)/shard_map/ppermute | solution.py:31
  95.4 3.3 %collective-permute-start.29 = (bf16[32,3072]{1,0:T(8,128)(2,1)S(1)}, bf16[32,3072]{1,0:T(8,128)(2,1)S(1)}, u32[]{:S(2)}, u32[]{:S(2)}) collective-permute-start(bf16[32,3072]{1,0:T(8,128)(2,1)S(1)} %add_convert_fusion.2), channel_id=1, source_target_pairs={{0,48},{4,20},{8,56},{12,28},{1,49},{5,21},{9,57},{13,29},{2,50},{... | collective-permute-start | bytes 589832 | tf_op jit(solution)/shard_map/ppermute | solution.py:31
  99.5 2.7 %collective-permute-done.31 = bf16[32,3072]{1,0:T(8,128)(2,1)S(1)} collective-permute-done((bf16[32,3072]{1,0:T(8,128)(2,1)S(1)}, bf16[32,3072]{1,0:T(8,128)(2,1)S(1)}, u32[]{:S(2)}, u32[]{:S(2)}) %collective-permute-start.31) | collective-permute-done | bytes 196640 | tf_op jit(solution)/shard_map/ppermute | solution.py:31
  102.3 2.1 %collective-permute-start.32 = (bf16[32,3072]{1,0:T(8,128)(2,1)S(1)}, bf16[32,3072]{1,0:T(8,128)(2,1)S(1)}, u32[]{:S(2)}, u32[]{:S(2)}) collective-permute-start(bf16[32,3072]{1,0:T(8,128)(2,1)S(1)} %add_convert_fusion.1), channel_id=1, source_target_pairs={{0,16},{4,52},{8,24},{12,60},{1,17},{5,53},{9,25},{13,61},{2,18},{... | collective-permute-start | bytes 589832 | tf_op jit(solution)/shard_map/ppermute | solution.py:31
  105.7 3.6 %collective-permute-done.32 = bf16[32,3072]{1,0:T(8,128)(2,1)S(1)} collective-permute-done((bf16[32,3072]{1,0:T(8,128)(2,1)S(1)}, bf16[32,3072]{1,0:T(8,128)(2,1)S(1)}, u32[]{:S(2)}, u32[]{:S(2)}) %collective-permute-start.32) | collective-permute-done | bytes 196640 | tf_op jit(solution)/shard_map/ppermute | solution.py:31
  109.3 1.3 %fusion.1 = bf16[128,3072]{1,0:T(8,128)(2,1)} fusion(bf16[32,128]{1,0:T(8,128)(2,1)S(1)} %get-tuple-element.88, bf16[128,3072]{1,0:T(8,128)(2,1)S(1)} %copy-done.8, bf16[128,3072]{1,0:T(8,128)(2,1)S(1)} %copy-done.2, pred[128]{0:T(512)(128)(4,1)S(1)} %bitcast.47, f32[32,3072]{1,0:T(8,128)S(1)} %get-tuple-element.64, ...), kind=kOutput, calls=%fused_computation.3 | convolution fusion | flops 28409856 | bytes 3547264 | tf_op jit(solution)/shard_map/dot_general | solution.py:423
  (95 shorter events, 23.2 us)
Async XLA Ops:
  2.8 26.3 %collective-permute-start.7 = (bf16[3072,512]{1,0:T(8,128)(2,1)}, bf16[3072,512]{1,0:T(8,128)(2,1)S(1)}, u32[]{:S(2)}, u32[]{:S(2)}) collective-permute-start(bf16[3072,512]{1,0:T(8,128)(2,1)} %gate), channel_id=1, source_target_pairs={{0,4},{4,0},{8,12},{12,8},{1,5},{5,1},{9,13},{13,9},{2,6},{6,2},{1... | collective-permute-start | bytes 9437192 | tf_op jit(solution)/shard_map/ppermute | solution.py:31
  2.9 26.2 %collective-permute-start.8 = (bf16[3072,512]{1,0:T(8,128)(2,1)}, bf16[3072,512]{1,0:T(8,128)(2,1)S(1)}, u32[]{:S(2)}, u32[]{:S(2)}) collective-permute-start(bf16[3072,512]{1,0:T(8,128)(2,1)} %up.1), channel_id=1, source_target_pairs={{0,4},{4,0},{8,12},{12,8},{1,5},{5,1},{9,13},{13,9},{2,6},{6,2},{1... | collective-permute-start | bytes 9437192 | tf_op jit(solution)/shard_map/ppermute | solution.py:31
  3.4 7.4 %collective-permute-start.1 = (bf16[32,3072]{1,0:T(8,128)(2,1)S(1)}, bf16[32,3072]{1,0:T(8,128)(2,1)S(1)}, u32[]{:S(2)}, u32[]{:S(2)}) collective-permute-start(bf16[32,3072]{1,0:T(8,128)(2,1)S(1)} %get-tuple-element.42.refs_0_.refs_4_), channel_id=1, source_target_pairs={{0,48},{4,20},{8,56},{12,28},{1,49},{5,21},{9,57},{13,29},{2,50},{... | collective-permute-start | bytes 589832 | tf_op jit(solution)/shard_map/ppermute | solution.py:31
  6.2 13.9 %collective-permute-start = (bf16[32,3072]{1,0:T(8,128)(2,1)S(1)}, bf16[32,3072]{1,0:T(8,128)(2,1)S(1)}, u32[]{:S(2)}, u32[]{:S(2)}) collective-permute-start(bf16[32,3072]{1,0:T(8,128)(2,1)S(1)} %get-tuple-element.42.refs_0_.refs_4_), channel_id=1, source_target_pairs={{0,16},{4,52},{8,24},{12,60},{1,17},{5,53},{9,25},{13,61},{2,18},{... | collective-permute-start | bytes 589832 | tf_op jit(solution)/shard_map/ppermute | solution.py:31
  6.2 14.1 %collective-permute-start.3 = (bf16[32,3072]{1,0:T(8,128)(2,1)S(1)}, bf16[32,3072]{1,0:T(8,128)(2,1)S(1)}, u32[]{:S(2)}, u32[]{:S(2)}) collective-permute-start(bf16[32,3072]{1,0:T(8,128)(2,1)S(1)} %get-tuple-element.42.refs_0_.refs_4_), channel_id=1, source_target_pairs={{0,8},{4,15},{8,0},{12,5},{1,9},{5,12},{9,1},{13,6},{2,10},{6,13},... | collective-permute-start | bytes 589832 | tf_op jit(solution)/shard_map/ppermute | solution.py:31
  10.8 11.4 %collective-permute-start.6 = (bf16[32,3072]{1,0:T(8,128)(2,1)S(1)}, bf16[32,3072]{1,0:T(8,128)(2,1)S(1)}, u32[]{:S(2)}, u32[]{:S(2)}) collective-permute-start(bf16[32,3072]{1,0:T(8,128)(2,1)S(1)} %collective-permute-done.1.refs_2_), channel_id=1, source_target_pairs={{0,56},{4,31},{8,48},{12,21},{1,57},{5,28},{9,49},{13,22},{2,58},{... | collective-permute-start | bytes 589832 | tf_op jit(solution)/shard_map/ppermute | solution.py:31
  20.1 5.8 %collective-permute-start.5 = (bf16[32,3072]{1,0:T(8,128)(2,1)S(1)}, bf16[32,3072]{1,0:T(8,128)(2,1)S(1)}, u32[]{:S(2)}, u32[]{:S(2)}) collective-permute-start(bf16[32,3072]{1,0:T(8,128)(2,1)S(1)} %collective-permute-done.1.refs_2_), channel_id=1, source_target_pairs={{0,8},{4,15},{8,0},{12,5},{1,9},{5,12},{9,1},{13,6},{2,10},{6,13},... | collective-permute-start | bytes 589832 | tf_op jit(solution)/shard_map/ppermute | solution.py:31
  20.3 7.7 %collective-permute-start.4 = (bf16[32,3072]{1,0:T(8,128)(2,1)S(1)}, bf16[32,3072]{1,0:T(8,128)(2,1)S(1)}, u32[]{:S(2)}, u32[]{:S(2)}) collective-permute-start(bf16[32,3072]{1,0:T(8,128)(2,1)S(1)} %collective-permute-done.refs_1_), channel_id=1, source_target_pairs={{0,8},{4,15},{8,0},{12,5},{1,9},{5,12},{9,1},{13,6},{2,10},{6,13},... | collective-permute-start | bytes 589832 | tf_op jit(solution)/shard_map/ppermute | solution.py:31
  22.2 6.9 %collective-permute-start.2 = (bf16[32,3072]{1,0:T(8,128)(2,1)S(1)}, bf16[32,3072]{1,0:T(8,128)(2,1)S(1)}, u32[]{:S(2)}, u32[]{:S(2)}) collective-permute-start(bf16[32,3072]{1,0:T(8,128)(2,1)S(1)} %collective-permute-done.refs_1_), channel_id=1, source_target_pairs={{0,16},{4,52},{8,24},{12,60},{1,17},{5,53},{9,25},{13,61},{2,18},{... | collective-permute-start | bytes 589832 | tf_op jit(solution)/shard_map/ppermute | solution.py:31
  36.5 5.7 %collective-permute-start.11 = (bf16[32,3072]{1,0:T(8,128)(2,1)S(1)}, bf16[32,3072]{1,0:T(8,128)(2,1)S(1)}, u32[]{:S(2)}, u32[]{:S(2)}) collective-permute-start(bf16[32,3072]{1,0:T(8,128)(2,1)S(1)} %get-tuple-element.55), channel_id=1, source_target_pairs={{0,48},{4,20},{8,56},{12,28},{1,49},{5,21},{9,57},{13,29},{2,50},{... | collective-permute-start | bytes 589832 | tf_op jit(solution)/shard_map/ppermute | solution.py:31
  36.6 5.9 %collective-permute-start.12 = (bf16[32,3072]{1,0:T(8,128)(2,1)S(1)}, bf16[32,3072]{1,0:T(8,128)(2,1)S(1)}, u32[]{:S(2)}, u32[]{:S(2)}) collective-permute-start(bf16[32,3072]{1,0:T(8,128)(2,1)S(1)} %get-tuple-element.56), channel_id=1, source_target_pairs={{0,8},{4,15},{8,0},{12,5},{1,9},{5,12},{9,1},{13,6},{2,10},{6,13},... | collective-permute-start | bytes 589832 | tf_op jit(solution)/shard_map/ppermute | solution.py:31
  37.5 13.1 %collective-permute-start.10 = (bf16[32,3072]{1,0:T(8,128)(2,1)S(1)}, bf16[32,3072]{1,0:T(8,128)(2,1)S(1)}, u32[]{:S(2)}, u32[]{:S(2)}) collective-permute-start(bf16[32,3072]{1,0:T(8,128)(2,1)S(1)} %get-tuple-element.53), channel_id=1, source_target_pairs={{0,8},{4,15},{8,0},{12,5},{1,9},{5,12},{9,1},{13,6},{2,10},{6,13},... | collective-permute-start | bytes 589832 | tf_op jit(solution)/shard_map/ppermute | solution.py:31
  39.0 7.8 %collective-permute-start.14 = (bf16[32,3072]{1,0:T(8,128)(2,1)S(1)}, bf16[32,3072]{1,0:T(8,128)(2,1)S(1)}, u32[]{:S(2)}, u32[]{:S(2)}) collective-permute-start(bf16[32,3072]{1,0:T(8,128)(2,1)S(1)} %get-tuple-element.58), channel_id=1, source_target_pairs={{0,8},{4,15},{8,0},{12,5},{1,9},{5,12},{9,1},{13,6},{2,10},{6,13},... | collective-permute-start | bytes 589832 | tf_op jit(solution)/shard_map/ppermute | solution.py:31
  39.5 8.4 %collective-permute-start.15 = (bf16[32,3072]{1,0:T(8,128)(2,1)S(1)}, bf16[32,3072]{1,0:T(8,128)(2,1)S(1)}, u32[]{:S(2)}, u32[]{:S(2)}) collective-permute-start(bf16[32,3072]{1,0:T(8,128)(2,1)S(1)} %get-tuple-element.59), channel_id=1, source_target_pairs={{0,24},{4,63},{8,16},{12,53},{1,25},{5,60},{9,17},{13,54},{2,26},{... | collective-permute-start | bytes 589832 | tf_op jit(solution)/shard_map/ppermute | solution.py:31
  42.7 7.9 %collective-permute-start.13 = (bf16[32,3072]{1,0:T(8,128)(2,1)S(1)}, bf16[32,3072]{1,0:T(8,128)(2,1)S(1)}, u32[]{:S(2)}, u32[]{:S(2)}) collective-permute-start(bf16[32,3072]{1,0:T(8,128)(2,1)S(1)} %add_convert_fusion.4), channel_id=1, source_target_pairs={{0,48},{4,20},{8,56},{12,28},{1,49},{5,21},{9,57},{13,29},{2,50},{... | collective-permute-start | bytes 589832 | tf_op jit(solution)/shard_map/ppermute | solution.py:31
  48.1 7.0 %collective-permute-start.16 = (bf16[32,3072]{1,0:T(8,128)(2,1)S(1)}, bf16[32,3072]{1,0:T(8,128)(2,1)S(1)}, u32[]{:S(2)}, u32[]{:S(2)}) collective-permute-start(bf16[32,3072]{1,0:T(8,128)(2,1)S(1)} %add_convert_fusion.3), channel_id=1, source_target_pairs={{0,16},{4,52},{8,24},{12,60},{1,17},{5,53},{9,25},{13,61},{2,18},{... | collective-permute-start | bytes 589832 | tf_op jit(solution)/shard_map/ppermute | solution.py:31
  55.7 9.0 %collective-permute-start.17 = (bf16[32,3200]{1,0:T(8,128)(2,1)S(1)}, bf16[32,3200]{1,0:T(8,128)(2,1)S(1)}, u32[]{:S(2)}, u32[]{:S(2)}) collective-permute-start(bf16[32,3200]{1,0:T(8,128)(2,1)S(1)} %get-tuple-element.65.refs_4_.refs_0_), channel_id=1, source_target_pairs={{0,16},{4,52},{8,24},{12,60},{1,17},{5,53},{9,25},{13,61},{2,18},{... | collective-permute-start | bytes 614408 | tf_op jit(solution)/shard_map/ppermute | solution.py:31
  56.9 7.7 %collective-permute-start.18 = (bf16[32,3200]{1,0:T(8,128)(2,1)S(1)}, bf16[32,3200]{1,0:T(8,128)(2,1)S(1)}, u32[]{:S(2)}, u32[]{:S(2)}) collective-permute-start(bf16[32,3200]{1,0:T(8,128)(2,1)S(1)} %get-tuple-element.65.refs_4_.refs_0_), channel_id=1, source_target_pairs={{0,48},{4,20},{8,56},{12,28},{1,49},{5,21},{9,57},{13,29},{2,50},{... | collective-permute-start | bytes 614408 | tf_op jit(solution)/shard_map/ppermute | solution.py:31
  64.7 9.2 %collective-permute-start.19 = (bf16[32,3200]{1,0:T(8,128)(2,1)S(1)}, bf16[32,3200]{1,0:T(8,128)(2,1)S(1)}, u32[]{:S(2)}, u32[]{:S(2)}) collective-permute-start(bf16[32,3200]{1,0:T(8,128)(2,1)S(1)} %collective-permute-done.17.refs_5_.refs_1_), channel_id=1, source_target_pairs={{0,16},{4,52},{8,24},{12,60},{1,17},{5,53},{9,25},{13,61},{2,18},{... | collective-permute-start | bytes 614408 | tf_op jit(solution)/shard_map/ppermute | solution.py:31
  64.7 13.0 %collective-permute-start.20 = (bf16[32,3200]{1,0:T(8,128)(2,1)S(1)}, bf16[32,3200]{1,0:T(8,128)(2,1)S(1)}, u32[]{:S(2)}, u32[]{:S(2)}) collective-permute-start(bf16[32,3200]{1,0:T(8,128)(2,1)S(1)} %get-tuple-element.65.refs_4_.refs_0_), channel_id=1, source_target_pairs={{0,8},{4,15},{8,0},{12,5},{1,9},{5,12},{9,1},{13,6},{2,10},{6,13},... | collective-permute-start | bytes 614408 | tf_op jit(solution)/shard_map/ppermute | solution.py:31
  64.7 12.9 %collective-permute-start.23 = (bf16[32,3200]{1,0:T(8,128)(2,1)S(1)}, bf16[32,3200]{1,0:T(8,128)(2,1)S(1)}, u32[]{:S(2)}, u32[]{:S(2)}) collective-permute-start(bf16[32,3200]{1,0:T(8,128)(2,1)S(1)} %collective-permute-done.18.refs_6_.refs_2_), channel_id=1, source_target_pairs={{0,56},{4,31},{8,48},{12,21},{1,57},{5,28},{9,49},{13,22},{2,58},{... | collective-permute-start | bytes 614408 | tf_op jit(solution)/shard_map/ppermute | solution.py:31
  69.4 8.3 %collective-permute-start.22 = (bf16[32,3200]{1,0:T(8,128)(2,1)S(1)}, bf16[32,3200]{1,0:T(8,128)(2,1)S(1)}, u32[]{:S(2)}, u32[]{:S(2)}) collective-permute-start(bf16[32,3200]{1,0:T(8,128)(2,1)S(1)} %collective-permute-done.18.refs_6_.refs_2_), channel_id=1, source_target_pairs={{0,8},{4,15},{8,0},{12,5},{1,9},{5,12},{9,1},{13,6},{2,10},{6,13},... | collective-permute-start | bytes 614408 | tf_op jit(solution)/shard_map/ppermute | solution.py:31
  69.4 8.3 %collective-permute-start.21 = (bf16[32,3200]{1,0:T(8,128)(2,1)S(1)}, bf16[32,3200]{1,0:T(8,128)(2,1)S(1)}, u32[]{:S(2)}, u32[]{:S(2)}) collective-permute-start(bf16[32,3200]{1,0:T(8,128)(2,1)S(1)} %collective-permute-done.17.refs_5_.refs_1_), channel_id=1, source_target_pairs={{0,8},{4,15},{8,0},{12,5},{1,9},{5,12},{9,1},{13,6},{2,10},{6,13},... | collective-permute-start | bytes 614408 | tf_op jit(solution)/shard_map/ppermute | solution.py:31
  81.0 12.8 %collective-permute-start.33 = (f32[8,3200]{1,0:T(8,128)S(1)}, f32[8,3200]{1,0:T(8,128)S(1)}, u32[]{:S(2)}, u32[]{:S(2)}) collective-permute-start(f32[8,3200]{1,0:T(8,128)S(1)} %add.68), channel_id=1, source_target_pairs={{0,128},{64,192},{128,0},{192,64},{1,129},{65,193},{129,1},{193,65... | collective-permute-start | bytes 307208 | tf_op jit(solution)/shard_map/ppermute | solution.py:416
  87.7 6.9 %collective-permute-start.27 = (bf16[32,3072]{1,0:T(8,128)(2,1)S(1)}, bf16[32,3072]{1,0:T(8,128)(2,1)S(1)}, u32[]{:S(2)}, u32[]{:S(2)}) collective-permute-start(bf16[32,3072]{1,0:T(8,128)(2,1)S(1)} %get-tuple-element.75), channel_id=1, source_target_pairs={{0,48},{4,20},{8,56},{12,28},{1,49},{5,21},{9,57},{13,29},{2,50},{... | collective-permute-start | bytes 589832 | tf_op jit(solution)/shard_map/ppermute | solution.py:31
  89.2 6.2 %collective-permute-start.28 = (bf16[32,3072]{1,0:T(8,128)(2,1)S(1)}, bf16[32,3072]{1,0:T(8,128)(2,1)S(1)}, u32[]{:S(2)}, u32[]{:S(2)}) collective-permute-start(bf16[32,3072]{1,0:T(8,128)(2,1)S(1)} %get-tuple-element.76), channel_id=1, source_target_pairs={{0,8},{4,15},{8,0},{12,5},{1,9},{5,12},{9,1},{13,6},{2,10},{6,13},... | collective-permute-start | bytes 589832 | tf_op jit(solution)/shard_map/ppermute | solution.py:31
  91.7 14.0 %collective-permute-start.26 = (bf16[32,3072]{1,0:T(8,128)(2,1)S(1)}, bf16[32,3072]{1,0:T(8,128)(2,1)S(1)}, u32[]{:S(2)}, u32[]{:S(2)}) collective-permute-start(bf16[32,3072]{1,0:T(8,128)(2,1)S(1)} %get-tuple-element.73), channel_id=1, source_target_pairs={{0,8},{4,15},{8,0},{12,5},{1,9},{5,12},{9,1},{13,6},{2,10},{6,13},... | collective-permute-start | bytes 589832 | tf_op jit(solution)/shard_map/ppermute | solution.py:31
  92.5 7.1 %collective-permute-start.30 = (bf16[32,3072]{1,0:T(8,128)(2,1)S(1)}, bf16[32,3072]{1,0:T(8,128)(2,1)S(1)}, u32[]{:S(2)}, u32[]{:S(2)}) collective-permute-start(bf16[32,3072]{1,0:T(8,128)(2,1)S(1)} %get-tuple-element.78), channel_id=1, source_target_pairs={{0,8},{4,15},{8,0},{12,5},{1,9},{5,12},{9,1},{13,6},{2,10},{6,13},... | collective-permute-start | bytes 589832 | tf_op jit(solution)/shard_map/ppermute | solution.py:31
  93.8 8.5 %collective-permute-start.31 = (bf16[32,3072]{1,0:T(8,128)(2,1)S(1)}, bf16[32,3072]{1,0:T(8,128)(2,1)S(1)}, u32[]{:S(2)}, u32[]{:S(2)}) collective-permute-start(bf16[32,3072]{1,0:T(8,128)(2,1)S(1)} %get-tuple-element.79), channel_id=1, source_target_pairs={{0,24},{4,63},{8,16},{12,53},{1,25},{5,60},{9,17},{13,54},{2,26},{... | collective-permute-start | bytes 589832 | tf_op jit(solution)/shard_map/ppermute | solution.py:31
  94.6 9.9 %collective-permute-start.34 = (f32[8,3200]{1,0:T(8,128)S(1)}, f32[8,3200]{1,0:T(8,128)S(1)}, u32[]{:S(2)}, u32[]{:S(2)}) collective-permute-start(f32[8,3200]{1,0:T(8,128)S(1)} %add.77), channel_id=1, source_target_pairs={{0,8},{4,12},{8,0},{12,4},{1,9},{5,13},{9,1},{13,5},{2,10},{6,14},... | collective-permute-start | bytes 307208 | tf_op jit(solution)/shard_map/ppermute | solution.py:31
  95.4 10.3 %collective-permute-start.29 = (bf16[32,3072]{1,0:T(8,128)(2,1)S(1)}, bf16[32,3072]{1,0:T(8,128)(2,1)S(1)}, u32[]{:S(2)}, u32[]{:S(2)}) collective-permute-start(bf16[32,3072]{1,0:T(8,128)(2,1)S(1)} %add_convert_fusion.2), channel_id=1, source_target_pairs={{0,48},{4,20},{8,56},{12,28},{1,49},{5,21},{9,57},{13,29},{2,50},{... | collective-permute-start | bytes 589832 | tf_op jit(solution)/shard_map/ppermute | solution.py:31
  102.3 7.0 %collective-permute-start.32 = (bf16[32,3072]{1,0:T(8,128)(2,1)S(1)}, bf16[32,3072]{1,0:T(8,128)(2,1)S(1)}, u32[]{:S(2)}, u32[]{:S(2)}) collective-permute-start(bf16[32,3072]{1,0:T(8,128)(2,1)S(1)} %add_convert_fusion.1), channel_id=1, source_target_pairs={{0,16},{4,52},{8,24},{12,60},{1,17},{5,53},{9,25},{13,61},{2,18},{... | collective-permute-start | bytes 589832 | tf_op jit(solution)/shard_map/ppermute | solution.py:31
  (13 other events, 53.4 us)

commit v3 on v2

--- a/solution.py
+++ b/solution.py
@@ -71,10 +71,11 @@
     f1 = ahead(own)
     b1 = behind(own)
     z0 = across(own)
-    x2 = ahead(after(f1, *others))
-    zf1 = across(f1)
-    zb1 = across(b1)
-    zx2 = behind_across(b1)
+    f1_late, b1_late = after(f1, *others), after(b1, *others)
+    x2 = ahead(f1_late)
+    zf1 = across(f1_late)
+    zb1 = across(b1_late)
+    zx2 = behind_across(b1_late)
     return [own, f1, b1, x2, z0, zf1, zb1, zx2]
 
 
@@ -88,7 +89,7 @@
     got_x2 = behind(x2)
     got_zf1 = across(zf1)
     got_zb1 = across(zb1)
-    got_z0 = across(z0)
+    got_z0 = across(after(z0, got_x2))
     got_f1 = behind(add(f1, got_x2, got_zf1))
     got_b1 = ahead(add(b1, got_zb1, got_zx2))
     return [own, got_z0, got_f1, got_b1]
@@ -404,9 +405,9 @@
     base = jnp.where(sub == 0, jnp.sum(plain_loss[:, None] * lang_hot, axis=0)[None, :], jnp.sum(lang_hot, axis=0)[None, :])
 
     combined, grad_slots, so_far = slots(scatter(terms), token_slots, teacher_slots, aux, slot_langs, base, router_weight.T)
-    grad_blocks = gather(grad_slots)
     placed = lax.dot_general(placing_half, combined, TN, preferred_element_type=f32)
     layer_out = jnp.where(chosen[:, None], placed.astype(bf16), tokens)
+    grad_blocks = gather(grad_slots, layer_out)
 
     summed = router_sum(token_blocks[:PLANE], grad_blocks[:PLANE], experts)
     summed = summed + twin(summed)

time: 112 us -> 107 us (0.955)
  starting transfers between devices: 48.7 us -> 44.4 us
  waiting for transfers between devices: 36.7 us -> 35.4 us
    ppermute x33, starting transfers between devices: 43.6 us -> 39.2 us  [move(): return lax.ppermute(value, GROUP, pairs)]
    ppermute x33, waiting for transfers between devices: 35.5 us -> 34.2 us  [move(): return lax.ppermute(value, GROUP, pairs)]
  transfers between devices with their start and end apart: 35 -> 35, of which waited for: 16 -> 16; matrix products, arithmetic and copies ran while one was open for 4% -> 4% of each run, Pallas kernels for 9% -> 6%
where the time goes in v3:
time: 107 us; the launch traced here: 105 us
  starting transfers between devices  44.4 us (41%)
  waiting for transfers between devices  35.4 us (33%)
  Pallas kernels  12.7 us (12%)
  local copies, waits for them, and re-layouts  6.49 us (6%)
  matrix products  3.19 us (3%)
  other arithmetic  1.77 us (2%)
    ppermute x33, starting transfers between devices, move(): return lax.ppermute(value, GROUP, pairs)  39.2 us
    ppermute x33, waiting for transfers between devices, move(): return lax.ppermute(value, GROUP, pairs)  34.2 us
    unnamed x20, local copies, waits for them, and re-layouts  5.9 us
    pallas_call x1, Pallas kernels, slot_grads(): pl.pallas_call(slot_grad_kernel, name='slot_grads', out_shape=[jax.ShapeD...  3.44 us
    pallas_call x1, Pallas kernels, hidden_units(): pl.pallas_call(hidden_kernel, name='hidden_units', out_shape=[jax.ShapeDt...  3.42 us
    ppermute x1, starting transfers between devices, local(): lax.ppermute(summed, 'expert', [(i, i ^ 2) for i in range(4)])  3.29 us
  transfers between devices with their start and end apart: 35, of which 16 were waited for; matrix products, arithmetic and copies ran while one was open for 4% of the time, Pallas kernels for 6%

profile of v3, /device:TPU:64, one launch (start us, length us, event | category | flops | bytes accessed | tf_op | source)
XLA Modules:
  0.0 105.0 jit_solution(13310029315834208253)
XLA Ops:
  4.9 1.7 %collective-permute-start.1 = (bf16[32,3072]{1,0:T(8,128)(2,1)S(1)}, bf16[32,3072]{1,0:T(8,128)(2,1)S(1)}, u32[]{:S(2)}, u32[]{:S(2)}) collective-permute-start(bf16[32,3072]{1,0:T(8,128)(2,1)S(1)} %get-tuple-element.47.refs_0_.refs_4_), channel_id=1, source_target_pairs={{0,48},{4,20},{8,56},{12,28},{1,49},{5,21},{9,57},{13,29},{2,50},{... | collective-permute-start | bytes 589832 | tf_op jit(solution)/shard_map/ppermute | solution.py:31
  6.7 1.9 %collective-permute-start.3 = (bf16[32,3072]{1,0:T(8,128)(2,1)S(1)}, bf16[32,3072]{1,0:T(8,128)(2,1)S(1)}, u32[]{:S(2)}, u32[]{:S(2)}) collective-permute-start(bf16[32,3072]{1,0:T(8,128)(2,1)S(1)} %get-tuple-element.47.refs_0_.refs_4_), channel_id=1, source_target_pairs={{0,8},{4,15},{8,0},{12,5},{1,9},{5,12},{9,1},{13,6},{2,10},{6,13},... | collective-permute-start | bytes 589832 | tf_op jit(solution)/shard_map/ppermute | solution.py:31
  8.6 1.9 %copy-done.3 = bf16[3072,512]{1,0:T(8,128)(2,1)S(1)} copy-done((bf16[3072,512]{1,0:T(8,128)(2,1)S(1)}, bf16[3072,512]{1,0:T(8,128)(2,1)}, u32[]{:S(2)}) %copy-start.3) | copy-done | bytes 3145752
  10.5 1.9 %copy-done.4 = bf16[3072,512]{1,0:T(8,128)(2,1)S(1)} copy-done((bf16[3072,512]{1,0:T(8,128)(2,1)S(1)}, bf16[3072,512]{1,0:T(8,128)(2,1)}, u32[]{:S(2)}) %copy-start.4) | copy-done | bytes 3145752
  15.2 4.6 %collective-permute-done.2.refs_3_ = bf16[32,3072]{1,0:T(8,128)(2,1)S(1)} collective-permute-done((bf16[32,3072]{1,0:T(8,128)(2,1)S(1)}, bf16[32,3072]{1,0:T(8,128)(2,1)S(1)}, u32[]{:S(2)}, u32[]{:S(2)}) %collective-permute-start.2) | collective-permute-done | bytes 196640 | tf_op jit(solution)/shard_map/ppermute | solution.py:31
  21.0 5.4 %collective-permute-done.6.refs_7_ = bf16[32,3072]{1,0:T(8,128)(2,1)S(1)} collective-permute-done((bf16[32,3072]{1,0:T(8,128)(2,1)S(1)}, bf16[32,3072]{1,0:T(8,128)(2,1)S(1)}, u32[]{:S(2)}, u32[]{:S(2)}) %collective-permute-start.6) | collective-permute-done | bytes 196640 | tf_op jit(solution)/shard_map/ppermute | solution.py:31
  26.4 3.4 %hidden_units.1 = (bf16[256,1024]{1,0:T(8,128)(2,1)S(1)}, f32[256,1024]{1,0:T(8,128)S(1)}, f32[256,1024]{1,0:T(8,128)S(1)}) custom-call(bf16[32,3072]{1,0:T(8,128)(2,1)S(1)} %get-tuple-element.47.refs_0_.refs_4_, bf16[32,3072]{1,0:T(8,128)(2,1)S(1)} %collective-permute-done.refs_1_, bf16[32,3072]{1,0:T(8,128)(2,1)S(1)} %collective-permute-done.1.refs_2_, ...), custom_call_target="tpu_custom_call" | custom-call | flops 3221225472 | bytes 12582912 | tf_op jit(solution)/shard_map/hidden_units/pallas_call | solution.py:125
  32.0 1.8 %slot_terms.1 = (bf16[32,3072]{1,0:T(8,128)(2,1)S(1)}, bf16[32,3072]{1,0:T(8,128)(2,1)S(1)}, bf16[32,3072]{1,0:T(8,128)(2,1)S(1)}, bf16[32,3072]{1,0:T(8,128)(2,...) custom-call(bf16[256,1024]{1,0:T(8,128)(2,1)S(1)} %get-tuple-element, ...), custom_call_target="tpu_custom_call" | custom-call | flops 1610612736 | bytes 6291456 | tf_op jit(solution)/shard_map/slot_terms/pallas_call | solution.py:153
  33.8 1.6 %collective-permute-start.10 = (bf16[32,3072]{1,0:T(8,128)(2,1)S(1)}, bf16[32,3072]{1,0:T(8,128)(2,1)S(1)}, u32[]{:S(2)}, u32[]{:S(2)}) collective-permute-start(bf16[32,3072]{1,0:T(8,128)(2,1)S(1)} %get-tuple-element.60), channel_id=1, source_target_pairs={{0,48},{4,20},{8,56},{12,28},{1,49},{5,21},{9,57},{13,29},{2,50},{... | collective-permute-start | bytes 589832 | tf_op jit(solution)/shard_map/ppermute | solution.py:31
  35.4 2.1 %collective-permute-start.12 = (bf16[32,3072]{1,0:T(8,128)(2,1)S(1)}, bf16[32,3072]{1,0:T(8,128)(2,1)S(1)}, u32[]{:S(2)}, u32[]{:S(2)}) collective-permute-start(bf16[32,3072]{1,0:T(8,128)(2,1)S(1)} %get-tuple-element.63), channel_id=1, source_target_pairs={{0,8},{4,15},{8,0},{12,5},{1,9},{5,12},{9,1},{13,6},{2,10},{6,13},... | collective-permute-start | bytes 589832 | tf_op jit(solution)/shard_map/ppermute | solution.py:31
  39.0 2.6 %collective-permute-done.10 = bf16[32,3072]{1,0:T(8,128)(2,1)S(1)} collective-permute-done((bf16[32,3072]{1,0:T(8,128)(2,1)S(1)}, bf16[32,3072]{1,0:T(8,128)(2,1)S(1)}, u32[]{:S(2)}, u32[]{:S(2)}) %collective-permute-start.10) | collective-permute-done | bytes 196640 | tf_op jit(solution)/shard_map/ppermute | solution.py:31
  41.7 2.9 %collective-permute-start.13 = (bf16[32,3072]{1,0:T(8,128)(2,1)S(1)}, bf16[32,3072]{1,0:T(8,128)(2,1)S(1)}, u32[]{:S(2)}, u32[]{:S(2)}) collective-permute-start(bf16[32,3072]{1,0:T(8,128)(2,1)S(1)} %add_convert_fusion.4), channel_id=1, source_target_pairs={{0,48},{4,20},{8,56},{12,28},{1,49},{5,21},{9,57},{13,29},{2,50},{... | collective-permute-start | bytes 589832 | tf_op jit(solution)/shard_map/ppermute | solution.py:31
  46.0 1.6 %collective-permute-done.11.refs_1_ = bf16[32,3072]{1,0:T(8,128)(2,1)S(1)} collective-permute-done((bf16[32,3072]{1,0:T(8,128)(2,1)S(1)}, bf16[32,3072]{1,0:T(8,128)(2,1)S(1)}, u32[]{:S(2)}, u32[]{:S(2)}) %collective-permute-start.11) | collective-permute-done | bytes 196640 | tf_op jit(solution)/shard_map/ppermute | solution.py:31
  47.6 2.0 %collective-permute-done.13.refs_2_ = bf16[32,3072]{1,0:T(8,128)(2,1)S(1)} collective-permute-done((bf16[32,3072]{1,0:T(8,128)(2,1)S(1)}, bf16[32,3072]{1,0:T(8,128)(2,1)S(1)}, u32[]{:S(2)}, u32[]{:S(2)}) %collective-permute-start.13) | collective-permute-done | bytes 196640 | tf_op jit(solution)/shard_map/ppermute | solution.py:31
  49.6 3.0 %collective-permute-done.16.refs_3_ = bf16[32,3072]{1,0:T(8,128)(2,1)S(1)} collective-permute-done((bf16[32,3072]{1,0:T(8,128)(2,1)S(1)}, bf16[32,3072]{1,0:T(8,128)(2,1)S(1)}, u32[]{:S(2)}, u32[]{:S(2)}) %collective-permute-start.16) | collective-permute-done | bytes 196640 | tf_op jit(solution)/shard_map/ppermute | solution.py:31
  53.4 3.2 %collective-permute-start.18 = (bf16[32,3200]{1,0:T(8,128)(2,1)S(1)}, bf16[32,3200]{1,0:T(8,128)(2,1)S(1)}, u32[]{:S(2)}, u32[]{:S(2)}) collective-permute-start(bf16[32,3200]{1,0:T(8,128)(2,1)S(1)} %get-tuple-element.72.refs_4_.refs_0_), channel_id=1, source_target_pairs={{0,48},{4,20},{8,56},{12,28},{1,49},{5,21},{9,57},{13,29},{2,50},{... | collective-permute-start | bytes 614408 | tf_op jit(solution)/shard_map/ppermute | solution.py:31
  57.9 4.2 %collective-permute-done.17.refs_5_.refs_1_ = bf16[32,3200]{1,0:T(8,128)(2,1)S(1)} collective-permute-done((bf16[32,3200]{1,0:T(8,128)(2,1)S(1)}, bf16[32,3200]{1,0:T(8,128)(2,1)S(1)}, u32[]{:S(2)}, u32[]{:S(2)}) %collective-permute-start.17) | collective-permute-done | bytes 204832 | tf_op jit(solution)/shard_map/ppermute | solution.py:31
  62.1 2.0 %collective-permute-start.20 = (bf16[32,3200]{1,0:T(8,128)(2,1)S(1)}, bf16[32,3200]{1,0:T(8,128)(2,1)S(1)}, u32[]{:S(2)}, u32[]{:S(2)}) collective-permute-start(bf16[32,3200]{1,0:T(8,128)(2,1)S(1)} %get-tuple-element.72.refs_4_.refs_0_), channel_id=1, source_target_pairs={{0,8},{4,15},{8,0},{12,5},{1,9},{5,12},{9,1},{13,6},{2,10},{6,13},... | collective-permute-start | bytes 614408 | tf_op jit(solution)/shard_map/ppermute | solution.py:31
  64.1 2.0 %collective-permute-start.22 = (bf16[32,3200]{1,0:T(8,128)(2,1)S(1)}, bf16[32,3200]{1,0:T(8,128)(2,1)S(1)}, u32[]{:S(2)}, u32[]{:S(2)}) collective-permute-start(bf16[32,3200]{1,0:T(8,128)(2,1)S(1)} %collective-permute-done.18.refs_6_.refs_2_), channel_id=1, source_target_pairs={{0,8},{4,15},{8,0},{12,5},{1,9},{5,12},{9,1},{13,6},{2,10},{6,13},... | collective-permute-start | bytes 614408 | tf_op jit(solution)/shard_map/ppermute | solution.py:31
  66.1 2.7 %collective-permute-start.23 = (bf16[32,3200]{1,0:T(8,128)(2,1)S(1)}, bf16[32,3200]{1,0:T(8,128)(2,1)S(1)}, u32[]{:S(2)}, u32[]{:S(2)}) collective-permute-start(bf16[32,3200]{1,0:T(8,128)(2,1)S(1)} %collective-permute-done.18.refs_6_.refs_2_), channel_id=1, source_target_pairs={{0,56},{4,31},{8,48},{12,21},{1,57},{5,28},{9,49},{13,22},{2,58},{... | collective-permute-start | bytes 614408 | tf_op jit(solution)/shard_map/ppermute | solution.py:31
  68.8 2.4 %collective-permute-done.19.refs_7_.refs_3_ = bf16[32,3200]{1,0:T(8,128)(2,1)S(1)} collective-permute-done((bf16[32,3200]{1,0:T(8,128)(2,1)S(1)}, bf16[32,3200]{1,0:T(8,128)(2,1)S(1)}, u32[]{:S(2)}, u32[]{:S(2)}) %collective-permute-start.19) | collective-permute-done | bytes 204832 | tf_op jit(solution)/shard_map/ppermute | solution.py:31
  73.1 1.9 %collective-permute-start.25 = (f32[8,3200]{1,0:T(8,128)S(1)}, f32[8,3200]{1,0:T(8,128)S(1)}, u32[]{:S(2)}, u32[]{:S(2)}) collective-permute-start(f32[8,3200]{1,0:T(8,128)S(1)} %add.67), channel_id=1, source_target_pairs={{0,64},{64,0},{128,192},{192,128},{1,65},{65,1},{129,193},{193,129... | collective-permute-start | bytes 307208 | tf_op jit(solution)/shard_map/ppermute | solution.py:415
  75.1 2.1 %hidden_grads.1 = (bf16[256,1024]{1,0:T(8,128)(2,1)S(1)}, bf16[256,1024]{1,0:T(8,128)(2,1)S(1)}) custom-call(bf16[32,3200]{1,0:T(8,128)(2,1)S(1)} %get-tuple-element.72.refs_4_.refs_0_, bf16[32,3200]{1,0:T(8,128)(2,1)S(1)} %collective-permute-done.17.refs_5_.refs_1_, bf16[32,3200]{1,0:T(8,128)(2,1)S(1)} %collective-permute-done.18.refs_6_.refs_2_, ...), custom_call_target="tpu_custom_call" | custom-call | flops 1610612736 | bytes 6291456 | tf_op jit(solution)/shard_map/hidden_grads/pallas_call | solution.py:182
  78.4 3.4 %slot_grads.1 = (bf16[32,3072]{1,0:T(8,128)(2,1)S(1)}, bf16[32,3072]{1,0:T(8,128)(2,1)S(1)}, bf16[32,3072]{1,0:T(8,128)(2,1)S(1)}, bf16[32,3072]{1,0:T(8,128)(2,...) custom-call(bf16[256,1024]{1,0:T(8,128)(2,1)S(1)} %get-tuple-element, ...), custom_call_target="tpu_custom_call" | custom-call | flops 3221225472 | bytes 12582912 | tf_op jit(solution)/shard_map/slot_grads/pallas_call | solution.py:214
  82.1 3.3 %collective-permute-start.33 = (f32[8,3200]{1,0:T(8,128)S(1)}, f32[8,3200]{1,0:T(8,128)S(1)}, u32[]{:S(2)}, u32[]{:S(2)}) collective-permute-start(f32[8,3200]{1,0:T(8,128)S(1)} %add.68), channel_id=1, source_target_pairs={{0,128},{64,192},{128,0},{192,64},{1,129},{65,193},{129,1},{193,65... | collective-permute-start | bytes 307208 | tf_op jit(solution)/shard_map/ppermute | solution.py:417
  85.3 1.9 %collective-permute-start.28 = (bf16[32,3072]{1,0:T(8,128)(2,1)S(1)}, bf16[32,3072]{1,0:T(8,128)(2,1)S(1)}, u32[]{:S(2)}, u32[]{:S(2)}) collective-permute-start(bf16[32,3072]{1,0:T(8,128)(2,1)S(1)} %get-tuple-element.86), channel_id=1, source_target_pairs={{0,8},{4,15},{8,0},{12,5},{1,9},{5,12},{9,1},{13,6},{2,10},{6,13},... | collective-permute-start | bytes 589832 | tf_op jit(solution)/shard_map/ppermute | solution.py:31
  87.3 2.6 %collective-permute-start.26 = (bf16[32,3072]{1,0:T(8,128)(2,1)S(1)}, bf16[32,3072]{1,0:T(8,128)(2,1)S(1)}, u32[]{:S(2)}, u32[]{:S(2)}) collective-permute-start(bf16[32,3072]{1,0:T(8,128)(2,1)S(1)} %get-tuple-element.83), channel_id=1, source_target_pairs={{0,48},{4,20},{8,56},{12,28},{1,49},{5,21},{9,57},{13,29},{2,50},{... | collective-permute-start | bytes 589832 | tf_op jit(solution)/shard_map/ppermute | solution.py:31
  89.9 2.1 %collective-permute-start.34 = (f32[8,3200]{1,0:T(8,128)S(1)}, f32[8,3200]{1,0:T(8,128)S(1)}, u32[]{:S(2)}, u32[]{:S(2)}) collective-permute-start(f32[8,3200]{1,0:T(8,128)S(1)} %add.77), channel_id=1, source_target_pairs={{0,8},{4,12},{8,0},{12,4},{1,9},{5,13},{9,1},{13,5},{2,10},{6,14},... | collective-permute-start | bytes 307208 | tf_op jit(solution)/shard_map/ppermute | solution.py:31
  92.1 2.0 %collective-permute-start.32 = (bf16[32,3072]{1,0:T(8,128)(2,1)S(1)}, bf16[32,3072]{1,0:T(8,128)(2,1)S(1)}, u32[]{:S(2)}, u32[]{:S(2)}) collective-permute-start(bf16[32,3072]{1,0:T(8,128)(2,1)S(1)} %add_convert_fusion.1), channel_id=1, source_target_pairs={{0,16},{4,52},{8,24},{12,60},{1,17},{5,53},{9,25},{13,61},{2,18},{... | collective-permute-start | bytes 589832 | tf_op jit(solution)/shard_map/ppermute | solution.py:31
  94.1 1.8 %collective-permute-done.26 = bf16[32,3072]{1,0:T(8,128)(2,1)S(1)} collective-permute-done((bf16[32,3072]{1,0:T(8,128)(2,1)S(1)}, bf16[32,3072]{1,0:T(8,128)(2,1)S(1)}, u32[]{:S(2)}, u32[]{:S(2)}) %collective-permute-start.26) | collective-permute-done | bytes 196640 | tf_op jit(solution)/shard_map/ppermute | solution.py:31
  96.0 2.0 %collective-permute-start.29 = (bf16[32,3072]{1,0:T(8,128)(2,1)S(1)}, bf16[32,3072]{1,0:T(8,128)(2,1)S(1)}, u32[]{:S(2)}, u32[]{:S(2)}) collective-permute-start(bf16[32,3072]{1,0:T(8,128)(2,1)S(1)} %add_convert_fusion.2), channel_id=1, source_target_pairs={{0,48},{4,20},{8,56},{12,28},{1,49},{5,21},{9,57},{13,29},{2,50},{... | collective-permute-start | bytes 589832 | tf_op jit(solution)/shard_map/ppermute | solution.py:31
  101.7 2.0 %collective-permute-done.27 = bf16[32,3072]{1,0:T(8,128)(2,1)S(1)} collective-permute-done((bf16[32,3072]{1,0:T(8,128)(2,1)S(1)}, bf16[32,3072]{1,0:T(8,128)(2,1)S(1)}, u32[]{:S(2)}, u32[]{:S(2)}) %collective-permute-start.27) | collective-permute-done | bytes 196640 | tf_op jit(solution)/shard_map/ppermute | solution.py:31
  (95 shorter events, 23.9 us)
Async XLA Ops:
  2.8 23.6 %collective-permute-start.7 = (bf16[3072,512]{1,0:T(8,128)(2,1)}, bf16[3072,512]{1,0:T(8,128)(2,1)S(1)}, u32[]{:S(2)}, u32[]{:S(2)}) collective-permute-start(bf16[3072,512]{1,0:T(8,128)(2,1)} %gate), channel_id=1, source_target_pairs={{0,4},{4,0},{8,12},{12,8},{1,5},{5,1},{9,13},{13,9},{2,6},{6,2},{1... | collective-permute-start | bytes 9437192 | tf_op jit(solution)/shard_map/ppermute | solution.py:31
  2.9 23.5 %collective-permute-start.8 = (bf16[3072,512]{1,0:T(8,128)(2,1)}, bf16[3072,512]{1,0:T(8,128)(2,1)S(1)}, u32[]{:S(2)}, u32[]{:S(2)}) collective-permute-start(bf16[3072,512]{1,0:T(8,128)(2,1)} %up.1), channel_id=1, source_target_pairs={{0,4},{4,0},{8,12},{12,8},{1,5},{5,1},{9,13},{13,9},{2,6},{6,2},{1... | collective-permute-start | bytes 9437192 | tf_op jit(solution)/shard_map/ppermute | solution.py:31
  3.4 9.4 %collective-permute-start = (bf16[32,3072]{1,0:T(8,128)(2,1)S(1)}, bf16[32,3072]{1,0:T(8,128)(2,1)S(1)}, u32[]{:S(2)}, u32[]{:S(2)}) collective-permute-start(bf16[32,3072]{1,0:T(8,128)(2,1)S(1)} %get-tuple-element.47.refs_0_.refs_4_), channel_id=1, source_target_pairs={{0,16},{4,52},{8,24},{12,60},{1,17},{5,53},{9,25},{13,61},{2,18},{... | collective-permute-start | bytes 589832 | tf_op jit(solution)/shard_map/ppermute | solution.py:31
  4.9 8.3 %collective-permute-start.1 = (bf16[32,3072]{1,0:T(8,128)(2,1)S(1)}, bf16[32,3072]{1,0:T(8,128)(2,1)S(1)}, u32[]{:S(2)}, u32[]{:S(2)}) collective-permute-start(bf16[32,3072]{1,0:T(8,128)(2,1)S(1)} %get-tuple-element.47.refs_0_.refs_4_), channel_id=1, source_target_pairs={{0,48},{4,20},{8,56},{12,28},{1,49},{5,21},{9,57},{13,29},{2,50},{... | collective-permute-start | bytes 589832 | tf_op jit(solution)/shard_map/ppermute | solution.py:31
  6.7 7.7 %collective-permute-start.3 = (bf16[32,3072]{1,0:T(8,128)(2,1)S(1)}, bf16[32,3072]{1,0:T(8,128)(2,1)S(1)}, u32[]{:S(2)}, u32[]{:S(2)}) collective-permute-start(bf16[32,3072]{1,0:T(8,128)(2,1)S(1)} %get-tuple-element.47.refs_0_.refs_4_), channel_id=1, source_target_pairs={{0,8},{4,15},{8,0},{12,5},{1,9},{5,12},{9,1},{13,6},{2,10},{6,13},... | collective-permute-start | bytes 589832 | tf_op jit(solution)/shard_map/ppermute | solution.py:31
  12.8 7.0 %collective-permute-start.2 = (bf16[32,3072]{1,0:T(8,128)(2,1)S(1)}, bf16[32,3072]{1,0:T(8,128)(2,1)S(1)}, u32[]{:S(2)}, u32[]{:S(2)}) collective-permute-start(bf16[32,3072]{1,0:T(8,128)(2,1)S(1)} %collective-permute-done.refs_1_), channel_id=1, source_target_pairs={{0,16},{4,52},{8,24},{12,60},{1,17},{5,53},{9,25},{13,61},{2,18},{... | collective-permute-start | bytes 589832 | tf_op jit(solution)/shard_map/ppermute | solution.py:31
  13.2 7.5 %collective-permute-start.4 = (bf16[32,3072]{1,0:T(8,128)(2,1)S(1)}, bf16[32,3072]{1,0:T(8,128)(2,1)S(1)}, u32[]{:S(2)}, u32[]{:S(2)}) collective-permute-start(bf16[32,3072]{1,0:T(8,128)(2,1)S(1)} %collective-permute-done.refs_1_), channel_id=1, source_target_pairs={{0,8},{4,15},{8,0},{12,5},{1,9},{5,12},{9,1},{13,6},{2,10},{6,13},... | collective-permute-start | bytes 589832 | tf_op jit(solution)/shard_map/ppermute | solution.py:31
  14.3 6.6 %collective-permute-start.5 = (bf16[32,3072]{1,0:T(8,128)(2,1)S(1)}, bf16[32,3072]{1,0:T(8,128)(2,1)S(1)}, u32[]{:S(2)}, u32[]{:S(2)}) collective-permute-start(bf16[32,3072]{1,0:T(8,128)(2,1)S(1)} %collective-permute-done.1.refs_2_), channel_id=1, source_target_pairs={{0,8},{4,15},{8,0},{12,5},{1,9},{5,12},{9,1},{13,6},{2,10},{6,13},... | collective-permute-start | bytes 589832 | tf_op jit(solution)/shard_map/ppermute | solution.py:31
  19.8 6.6 %collective-permute-start.6 = (bf16[32,3072]{1,0:T(8,128)(2,1)S(1)}, bf16[32,3072]{1,0:T(8,128)(2,1)S(1)}, u32[]{:S(2)}, u32[]{:S(2)}) collective-permute-start(bf16[32,3072]{1,0:T(8,128)(2,1)S(1)} %collective-permute-done.1.refs_2_), channel_id=1, source_target_pairs={{0,56},{4,31},{8,48},{12,21},{1,57},{5,28},{9,49},{13,22},{2,58},{... | collective-permute-start | bytes 589832 | tf_op jit(solution)/shard_map/ppermute | solution.py:31
  33.8 7.9 %collective-permute-start.10 = (bf16[32,3072]{1,0:T(8,128)(2,1)S(1)}, bf16[32,3072]{1,0:T(8,128)(2,1)S(1)}, u32[]{:S(2)}, u32[]{:S(2)}) collective-permute-start(bf16[32,3072]{1,0:T(8,128)(2,1)S(1)} %get-tuple-element.60), channel_id=1, source_target_pairs={{0,48},{4,20},{8,56},{12,28},{1,49},{5,21},{9,57},{13,29},{2,50},{... | collective-permute-start | bytes 589832 | tf_op jit(solution)/shard_map/ppermute | solution.py:31
  35.4 6.2 %collective-permute-start.12 = (bf16[32,3072]{1,0:T(8,128)(2,1)S(1)}, bf16[32,3072]{1,0:T(8,128)(2,1)S(1)}, u32[]{:S(2)}, u32[]{:S(2)}) collective-permute-start(bf16[32,3072]{1,0:T(8,128)(2,1)S(1)} %get-tuple-element.63), channel_id=1, source_target_pairs={{0,8},{4,15},{8,0},{12,5},{1,9},{5,12},{9,1},{13,6},{2,10},{6,13},... | collective-permute-start | bytes 589832 | tf_op jit(solution)/shard_map/ppermute | solution.py:31
  37.6 7.9 %collective-permute-start.15 = (bf16[32,3072]{1,0:T(8,128)(2,1)S(1)}, bf16[32,3072]{1,0:T(8,128)(2,1)S(1)}, u32[]{:S(2)}, u32[]{:S(2)}) collective-permute-start(bf16[32,3072]{1,0:T(8,128)(2,1)S(1)} %get-tuple-element.66), channel_id=1, source_target_pairs={{0,24},{4,63},{8,16},{12,53},{1,25},{5,60},{9,17},{13,54},{2,26},{... | collective-permute-start | bytes 589832 | tf_op jit(solution)/shard_map/ppermute | solution.py:31
  37.7 7.9 %collective-permute-start.14 = (bf16[32,3072]{1,0:T(8,128)(2,1)S(1)}, bf16[32,3072]{1,0:T(8,128)(2,1)S(1)}, u32[]{:S(2)}, u32[]{:S(2)}) collective-permute-start(bf16[32,3072]{1,0:T(8,128)(2,1)S(1)} %get-tuple-element.65), channel_id=1, source_target_pairs={{0,8},{4,15},{8,0},{12,5},{1,9},{5,12},{9,1},{13,6},{2,10},{6,13},... | collective-permute-start | bytes 589832 | tf_op jit(solution)/shard_map/ppermute | solution.py:31
  41.6 5.9 %collective-permute-start.11 = (bf16[32,3072]{1,0:T(8,128)(2,1)S(1)}, bf16[32,3072]{1,0:T(8,128)(2,1)S(1)}, u32[]{:S(2)}, u32[]{:S(2)}) collective-permute-start(bf16[32,3072]{1,0:T(8,128)(2,1)S(1)} %get-tuple-element.61), channel_id=1, source_target_pairs={{0,8},{4,15},{8,0},{12,5},{1,9},{5,12},{9,1},{13,6},{2,10},{6,13},... | collective-permute-start | bytes 589832 | tf_op jit(solution)/shard_map/ppermute | solution.py:31
  41.7 7.9 %collective-permute-start.13 = (bf16[32,3072]{1,0:T(8,128)(2,1)S(1)}, bf16[32,3072]{1,0:T(8,128)(2,1)S(1)}, u32[]{:S(2)}, u32[]{:S(2)}) collective-permute-start(bf16[32,3072]{1,0:T(8,128)(2,1)S(1)} %add_convert_fusion.4), channel_id=1, source_target_pairs={{0,48},{4,20},{8,56},{12,28},{1,49},{5,21},{9,57},{13,29},{2,50},{... | collective-permute-start | bytes 589832 | tf_op jit(solution)/shard_map/ppermute | solution.py:31
  45.6 7.0 %collective-permute-start.16 = (bf16[32,3072]{1,0:T(8,128)(2,1)S(1)}, bf16[32,3072]{1,0:T(8,128)(2,1)S(1)}, u32[]{:S(2)}, u32[]{:S(2)}) collective-permute-start(bf16[32,3072]{1,0:T(8,128)(2,1)S(1)} %add_convert_fusion.3), channel_id=1, source_target_pairs={{0,16},{4,52},{8,24},{12,60},{1,17},{5,53},{9,25},{13,61},{2,18},{... | collective-permute-start | bytes 589832 | tf_op jit(solution)/shard_map/ppermute | solution.py:31
  53.3 8.8 %collective-permute-start.17 = (bf16[32,3200]{1,0:T(8,128)(2,1)S(1)}, bf16[32,3200]{1,0:T(8,128)(2,1)S(1)}, u32[]{:S(2)}, u32[]{:S(2)}) collective-permute-start(bf16[32,3200]{1,0:T(8,128)(2,1)S(1)} %get-tuple-element.72.refs_4_.refs_0_), channel_id=1, source_target_pairs={{0,16},{4,52},{8,24},{12,60},{1,17},{5,53},{9,25},{13,61},{2,18},{... | collective-permute-start | bytes 614408 | tf_op jit(solution)/shard_map/ppermute | solution.py:31
  53.4 10.8 %collective-permute-start.18 = (bf16[32,3200]{1,0:T(8,128)(2,1)S(1)}, bf16[32,3200]{1,0:T(8,128)(2,1)S(1)}, u32[]{:S(2)}, u32[]{:S(2)}) collective-permute-start(bf16[32,3200]{1,0:T(8,128)(2,1)S(1)} %get-tuple-element.72.refs_4_.refs_0_), channel_id=1, source_target_pairs={{0,48},{4,20},{8,56},{12,28},{1,49},{5,21},{9,57},{13,29},{2,50},{... | collective-permute-start | bytes 614408 | tf_op jit(solution)/shard_map/ppermute | solution.py:31
  62.1 9.2 %collective-permute-start.19 = (bf16[32,3200]{1,0:T(8,128)(2,1)S(1)}, bf16[32,3200]{1,0:T(8,128)(2,1)S(1)}, u32[]{:S(2)}, u32[]{:S(2)}) collective-permute-start(bf16[32,3200]{1,0:T(8,128)(2,1)S(1)} %collective-permute-done.17.refs_5_.refs_1_), channel_id=1, source_target_pairs={{0,16},{4,52},{8,24},{12,60},{1,17},{5,53},{9,25},{13,61},{2,18},{... | collective-permute-start | bytes 614408 | tf_op jit(solution)/shard_map/ppermute | solution.py:31
  62.1 12.9 %collective-permute-start.20 = (bf16[32,3200]{1,0:T(8,128)(2,1)S(1)}, bf16[32,3200]{1,0:T(8,128)(2,1)S(1)}, u32[]{:S(2)}, u32[]{:S(2)}) collective-permute-start(bf16[32,3200]{1,0:T(8,128)(2,1)S(1)} %get-tuple-element.72.refs_4_.refs_0_), channel_id=1, source_target_pairs={{0,8},{4,15},{8,0},{12,5},{1,9},{5,12},{9,1},{13,6},{2,10},{6,13},... | collective-permute-start | bytes 614408 | tf_op jit(solution)/shard_map/ppermute | solution.py:31
  64.1 11.0 %collective-permute-start.21 = (bf16[32,3200]{1,0:T(8,128)(2,1)S(1)}, bf16[32,3200]{1,0:T(8,128)(2,1)S(1)}, u32[]{:S(2)}, u32[]{:S(2)}) collective-permute-start(bf16[32,3200]{1,0:T(8,128)(2,1)S(1)} %collective-permute-done.17.refs_5_.refs_1_), channel_id=1, source_target_pairs={{0,8},{4,15},{8,0},{12,5},{1,9},{5,12},{9,1},{13,6},{2,10},{6,13},... | collective-permute-start | bytes 614408 | tf_op jit(solution)/shard_map/ppermute | solution.py:31
  64.1 10.9 %collective-permute-start.22 = (bf16[32,3200]{1,0:T(8,128)(2,1)S(1)}, bf16[32,3200]{1,0:T(8,128)(2,1)S(1)}, u32[]{:S(2)}, u32[]{:S(2)}) collective-permute-start(bf16[32,3200]{1,0:T(8,128)(2,1)S(1)} %collective-permute-done.18.refs_6_.refs_2_), channel_id=1, source_target_pairs={{0,8},{4,15},{8,0},{12,5},{1,9},{5,12},{9,1},{13,6},{2,10},{6,13},... | collective-permute-start | bytes 614408 | tf_op jit(solution)/shard_map/ppermute | solution.py:31
  66.1 8.9 %collective-permute-start.23 = (bf16[32,3200]{1,0:T(8,128)(2,1)S(1)}, bf16[32,3200]{1,0:T(8,128)(2,1)S(1)}, u32[]{:S(2)}, u32[]{:S(2)}) collective-permute-start(bf16[32,3200]{1,0:T(8,128)(2,1)S(1)} %collective-permute-done.18.refs_6_.refs_2_), channel_id=1, source_target_pairs={{0,56},{4,31},{8,48},{12,21},{1,57},{5,28},{9,49},{13,22},{2,58},{... | collective-permute-start | bytes 614408 | tf_op jit(solution)/shard_map/ppermute | solution.py:31
  81.9 10.1 %collective-permute-start.31 = (bf16[32,3072]{1,0:T(8,128)(2,1)S(1)}, bf16[32,3072]{1,0:T(8,128)(2,1)S(1)}, u32[]{:S(2)}, u32[]{:S(2)}) collective-permute-start(bf16[32,3072]{1,0:T(8,128)(2,1)S(1)} %get-tuple-element.89), channel_id=1, source_target_pairs={{0,24},{4,63},{8,16},{12,53},{1,25},{5,60},{9,17},{13,54},{2,26},{... | collective-permute-start | bytes 589832 | tf_op jit(solution)/shard_map/ppermute | solution.py:31
  82.0 10.0 %collective-permute-start.30 = (bf16[32,3072]{1,0:T(8,128)(2,1)S(1)}, bf16[32,3072]{1,0:T(8,128)(2,1)S(1)}, u32[]{:S(2)}, u32[]{:S(2)}) collective-permute-start(bf16[32,3072]{1,0:T(8,128)(2,1)S(1)} %get-tuple-element.88), channel_id=1, source_target_pairs={{0,8},{4,15},{8,0},{12,5},{1,9},{5,12},{9,1},{13,6},{2,10},{6,13},... | collective-permute-start | bytes 589832 | tf_op jit(solution)/shard_map/ppermute | solution.py:31
  82.1 7.8 %collective-permute-start.33 = (f32[8,3200]{1,0:T(8,128)S(1)}, f32[8,3200]{1,0:T(8,128)S(1)}, u32[]{:S(2)}, u32[]{:S(2)}) collective-permute-start(f32[8,3200]{1,0:T(8,128)S(1)} %add.68), channel_id=1, source_target_pairs={{0,128},{64,192},{128,0},{192,64},{1,129},{65,193},{129,1},{193,65... | collective-permute-start | bytes 307208 | tf_op jit(solution)/shard_map/ppermute | solution.py:417
  85.3 8.7 %collective-permute-start.28 = (bf16[32,3072]{1,0:T(8,128)(2,1)S(1)}, bf16[32,3072]{1,0:T(8,128)(2,1)S(1)}, u32[]{:S(2)}, u32[]{:S(2)}) collective-permute-start(bf16[32,3072]{1,0:T(8,128)(2,1)S(1)} %get-tuple-element.86), channel_id=1, source_target_pairs={{0,8},{4,15},{8,0},{12,5},{1,9},{5,12},{9,1},{13,6},{2,10},{6,13},... | collective-permute-start | bytes 589832 | tf_op jit(solution)/shard_map/ppermute | solution.py:31
  87.3 8.6 %collective-permute-start.26 = (bf16[32,3072]{1,0:T(8,128)(2,1)S(1)}, bf16[32,3072]{1,0:T(8,128)(2,1)S(1)}, u32[]{:S(2)}, u32[]{:S(2)}) collective-permute-start(bf16[32,3072]{1,0:T(8,128)(2,1)S(1)} %get-tuple-element.83), channel_id=1, source_target_pairs={{0,48},{4,20},{8,56},{12,28},{1,49},{5,21},{9,57},{13,29},{2,50},{... | collective-permute-start | bytes 589832 | tf_op jit(solution)/shard_map/ppermute | solution.py:31
  89.9 9.0 %collective-permute-start.34 = (f32[8,3200]{1,0:T(8,128)S(1)}, f32[8,3200]{1,0:T(8,128)S(1)}, u32[]{:S(2)}, u32[]{:S(2)}) collective-permute-start(f32[8,3200]{1,0:T(8,128)S(1)} %add.77), channel_id=1, source_target_pairs={{0,8},{4,12},{8,0},{12,4},{1,9},{5,13},{9,1},{13,5},{2,10},{6,14},... | collective-permute-start | bytes 307208 | tf_op jit(solution)/shard_map/ppermute | solution.py:31
  92.1 8.1 %collective-permute-start.32 = (bf16[32,3072]{1,0:T(8,128)(2,1)S(1)}, bf16[32,3072]{1,0:T(8,128)(2,1)S(1)}, u32[]{:S(2)}, u32[]{:S(2)}) collective-permute-start(bf16[32,3072]{1,0:T(8,128)(2,1)S(1)} %add_convert_fusion.1), channel_id=1, source_target_pairs={{0,16},{4,52},{8,24},{12,60},{1,17},{5,53},{9,25},{13,61},{2,18},{... | collective-permute-start | bytes 589832 | tf_op jit(solution)/shard_map/ppermute | solution.py:31
  96.0 5.7 %collective-permute-start.29 = (bf16[32,3072]{1,0:T(8,128)(2,1)S(1)}, bf16[32,3072]{1,0:T(8,128)(2,1)S(1)}, u32[]{:S(2)}, u32[]{:S(2)}) collective-permute-start(bf16[32,3072]{1,0:T(8,128)(2,1)S(1)} %add_convert_fusion.2), channel_id=1, source_target_pairs={{0,48},{4,20},{8,56},{12,28},{1,49},{5,21},{9,57},{13,29},{2,50},{... | collective-permute-start | bytes 589832 | tf_op jit(solution)/shard_map/ppermute | solution.py:31
  98.0 5.7 %collective-permute-start.27 = (bf16[32,3072]{1,0:T(8,128)(2,1)S(1)}, bf16[32,3072]{1,0:T(8,128)(2,1)S(1)}, u32[]{:S(2)}, u32[]{:S(2)}) collective-permute-start(bf16[32,3072]{1,0:T(8,128)(2,1)S(1)} %get-tuple-element.84), channel_id=1, source_target_pairs={{0,8},{4,15},{8,0},{12,5},{1,9},{5,12},{9,1},{13,6},{2,10},{6,13},... | collective-permute-start | bytes 589832 | tf_op jit(solution)/shard_map/ppermute | solution.py:31
  (13 other events, 50.7 us)

commit v4 on v3

--- a/solution.py
+++ b/solution.py
@@ -67,11 +67,11 @@
     return lax.optimization_barrier((value, *others))[0]
 
 
-def gather(own, *others):
+def gather(own, early, *late):
     f1 = ahead(own)
     b1 = behind(own)
     z0 = across(own)
-    f1_late, b1_late = after(f1, *others), after(b1, *others)
+    f1_late, b1_late = after(f1, early, *late), after(b1, early)
     x2 = ahead(f1_late)
     zf1 = across(f1_late)
     zb1 = across(b1_late)
@@ -372,9 +372,9 @@
     placing, token_slots = place(routes.T, tokens)
 
     own_gate, own_up = load(after(gate_weight, token_slots), up_weight)
-    token_blocks = gather(token_slots, own_gate)
     gates = [own_gate, twin(after(gate_weight, token_slots))]
     ups = [own_up, twin(after(up_weight, token_slots))]
+    token_blocks = gather(token_slots, own_gate, gates[1], ups[1])
     downs = [down_weight, twin(after(down_weight, *token_blocks[1:]))]
     hidden, pre_gate, pre_up = hidden_units(token_blocks, gates, ups)
     terms = slot_terms(hidden, downs)

time: 107 us -> 104 us (0.972); the launches traced: 105 us -> 104 us
  waiting for transfers between devices: 35.4 us -> 31.2 us
  starting transfers between devices: 44.4 us -> 47.5 us
    ppermute x33, waiting for transfers between devices: 34.2 us -> 30 us  [move(): return lax.ppermute(value, GROUP, pairs)]
    ppermute x33, starting transfers between devices: 39.2 us -> 42.3 us  [move(): return lax.ppermute(value, GROUP, pairs)]
  transfers between devices with their start and end apart: 35 -> 35, of which waited for: 16 -> 17; matrix products, arithmetic and copies ran while one was open for 4% -> 4% of each run, Pallas kernels for 6% -> 6%
where the time goes in v4:
time: 104 us
  starting transfers between devices  47.5 us (46%)
  waiting for transfers between devices  31.2 us (30%)
  Pallas kernels  12.7 us (12%)
  local copies, waits for them, and re-layouts  6.49 us (6%)
  matrix products  3.19 us (3%)
  other arithmetic  1.77 us (2%)
    ppermute x33, starting transfers between devices, move(): return lax.ppermute(value, GROUP, pairs)  42.3 us
    ppermute x33, waiting for transfers between devices, move(): return lax.ppermute(value, GROUP, pairs)  30 us
    unnamed x20, local copies, waits for them, and re-layouts  5.9 us
    pallas_call x1, Pallas kernels, slot_grads(): pl.pallas_call(slot_grad_kernel, name='slot_grads', out_shape=[jax.ShapeD...  3.44 us
    pallas_call x1, Pallas kernels, hidden_units(): pl.pallas_call(hidden_kernel, name='hidden_units', out_shape=[jax.ShapeDt...  3.42 us
    ppermute x1, starting transfers between devices, local(): lax.ppermute(summed, 'expert', [(i, i ^ 2) for i in range(4)])  3.27 us
    pallas_call x1, Pallas kernels, hidden_grads(): pl.pallas_call(hidden_grad_kernel, name='hidden_grads', out_shape=[jax.Sh...  2.11 us
  transfers between devices with their start and end apart: 35, of which 17 were waited for; matrix products, arithmetic and copies ran while one was open for 4% of the time, Pallas kernels for 6%

profile of v4, /device:TPU:64, one launch (start us, length us, event | category | flops | bytes accessed | tf_op | source)
XLA Modules:
  0.0 103.8 jit_solution(9986216720593481205)
XLA Ops:
  3.4 2.8 %collective-permute-start.1 = (bf16[32,3072]{1,0:T(8,128)(2,1)S(1)}, bf16[32,3072]{1,0:T(8,128)(2,1)S(1)}, u32[]{:S(2)}, u32[]{:S(2)}) collective-permute-start(bf16[32,3072]{1,0:T(8,128)(2,1)S(1)} %get-tuple-element.47.refs_0_.refs_4_), channel_id=1, source_target_pairs={{0,48},{4,20},{8,56},{12,28},{1,49},{5,21},{9,57},{13,29},{2,50},{... | collective-permute-start | bytes 589832 | tf_op jit(solution)/shard_map/ppermute | solution.py:31
  6.2 1.9 %collective-permute-start.5 = (bf16[32,3072]{1,0:T(8,128)(2,1)S(1)}, bf16[32,3072]{1,0:T(8,128)(2,1)S(1)}, u32[]{:S(2)}, u32[]{:S(2)}) collective-permute-start(bf16[32,3072]{1,0:T(8,128)(2,1)S(1)} %get-tuple-element.47.refs_0_.refs_4_), channel_id=1, source_target_pairs={{0,8},{4,15},{8,0},{12,5},{1,9},{5,12},{9,1},{13,6},{2,10},{6,13},... | collective-permute-start | bytes 589832 | tf_op jit(solution)/shard_map/ppermute | solution.py:31
  8.1 1.9 %copy-done.3 = bf16[3072,512]{1,0:T(8,128)(2,1)S(1)} copy-done((bf16[3072,512]{1,0:T(8,128)(2,1)S(1)}, bf16[3072,512]{1,0:T(8,128)(2,1)}, u32[]{:S(2)}) %copy-start.3) | copy-done | bytes 3145752
  10.0 1.9 %copy-done.4 = bf16[3072,512]{1,0:T(8,128)(2,1)S(1)} copy-done((bf16[3072,512]{1,0:T(8,128)(2,1)S(1)}, bf16[3072,512]{1,0:T(8,128)(2,1)}, u32[]{:S(2)}) %copy-start.4) | copy-done | bytes 3145752
  13.1 4.1 %collective-permute-start.8 = (bf16[32,3072]{1,0:T(8,128)(2,1)S(1)}, bf16[32,3072]{1,0:T(8,128)(2,1)S(1)}, u32[]{:S(2)}, u32[]{:S(2)}) collective-permute-start(bf16[32,3072]{1,0:T(8,128)(2,1)S(1)} %collective-permute-done.1.refs_2_), channel_id=1, source_target_pairs={{0,56},{4,31},{8,48},{12,21},{1,57},{5,28},{9,49},{13,22},{2,58},{... | collective-permute-start | bytes 589832 | tf_op jit(solution)/shard_map/ppermute | solution.py:31
  18.1 2.3 %collective-permute-done.8.refs_7_ = bf16[32,3072]{1,0:T(8,128)(2,1)S(1)} collective-permute-done((bf16[32,3072]{1,0:T(8,128)(2,1)S(1)}, bf16[32,3072]{1,0:T(8,128)(2,1)S(1)}, u32[]{:S(2)}, u32[]{:S(2)}) %collective-permute-start.8) | collective-permute-done | bytes 196640 | tf_op jit(solution)/shard_map/ppermute | solution.py:31
  20.4 3.6 %collective-permute-done.4.refs_3_ = bf16[32,3072]{1,0:T(8,128)(2,1)S(1)} collective-permute-done((bf16[32,3072]{1,0:T(8,128)(2,1)S(1)}, bf16[32,3072]{1,0:T(8,128)(2,1)S(1)}, u32[]{:S(2)}, u32[]{:S(2)}) %collective-permute-start.4) | collective-permute-done | bytes 196640 | tf_op jit(solution)/shard_map/ppermute | solution.py:31
  24.1 3.4 %hidden_units.1 = (bf16[256,1024]{1,0:T(8,128)(2,1)S(1)}, f32[256,1024]{1,0:T(8,128)S(1)}, f32[256,1024]{1,0:T(8,128)S(1)}) custom-call(bf16[32,3072]{1,0:T(8,128)(2,1)S(1)} %get-tuple-element.47.refs_0_.refs_4_, bf16[32,3072]{1,0:T(8,128)(2,1)S(1)} %collective-permute-done.refs_1_, bf16[32,3072]{1,0:T(8,128)(2,1)S(1)} %collective-permute-done.1.refs_2_, ...), custom_call_target="tpu_custom_call" | custom-call | flops 3221225472 | bytes 12582912 | tf_op jit(solution)/shard_map/hidden_units/pallas_call | solution.py:125
  29.7 1.8 %slot_terms.1 = (bf16[32,3072]{1,0:T(8,128)(2,1)S(1)}, bf16[32,3072]{1,0:T(8,128)(2,1)S(1)}, bf16[32,3072]{1,0:T(8,128)(2,1)S(1)}, bf16[32,3072]{1,0:T(8,128)(2,...) custom-call(bf16[256,1024]{1,0:T(8,128)(2,1)S(1)} %get-tuple-element, ...), custom_call_target="tpu_custom_call" | custom-call | flops 1610612736 | bytes 6291456 | tf_op jit(solution)/shard_map/slot_terms/pallas_call | solution.py:153
  31.5 2.1 %collective-permute-start.10 = (bf16[32,3072]{1,0:T(8,128)(2,1)S(1)}, bf16[32,3072]{1,0:T(8,128)(2,1)S(1)}, u32[]{:S(2)}, u32[]{:S(2)}) collective-permute-start(bf16[32,3072]{1,0:T(8,128)(2,1)S(1)} %get-tuple-element.60), channel_id=1, source_target_pairs={{0,48},{4,20},{8,56},{12,28},{1,49},{5,21},{9,57},{13,29},{2,50},{... | collective-permute-start | bytes 589832 | tf_op jit(solution)/shard_map/ppermute | solution.py:31
  35.5 2.0 %collective-permute-start.14 = (bf16[32,3072]{1,0:T(8,128)(2,1)S(1)}, bf16[32,3072]{1,0:T(8,128)(2,1)S(1)}, u32[]{:S(2)}, u32[]{:S(2)}) collective-permute-start(bf16[32,3072]{1,0:T(8,128)(2,1)S(1)} %get-tuple-element.65), channel_id=1, source_target_pairs={{0,8},{4,15},{8,0},{12,5},{1,9},{5,12},{9,1},{13,6},{2,10},{6,13},... | collective-permute-start | bytes 589832 | tf_op jit(solution)/shard_map/ppermute | solution.py:31
  37.5 1.8 %collective-permute-done.10 = bf16[32,3072]{1,0:T(8,128)(2,1)S(1)} collective-permute-done((bf16[32,3072]{1,0:T(8,128)(2,1)S(1)}, bf16[32,3072]{1,0:T(8,128)(2,1)S(1)}, u32[]{:S(2)}, u32[]{:S(2)}) %collective-permute-start.10) | collective-permute-done | bytes 196640 | tf_op jit(solution)/shard_map/ppermute | solution.py:31
  39.7 3.0 %collective-permute-start.13 = (bf16[32,3072]{1,0:T(8,128)(2,1)S(1)}, bf16[32,3072]{1,0:T(8,128)(2,1)S(1)}, u32[]{:S(2)}, u32[]{:S(2)}) collective-permute-start(bf16[32,3072]{1,0:T(8,128)(2,1)S(1)} %add_convert_fusion.4), channel_id=1, source_target_pairs={{0,48},{4,20},{8,56},{12,28},{1,49},{5,21},{9,57},{13,29},{2,50},{... | collective-permute-start | bytes 589832 | tf_op jit(solution)/shard_map/ppermute | solution.py:31
  44.0 1.6 %collective-permute-done.11.refs_1_ = bf16[32,3072]{1,0:T(8,128)(2,1)S(1)} collective-permute-done((bf16[32,3072]{1,0:T(8,128)(2,1)S(1)}, bf16[32,3072]{1,0:T(8,128)(2,1)S(1)}, u32[]{:S(2)}, u32[]{:S(2)}) %collective-permute-start.11) | collective-permute-done | bytes 196640 | tf_op jit(solution)/shard_map/ppermute | solution.py:31
  45.6 2.3 %collective-permute-done.13.refs_2_ = bf16[32,3072]{1,0:T(8,128)(2,1)S(1)} collective-permute-done((bf16[32,3072]{1,0:T(8,128)(2,1)S(1)}, bf16[32,3072]{1,0:T(8,128)(2,1)S(1)}, u32[]{:S(2)}, u32[]{:S(2)}) %collective-permute-start.13) | collective-permute-done | bytes 196640 | tf_op jit(solution)/shard_map/ppermute | solution.py:31
  47.9 2.7 %collective-permute-done.16.refs_3_ = bf16[32,3072]{1,0:T(8,128)(2,1)S(1)} collective-permute-done((bf16[32,3072]{1,0:T(8,128)(2,1)S(1)}, bf16[32,3072]{1,0:T(8,128)(2,1)S(1)}, u32[]{:S(2)}, u32[]{:S(2)}) %collective-permute-start.16) | collective-permute-done | bytes 196640 | tf_op jit(solution)/shard_map/ppermute | solution.py:31
  51.3 3.2 %collective-permute-start.18 = (bf16[32,3200]{1,0:T(8,128)(2,1)S(1)}, bf16[32,3200]{1,0:T(8,128)(2,1)S(1)}, u32[]{:S(2)}, u32[]{:S(2)}) collective-permute-start(bf16[32,3200]{1,0:T(8,128)(2,1)S(1)} %get-tuple-element.72.refs_4_.refs_0_), channel_id=1, source_target_pairs={{0,48},{4,20},{8,56},{12,28},{1,49},{5,21},{9,57},{13,29},{2,50},{... | collective-permute-start | bytes 614408 | tf_op jit(solution)/shard_map/ppermute | solution.py:31
  55.8 4.6 %collective-permute-done.17.refs_5_.refs_1_ = bf16[32,3200]{1,0:T(8,128)(2,1)S(1)} collective-permute-done((bf16[32,3200]{1,0:T(8,128)(2,1)S(1)}, bf16[32,3200]{1,0:T(8,128)(2,1)S(1)}, u32[]{:S(2)}, u32[]{:S(2)}) %collective-permute-start.17) | collective-permute-done | bytes 204832 | tf_op jit(solution)/shard_map/ppermute | solution.py:31
  63.3 3.8 %collective-permute-start.23 = (bf16[32,3200]{1,0:T(8,128)(2,1)S(1)}, bf16[32,3200]{1,0:T(8,128)(2,1)S(1)}, u32[]{:S(2)}, u32[]{:S(2)}) collective-permute-start(bf16[32,3200]{1,0:T(8,128)(2,1)S(1)} %collective-permute-done.18.refs_6_.refs_2_), channel_id=1, source_target_pairs={{0,56},{4,31},{8,48},{12,21},{1,57},{5,28},{9,49},{13,22},{2,58},{... | collective-permute-start | bytes 614408 | tf_op jit(solution)/shard_map/ppermute | solution.py:31
  67.1 2.4 %collective-permute-done.19.refs_7_.refs_3_ = bf16[32,3200]{1,0:T(8,128)(2,1)S(1)} collective-permute-done((bf16[32,3200]{1,0:T(8,128)(2,1)S(1)}, bf16[32,3200]{1,0:T(8,128)(2,1)S(1)}, u32[]{:S(2)}, u32[]{:S(2)}) %collective-permute-start.19) | collective-permute-done | bytes 204832 | tf_op jit(solution)/shard_map/ppermute | solution.py:31
  71.4 1.9 %collective-permute-start.25 = (f32[8,3200]{1,0:T(8,128)S(1)}, f32[8,3200]{1,0:T(8,128)S(1)}, u32[]{:S(2)}, u32[]{:S(2)}) collective-permute-start(f32[8,3200]{1,0:T(8,128)S(1)} %add.67), channel_id=1, source_target_pairs={{0,64},{64,0},{128,192},{192,128},{1,65},{65,1},{129,193},{193,129... | collective-permute-start | bytes 307208 | tf_op jit(solution)/shard_map/ppermute | solution.py:415
  73.3 2.1 %hidden_grads.1 = (bf16[256,1024]{1,0:T(8,128)(2,1)S(1)}, bf16[256,1024]{1,0:T(8,128)(2,1)S(1)}) custom-call(bf16[32,3200]{1,0:T(8,128)(2,1)S(1)} %get-tuple-element.72.refs_4_.refs_0_, bf16[32,3200]{1,0:T(8,128)(2,1)S(1)} %collective-permute-done.17.refs_5_.refs_1_, bf16[32,3200]{1,0:T(8,128)(2,1)S(1)} %collective-permute-done.18.refs_6_.refs_2_, ...), custom_call_target="tpu_custom_call" | custom-call | flops 1610612736 | bytes 6291456 | tf_op jit(solution)/shard_map/hidden_grads/pallas_call | solution.py:182
  76.7 3.4 %slot_grads.1 = (bf16[32,3072]{1,0:T(8,128)(2,1)S(1)}, bf16[32,3072]{1,0:T(8,128)(2,1)S(1)}, bf16[32,3072]{1,0:T(8,128)(2,1)S(1)}, bf16[32,3072]{1,0:T(8,128)(2,...) custom-call(bf16[256,1024]{1,0:T(8,128)(2,1)S(1)} %get-tuple-element, ...), custom_call_target="tpu_custom_call" | custom-call | flops 3221225472 | bytes 12582912 | tf_op jit(solution)/shard_map/slot_grads/pallas_call | solution.py:214
  80.3 3.3 %collective-permute-start.33 = (f32[8,3200]{1,0:T(8,128)S(1)}, f32[8,3200]{1,0:T(8,128)S(1)}, u32[]{:S(2)}, u32[]{:S(2)}) collective-permute-start(f32[8,3200]{1,0:T(8,128)S(1)} %add.68), channel_id=1, source_target_pairs={{0,128},{64,192},{128,0},{192,64},{1,129},{65,193},{129,1},{193,65... | collective-permute-start | bytes 307208 | tf_op jit(solution)/shard_map/ppermute | solution.py:417
  83.6 1.9 %collective-permute-start.28 = (bf16[32,3072]{1,0:T(8,128)(2,1)S(1)}, bf16[32,3072]{1,0:T(8,128)(2,1)S(1)}, u32[]{:S(2)}, u32[]{:S(2)}) collective-permute-start(bf16[32,3072]{1,0:T(8,128)(2,1)S(1)} %get-tuple-element.86), channel_id=1, source_target_pairs={{0,8},{4,15},{8,0},{12,5},{1,9},{5,12},{9,1},{13,6},{2,10},{6,13},... | collective-permute-start | bytes 589832 | tf_op jit(solution)/shard_map/ppermute | solution.py:31
  85.5 2.6 %collective-permute-start.26 = (bf16[32,3072]{1,0:T(8,128)(2,1)S(1)}, bf16[32,3072]{1,0:T(8,128)(2,1)S(1)}, u32[]{:S(2)}, u32[]{:S(2)}) collective-permute-start(bf16[32,3072]{1,0:T(8,128)(2,1)S(1)} %get-tuple-element.83), channel_id=1, source_target_pairs={{0,48},{4,20},{8,56},{12,28},{1,49},{5,21},{9,57},{13,29},{2,50},{... | collective-permute-start | bytes 589832 | tf_op jit(solution)/shard_map/ppermute | solution.py:31
  88.1 2.1 %collective-permute-start.34 = (f32[8,3200]{1,0:T(8,128)S(1)}, f32[8,3200]{1,0:T(8,128)S(1)}, u32[]{:S(2)}, u32[]{:S(2)}) collective-permute-start(f32[8,3200]{1,0:T(8,128)S(1)} %add.77), channel_id=1, source_target_pairs={{0,8},{4,12},{8,0},{12,4},{1,9},{5,13},{9,1},{13,5},{2,10},{6,14},... | collective-permute-start | bytes 307208 | tf_op jit(solution)/shard_map/ppermute | solution.py:31
  91.3 1.7 %collective-permute-done.26 = bf16[32,3072]{1,0:T(8,128)(2,1)S(1)} collective-permute-done((bf16[32,3072]{1,0:T(8,128)(2,1)S(1)}, bf16[32,3072]{1,0:T(8,128)(2,1)S(1)}, u32[]{:S(2)}, u32[]{:S(2)}) %collective-permute-start.26) | collective-permute-done | bytes 196640 | tf_op jit(solution)/shard_map/ppermute | solution.py:31
  93.0 3.8 %collective-permute-start.29 = (bf16[32,3072]{1,0:T(8,128)(2,1)S(1)}, bf16[32,3072]{1,0:T(8,128)(2,1)S(1)}, u32[]{:S(2)}, u32[]{:S(2)}) collective-permute-start(bf16[32,3072]{1,0:T(8,128)(2,1)S(1)} %add_convert_fusion.2), channel_id=1, source_target_pairs={{0,48},{4,20},{8,56},{12,28},{1,49},{5,21},{9,57},{13,29},{2,50},{... | collective-permute-start | bytes 589832 | tf_op jit(solution)/shard_map/ppermute | solution.py:31
  98.4 1.5 %collective-permute-done.29 = bf16[32,3072]{1,0:T(8,128)(2,1)S(1)} collective-permute-done((bf16[32,3072]{1,0:T(8,128)(2,1)S(1)}, bf16[32,3072]{1,0:T(8,128)(2,1)S(1)}, u32[]{:S(2)}, u32[]{:S(2)}) %collective-permute-start.29) | collective-permute-done | bytes 196640 | tf_op jit(solution)/shard_map/ppermute | solution.py:31
  100.0 2.5 %collective-permute-done.27 = bf16[32,3072]{1,0:T(8,128)(2,1)S(1)} collective-permute-done((bf16[32,3072]{1,0:T(8,128)(2,1)S(1)}, bf16[32,3072]{1,0:T(8,128)(2,1)S(1)}, u32[]{:S(2)}, u32[]{:S(2)}) %collective-permute-start.27) | collective-permute-done | bytes 196640 | tf_op jit(solution)/shard_map/ppermute | solution.py:31
  102.5 1.3 %fusion.1 = bf16[128,3072]{1,0:T(8,128)(2,1)} fusion(bf16[32,128]{1,0:T(8,128)(2,1)S(1)} %get-tuple-element.98, bf16[128,3072]{1,0:T(8,128)(2,1)S(1)} %copy-done.8, bf16[128,3072]{1,0:T(8,128)(2,1)S(1)} %copy-done.2, pred[128]{0:T(512)(128)(4,1)S(1)} %bitcast.47, f32[32,3072]{1,0:T(8,128)S(1)} %get-tuple-element.71, ...), kind=kOutput, calls=%fused_computation.3 | convolution fusion | flops 28409856 | bytes 3547264 | tf_op jit(solution)/shard_map/dot_general | solution.py:424
  (95 shorter events, 21.6 us)
Async XLA Ops:
  2.8 14.3 %collective-permute-start.2 = (bf16[3072,512]{1,0:T(8,128)(2,1)}, bf16[3072,512]{1,0:T(8,128)(2,1)S(1)}, u32[]{:S(2)}, u32[]{:S(2)}) collective-permute-start(bf16[3072,512]{1,0:T(8,128)(2,1)} %gate), channel_id=1, source_target_pairs={{0,4},{4,0},{8,12},{12,8},{1,5},{5,1},{9,13},{13,9},{2,6},{6,2},{1... | collective-permute-start | bytes 9437192 | tf_op jit(solution)/shard_map/ppermute | solution.py:31
  2.9 14.2 %collective-permute-start.3 = (bf16[3072,512]{1,0:T(8,128)(2,1)}, bf16[3072,512]{1,0:T(8,128)(2,1)S(1)}, u32[]{:S(2)}, u32[]{:S(2)}) collective-permute-start(bf16[3072,512]{1,0:T(8,128)(2,1)} %up.1), channel_id=1, source_target_pairs={{0,4},{4,0},{8,12},{12,8},{1,5},{5,1},{9,13},{13,9},{2,6},{6,2},{1... | collective-permute-start | bytes 9437192 | tf_op jit(solution)/shard_map/ppermute | solution.py:31
  3.4 8.9 %collective-permute-start.1 = (bf16[32,3072]{1,0:T(8,128)(2,1)S(1)}, bf16[32,3072]{1,0:T(8,128)(2,1)S(1)}, u32[]{:S(2)}, u32[]{:S(2)}) collective-permute-start(bf16[32,3072]{1,0:T(8,128)(2,1)S(1)} %get-tuple-element.47.refs_0_.refs_4_), channel_id=1, source_target_pairs={{0,48},{4,20},{8,56},{12,28},{1,49},{5,21},{9,57},{13,29},{2,50},{... | collective-permute-start | bytes 589832 | tf_op jit(solution)/shard_map/ppermute | solution.py:31
  6.2 6.9 %collective-permute-start = (bf16[32,3072]{1,0:T(8,128)(2,1)S(1)}, bf16[32,3072]{1,0:T(8,128)(2,1)S(1)}, u32[]{:S(2)}, u32[]{:S(2)}) collective-permute-start(bf16[32,3072]{1,0:T(8,128)(2,1)S(1)} %get-tuple-element.47.refs_0_.refs_4_), channel_id=1, source_target_pairs={{0,16},{4,52},{8,24},{12,60},{1,17},{5,53},{9,25},{13,61},{2,18},{... | collective-permute-start | bytes 589832 | tf_op jit(solution)/shard_map/ppermute | solution.py:31
  6.2 11.8 %collective-permute-start.5 = (bf16[32,3072]{1,0:T(8,128)(2,1)S(1)}, bf16[32,3072]{1,0:T(8,128)(2,1)S(1)}, u32[]{:S(2)}, u32[]{:S(2)}) collective-permute-start(bf16[32,3072]{1,0:T(8,128)(2,1)S(1)} %get-tuple-element.47.refs_0_.refs_4_), channel_id=1, source_target_pairs={{0,8},{4,15},{8,0},{12,5},{1,9},{5,12},{9,1},{13,6},{2,10},{6,13},... | collective-permute-start | bytes 589832 | tf_op jit(solution)/shard_map/ppermute | solution.py:31
  12.3 5.8 %collective-permute-start.7 = (bf16[32,3072]{1,0:T(8,128)(2,1)S(1)}, bf16[32,3072]{1,0:T(8,128)(2,1)S(1)}, u32[]{:S(2)}, u32[]{:S(2)}) collective-permute-start(bf16[32,3072]{1,0:T(8,128)(2,1)S(1)} %collective-permute-done.1.refs_2_), channel_id=1, source_target_pairs={{0,8},{4,15},{8,0},{12,5},{1,9},{5,12},{9,1},{13,6},{2,10},{6,13},... | collective-permute-start | bytes 589832 | tf_op jit(solution)/shard_map/ppermute | solution.py:31
  13.1 7.3 %collective-permute-start.8 = (bf16[32,3072]{1,0:T(8,128)(2,1)S(1)}, bf16[32,3072]{1,0:T(8,128)(2,1)S(1)}, u32[]{:S(2)}, u32[]{:S(2)}) collective-permute-start(bf16[32,3072]{1,0:T(8,128)(2,1)S(1)} %collective-permute-done.1.refs_2_), channel_id=1, source_target_pairs={{0,56},{4,31},{8,48},{12,21},{1,57},{5,28},{9,49},{13,22},{2,58},{... | collective-permute-start | bytes 589832 | tf_op jit(solution)/shard_map/ppermute | solution.py:31
  17.1 6.9 %collective-permute-start.4 = (bf16[32,3072]{1,0:T(8,128)(2,1)S(1)}, bf16[32,3072]{1,0:T(8,128)(2,1)S(1)}, u32[]{:S(2)}, u32[]{:S(2)}) collective-permute-start(bf16[32,3072]{1,0:T(8,128)(2,1)S(1)} %collective-permute-done.refs_1_), channel_id=1, source_target_pairs={{0,16},{4,52},{8,24},{12,60},{1,17},{5,53},{9,25},{13,61},{2,18},{... | collective-permute-start | bytes 589832 | tf_op jit(solution)/shard_map/ppermute | solution.py:31
  17.1 6.9 %collective-permute-start.6 = (bf16[32,3072]{1,0:T(8,128)(2,1)S(1)}, bf16[32,3072]{1,0:T(8,128)(2,1)S(1)}, u32[]{:S(2)}, u32[]{:S(2)}) collective-permute-start(bf16[32,3072]{1,0:T(8,128)(2,1)S(1)} %collective-permute-done.refs_1_), channel_id=1, source_target_pairs={{0,8},{4,15},{8,0},{12,5},{1,9},{5,12},{9,1},{13,6},{2,10},{6,13},... | collective-permute-start | bytes 589832 | tf_op jit(solution)/shard_map/ppermute | solution.py:31
  31.5 7.9 %collective-permute-start.10 = (bf16[32,3072]{1,0:T(8,128)(2,1)S(1)}, bf16[32,3072]{1,0:T(8,128)(2,1)S(1)}, u32[]{:S(2)}, u32[]{:S(2)}) collective-permute-start(bf16[32,3072]{1,0:T(8,128)(2,1)S(1)} %get-tuple-element.60), channel_id=1, source_target_pairs={{0,48},{4,20},{8,56},{12,28},{1,49},{5,21},{9,57},{13,29},{2,50},{... | collective-permute-start | bytes 589832 | tf_op jit(solution)/shard_map/ppermute | solution.py:31
  33.6 6.0 %collective-permute-start.12 = (bf16[32,3072]{1,0:T(8,128)(2,1)S(1)}, bf16[32,3072]{1,0:T(8,128)(2,1)S(1)}, u32[]{:S(2)}, u32[]{:S(2)}) collective-permute-start(bf16[32,3072]{1,0:T(8,128)(2,1)S(1)} %get-tuple-element.63), channel_id=1, source_target_pairs={{0,8},{4,15},{8,0},{12,5},{1,9},{5,12},{9,1},{13,6},{2,10},{6,13},... | collective-permute-start | bytes 589832 | tf_op jit(solution)/shard_map/ppermute | solution.py:31
  34.6 8.1 %collective-permute-start.15 = (bf16[32,3072]{1,0:T(8,128)(2,1)S(1)}, bf16[32,3072]{1,0:T(8,128)(2,1)S(1)}, u32[]{:S(2)}, u32[]{:S(2)}) collective-permute-start(bf16[32,3072]{1,0:T(8,128)(2,1)S(1)} %get-tuple-element.66), channel_id=1, source_target_pairs={{0,24},{4,63},{8,16},{12,53},{1,25},{5,60},{9,17},{13,54},{2,26},{... | collective-permute-start | bytes 589832 | tf_op jit(solution)/shard_map/ppermute | solution.py:31
  35.5 8.0 %collective-permute-start.14 = (bf16[32,3072]{1,0:T(8,128)(2,1)S(1)}, bf16[32,3072]{1,0:T(8,128)(2,1)S(1)}, u32[]{:S(2)}, u32[]{:S(2)}) collective-permute-start(bf16[32,3072]{1,0:T(8,128)(2,1)S(1)} %get-tuple-element.65), channel_id=1, source_target_pairs={{0,8},{4,15},{8,0},{12,5},{1,9},{5,12},{9,1},{13,6},{2,10},{6,13},... | collective-permute-start | bytes 589832 | tf_op jit(solution)/shard_map/ppermute | solution.py:31
  39.3 6.3 %collective-permute-start.11 = (bf16[32,3072]{1,0:T(8,128)(2,1)S(1)}, bf16[32,3072]{1,0:T(8,128)(2,1)S(1)}, u32[]{:S(2)}, u32[]{:S(2)}) collective-permute-start(bf16[32,3072]{1,0:T(8,128)(2,1)S(1)} %get-tuple-element.61), channel_id=1, source_target_pairs={{0,8},{4,15},{8,0},{12,5},{1,9},{5,12},{9,1},{13,6},{2,10},{6,13},... | collective-permute-start | bytes 589832 | tf_op jit(solution)/shard_map/ppermute | solution.py:31
  39.7 8.2 %collective-permute-start.13 = (bf16[32,3072]{1,0:T(8,128)(2,1)S(1)}, bf16[32,3072]{1,0:T(8,128)(2,1)S(1)}, u32[]{:S(2)}, u32[]{:S(2)}) collective-permute-start(bf16[32,3072]{1,0:T(8,128)(2,1)S(1)} %add_convert_fusion.4), channel_id=1, source_target_pairs={{0,48},{4,20},{8,56},{12,28},{1,49},{5,21},{9,57},{13,29},{2,50},{... | collective-permute-start | bytes 589832 | tf_op jit(solution)/shard_map/ppermute | solution.py:31
  43.6 7.0 %collective-permute-start.16 = (bf16[32,3072]{1,0:T(8,128)(2,1)S(1)}, bf16[32,3072]{1,0:T(8,128)(2,1)S(1)}, u32[]{:S(2)}, u32[]{:S(2)}) collective-permute-start(bf16[32,3072]{1,0:T(8,128)(2,1)S(1)} %add_convert_fusion.3), channel_id=1, source_target_pairs={{0,16},{4,52},{8,24},{12,60},{1,17},{5,53},{9,25},{13,61},{2,18},{... | collective-permute-start | bytes 589832 | tf_op jit(solution)/shard_map/ppermute | solution.py:31
  51.2 9.1 %collective-permute-start.17 = (bf16[32,3200]{1,0:T(8,128)(2,1)S(1)}, bf16[32,3200]{1,0:T(8,128)(2,1)S(1)}, u32[]{:S(2)}, u32[]{:S(2)}) collective-permute-start(bf16[32,3200]{1,0:T(8,128)(2,1)S(1)} %get-tuple-element.72.refs_4_.refs_0_), channel_id=1, source_target_pairs={{0,16},{4,52},{8,24},{12,60},{1,17},{5,53},{9,25},{13,61},{2,18},{... | collective-permute-start | bytes 614408 | tf_op jit(solution)/shard_map/ppermute | solution.py:31
  51.3 11.1 %collective-permute-start.18 = (bf16[32,3200]{1,0:T(8,128)(2,1)S(1)}, bf16[32,3200]{1,0:T(8,128)(2,1)S(1)}, u32[]{:S(2)}, u32[]{:S(2)}) collective-permute-start(bf16[32,3200]{1,0:T(8,128)(2,1)S(1)} %get-tuple-element.72.refs_4_.refs_0_), channel_id=1, source_target_pairs={{0,48},{4,20},{8,56},{12,28},{1,49},{5,21},{9,57},{13,29},{2,50},{... | collective-permute-start | bytes 614408 | tf_op jit(solution)/shard_map/ppermute | solution.py:31
  60.4 9.2 %collective-permute-start.19 = (bf16[32,3200]{1,0:T(8,128)(2,1)S(1)}, bf16[32,3200]{1,0:T(8,128)(2,1)S(1)}, u32[]{:S(2)}, u32[]{:S(2)}) collective-permute-start(bf16[32,3200]{1,0:T(8,128)(2,1)S(1)} %collective-permute-done.17.refs_5_.refs_1_), channel_id=1, source_target_pairs={{0,16},{4,52},{8,24},{12,60},{1,17},{5,53},{9,25},{13,61},{2,18},{... | collective-permute-start | bytes 614408 | tf_op jit(solution)/shard_map/ppermute | solution.py:31
  60.4 12.9 %collective-permute-start.20 = (bf16[32,3200]{1,0:T(8,128)(2,1)S(1)}, bf16[32,3200]{1,0:T(8,128)(2,1)S(1)}, u32[]{:S(2)}, u32[]{:S(2)}) collective-permute-start(bf16[32,3200]{1,0:T(8,128)(2,1)S(1)} %get-tuple-element.72.refs_4_.refs_0_), channel_id=1, source_target_pairs={{0,8},{4,15},{8,0},{12,5},{1,9},{5,12},{9,1},{13,6},{2,10},{6,13},... | collective-permute-start | bytes 614408 | tf_op jit(solution)/shard_map/ppermute | solution.py:31
  61.3 12.0 %collective-permute-start.21 = (bf16[32,3200]{1,0:T(8,128)(2,1)S(1)}, bf16[32,3200]{1,0:T(8,128)(2,1)S(1)}, u32[]{:S(2)}, u32[]{:S(2)}) collective-permute-start(bf16[32,3200]{1,0:T(8,128)(2,1)S(1)} %collective-permute-done.17.refs_5_.refs_1_), channel_id=1, source_target_pairs={{0,8},{4,15},{8,0},{12,5},{1,9},{5,12},{9,1},{13,6},{2,10},{6,13},... | collective-permute-start | bytes 614408 | tf_op jit(solution)/shard_map/ppermute | solution.py:31
  62.4 10.9 %collective-permute-start.22 = (bf16[32,3200]{1,0:T(8,128)(2,1)S(1)}, bf16[32,3200]{1,0:T(8,128)(2,1)S(1)}, u32[]{:S(2)}, u32[]{:S(2)}) collective-permute-start(bf16[32,3200]{1,0:T(8,128)(2,1)S(1)} %collective-permute-done.18.refs_6_.refs_2_), channel_id=1, source_target_pairs={{0,8},{4,15},{8,0},{12,5},{1,9},{5,12},{9,1},{13,6},{2,10},{6,13},... | collective-permute-start | bytes 614408 | tf_op jit(solution)/shard_map/ppermute | solution.py:31
  63.3 10.0 %collective-permute-start.23 = (bf16[32,3200]{1,0:T(8,128)(2,1)S(1)}, bf16[32,3200]{1,0:T(8,128)(2,1)S(1)}, u32[]{:S(2)}, u32[]{:S(2)}) collective-permute-start(bf16[32,3200]{1,0:T(8,128)(2,1)S(1)} %collective-permute-done.18.refs_6_.refs_2_), channel_id=1, source_target_pairs={{0,56},{4,31},{8,48},{12,21},{1,57},{5,28},{9,49},{13,22},{2,58},{... | collective-permute-start | bytes 614408 | tf_op jit(solution)/shard_map/ppermute | solution.py:31
  80.1 10.1 %collective-permute-start.31 = (bf16[32,3072]{1,0:T(8,128)(2,1)S(1)}, bf16[32,3072]{1,0:T(8,128)(2,1)S(1)}, u32[]{:S(2)}, u32[]{:S(2)}) collective-permute-start(bf16[32,3072]{1,0:T(8,128)(2,1)S(1)} %get-tuple-element.89), channel_id=1, source_target_pairs={{0,24},{4,63},{8,16},{12,53},{1,25},{5,60},{9,17},{13,54},{2,26},{... | collective-permute-start | bytes 589832 | tf_op jit(solution)/shard_map/ppermute | solution.py:31
  80.2 10.0 %collective-permute-start.30 = (bf16[32,3072]{1,0:T(8,128)(2,1)S(1)}, bf16[32,3072]{1,0:T(8,128)(2,1)S(1)}, u32[]{:S(2)}, u32[]{:S(2)}) collective-permute-start(bf16[32,3072]{1,0:T(8,128)(2,1)S(1)} %get-tuple-element.88), channel_id=1, source_target_pairs={{0,8},{4,15},{8,0},{12,5},{1,9},{5,12},{9,1},{13,6},{2,10},{6,13},... | collective-permute-start | bytes 589832 | tf_op jit(solution)/shard_map/ppermute | solution.py:31
  80.3 7.8 %collective-permute-start.33 = (f32[8,3200]{1,0:T(8,128)S(1)}, f32[8,3200]{1,0:T(8,128)S(1)}, u32[]{:S(2)}, u32[]{:S(2)}) collective-permute-start(f32[8,3200]{1,0:T(8,128)S(1)} %add.68), channel_id=1, source_target_pairs={{0,128},{64,192},{128,0},{192,64},{1,129},{65,193},{129,1},{193,65... | collective-permute-start | bytes 307208 | tf_op jit(solution)/shard_map/ppermute | solution.py:417
  83.6 7.7 %collective-permute-start.28 = (bf16[32,3072]{1,0:T(8,128)(2,1)S(1)}, bf16[32,3072]{1,0:T(8,128)(2,1)S(1)}, u32[]{:S(2)}, u32[]{:S(2)}) collective-permute-start(bf16[32,3072]{1,0:T(8,128)(2,1)S(1)} %get-tuple-element.86), channel_id=1, source_target_pairs={{0,8},{4,15},{8,0},{12,5},{1,9},{5,12},{9,1},{13,6},{2,10},{6,13},... | collective-permute-start | bytes 589832 | tf_op jit(solution)/shard_map/ppermute | solution.py:31
  85.5 7.4 %collective-permute-start.26 = (bf16[32,3072]{1,0:T(8,128)(2,1)S(1)}, bf16[32,3072]{1,0:T(8,128)(2,1)S(1)}, u32[]{:S(2)}, u32[]{:S(2)}) collective-permute-start(bf16[32,3072]{1,0:T(8,128)(2,1)S(1)} %get-tuple-element.83), channel_id=1, source_target_pairs={{0,48},{4,20},{8,56},{12,28},{1,49},{5,21},{9,57},{13,29},{2,50},{... | collective-permute-start | bytes 589832 | tf_op jit(solution)/shard_map/ppermute | solution.py:31
  88.1 9.0 %collective-permute-start.34 = (f32[8,3200]{1,0:T(8,128)S(1)}, f32[8,3200]{1,0:T(8,128)S(1)}, u32[]{:S(2)}, u32[]{:S(2)}) collective-permute-start(f32[8,3200]{1,0:T(8,128)S(1)} %add.77), channel_id=1, source_target_pairs={{0,8},{4,12},{8,0},{12,4},{1,9},{5,13},{9,1},{13,5},{2,10},{6,14},... | collective-permute-start | bytes 307208 | tf_op jit(solution)/shard_map/ppermute | solution.py:31
  90.3 8.1 %collective-permute-start.32 = (bf16[32,3072]{1,0:T(8,128)(2,1)S(1)}, bf16[32,3072]{1,0:T(8,128)(2,1)S(1)}, u32[]{:S(2)}, u32[]{:S(2)}) collective-permute-start(bf16[32,3072]{1,0:T(8,128)(2,1)S(1)} %add_convert_fusion.1), channel_id=1, source_target_pairs={{0,16},{4,52},{8,24},{12,60},{1,17},{5,53},{9,25},{13,61},{2,18},{... | collective-permute-start | bytes 589832 | tf_op jit(solution)/shard_map/ppermute | solution.py:31
  93.0 7.0 %collective-permute-start.29 = (bf16[32,3072]{1,0:T(8,128)(2,1)S(1)}, bf16[32,3072]{1,0:T(8,128)(2,1)S(1)}, u32[]{:S(2)}, u32[]{:S(2)}) collective-permute-start(bf16[32,3072]{1,0:T(8,128)(2,1)S(1)} %add_convert_fusion.2), channel_id=1, source_target_pairs={{0,48},{4,20},{8,56},{12,28},{1,49},{5,21},{9,57},{13,29},{2,50},{... | collective-permute-start | bytes 589832 | tf_op jit(solution)/shard_map/ppermute | solution.py:31
  96.8 5.7 %collective-permute-start.27 = (bf16[32,3072]{1,0:T(8,128)(2,1)S(1)}, bf16[32,3072]{1,0:T(8,128)(2,1)S(1)}, u32[]{:S(2)}, u32[]{:S(2)}) collective-permute-start(bf16[32,3072]{1,0:T(8,128)(2,1)S(1)} %get-tuple-element.84), channel_id=1, source_target_pairs={{0,8},{4,15},{8,0},{12,5},{1,9},{5,12},{9,1},{13,6},{2,10},{6,13},... | collective-permute-start | bytes 589832 | tf_op jit(solution)/shard_map/ppermute | solution.py:31
  (13 other events, 48.3 us)

commit v5 on v4

--- a/solution.py
+++ b/solution.py
@@ -92,7 +92,7 @@
     got_z0 = across(after(z0, got_x2))
     got_f1 = behind(add(f1, got_x2, got_zf1))
     got_b1 = ahead(add(b1, got_zb1, got_zx2))
-    return [own, got_z0, got_f1, got_b1]
+    return [own, got_z0, got_f1, got_b1], got_x2
 
 
 def stack_rows(blocks, rows):
@@ -404,7 +404,7 @@
     sub = lax.broadcasted_iota(jnp.int32, (8, LANES), 0)
     base = jnp.where(sub == 0, jnp.sum(plain_loss[:, None] * lang_hot, axis=0)[None, :], jnp.sum(lang_hot, axis=0)[None, :])
 
-    combined, grad_slots, so_far = slots(scatter(terms), token_slots, teacher_slots, aux, slot_langs, base, router_weight.T)
+    combined, grad_slots, so_far = slots(scatter(terms)[0], token_slots, teacher_slots, aux, slot_langs, base, router_weight.T)
     placed = lax.dot_general(placing_half, combined, TN, preferred_element_type=f32)
     layer_out = jnp.where(chosen[:, None], placed.astype(bf16), tokens)
     grad_blocks = gather(grad_slots, layer_out)
@@ -414,12 +414,14 @@
     gate_grad, up_grad = hidden_grads(grad_blocks, downs, after(pre_gate, summed), pre_up)
     summed = summed + lax.ppermute(summed, "expert", [(i, i ^ 1) for i in range(4)])
     back_terms = slot_grads(after(gate_grad, summed), up_grad, gates, ups)
+    back_parts, first_part = scatter(list(back_terms))
+    summed = after(summed, first_part)
     summed = summed + lax.ppermute(summed, "expert", [(i, i ^ 2) for i in range(4)])
     summed = summed + pair(summed)
     grad_router = summed[:, :width].T / all_tokens
     lang_loss = (summed[0, width:] / jnp.maximum(summed[1, width:], 1.0))[SHIFT : SHIFT + LANGS]
 
-    own_back = sum(t.astype(f32) for t in scatter(list(back_terms)))
+    own_back = sum(t.astype(f32) for t in back_parts)
     slot_grad = (so_far + own_back).astype(bf16)
     placed_grad = lax.dot_general(placing_half, slot_grad, TN, preferred_element_type=f32)
     grad_tokens = jnp.where(chosen[:, None], placed_grad.astype(bf16), plain_grad)

time: 104 us -> 106 us (1.019)
  the two profiles are of different devices: /device:TPU:64 before, /device:TPU:16 now
where the time goes in v5:
time: 106 us
  waiting for transfers between devices  43.7 us (41%)
  starting transfers between devices  37.2 us (35%)
  Pallas kernels  12.8 us (12%)
  local copies, waits for them, and re-layouts  6.48 us (6%)
  matrix products  3.2 us (3%)
  other arithmetic  1.77 us (2%)
    ppermute x33, waiting for transfers between devices, move(): return lax.ppermute(value, GROUP, pairs)  37.5 us
    ppermute x33, starting transfers between devices, move(): return lax.ppermute(value, GROUP, pairs)  35.3 us
    ppermute x1, waiting for transfers between devices, local(): lax.ppermute(summed, 'expert', [(i, i ^ 2) for i in range(4)])  6.27 us
    unnamed x20, local copies, waits for them, and re-layouts  5.9 us
    pallas_call x1, Pallas kernels, slot_grads(): pl.pallas_call(slot_grad_kernel, name='slot_grads', out_shape=[jax.ShapeD...  3.44 us
    pallas_call x1, Pallas kernels, hidden_units(): pl.pallas_call(hidden_kernel, name='hidden_units', out_shape=[jax.ShapeDt...  3.42 us
  transfers between devices with their start and end apart: 35, of which 22 were waited for; matrix products, arithmetic and copies ran while one was open for 4% of the time, Pallas kernels for 6%

profile of v5, /device:TPU:16, one launch (start us, length us, event | category | flops | bytes accessed | tf_op | source)
XLA Modules:
  0.0 106.2 jit_solution(5148593587970419559)
XLA Ops:
  3.4 2.8 %collective-permute-start.1 = (bf16[32,3072]{1,0:T(8,128)(2,1)S(1)}, bf16[32,3072]{1,0:T(8,128)(2,1)S(1)}, u32[]{:S(2)}, u32[]{:S(2)}) collective-permute-start(bf16[32,3072]{1,0:T(8,128)(2,1)S(1)} %get-tuple-element.48.refs_0_.refs_4_), channel_id=1, source_target_pairs={{0,48},{4,20},{8,56},{12,28},{1,49},{5,21},{9,57},{13,29},{2,50},{... | collective-permute-start | bytes 589832 | tf_op jit(solution)/shard_map/ppermute | solution.py:31
  6.2 1.9 %collective-permute-start.5 = (bf16[32,3072]{1,0:T(8,128)(2,1)S(1)}, bf16[32,3072]{1,0:T(8,128)(2,1)S(1)}, u32[]{:S(2)}, u32[]{:S(2)}) collective-permute-start(bf16[32,3072]{1,0:T(8,128)(2,1)S(1)} %get-tuple-element.48.refs_0_.refs_4_), channel_id=1, source_target_pairs={{0,8},{4,15},{8,0},{12,5},{1,9},{5,12},{9,1},{13,6},{2,10},{6,13},... | collective-permute-start | bytes 589832 | tf_op jit(solution)/shard_map/ppermute | solution.py:31
  8.1 1.9 %copy-done.3 = bf16[3072,512]{1,0:T(8,128)(2,1)S(1)} copy-done((bf16[3072,512]{1,0:T(8,128)(2,1)S(1)}, bf16[3072,512]{1,0:T(8,128)(2,1)}, u32[]{:S(2)}) %copy-start.3) | copy-done | bytes 3145752
  10.0 1.9 %copy-done.4 = bf16[3072,512]{1,0:T(8,128)(2,1)S(1)} copy-done((bf16[3072,512]{1,0:T(8,128)(2,1)S(1)}, bf16[3072,512]{1,0:T(8,128)(2,1)}, u32[]{:S(2)}) %copy-start.4) | copy-done | bytes 3145752
  12.3 3.5 %collective-permute-start.8 = (bf16[32,3072]{1,0:T(8,128)(2,1)S(1)}, bf16[32,3072]{1,0:T(8,128)(2,1)S(1)}, u32[]{:S(2)}, u32[]{:S(2)}) collective-permute-start(bf16[32,3072]{1,0:T(8,128)(2,1)S(1)} %collective-permute-done.1.refs_2_), channel_id=1, source_target_pairs={{0,56},{4,31},{8,48},{12,21},{1,57},{5,28},{9,49},{13,22},{2,58},{... | collective-permute-start | bytes 589832 | tf_op jit(solution)/shard_map/ppermute | solution.py:31
  19.0 3.8 %collective-permute-done.7.refs_6_ = bf16[32,3072]{1,0:T(8,128)(2,1)S(1)} collective-permute-done((bf16[32,3072]{1,0:T(8,128)(2,1)S(1)}, bf16[32,3072]{1,0:T(8,128)(2,1)S(1)}, u32[]{:S(2)}, u32[]{:S(2)}) %collective-permute-start.7) | collective-permute-done | bytes 196640 | tf_op jit(solution)/shard_map/ppermute | solution.py:31
  22.9 2.1 %collective-permute-done.6.refs_5_ = bf16[32,3072]{1,0:T(8,128)(2,1)S(1)} collective-permute-done((bf16[32,3072]{1,0:T(8,128)(2,1)S(1)}, bf16[32,3072]{1,0:T(8,128)(2,1)S(1)}, u32[]{:S(2)}, u32[]{:S(2)}) %collective-permute-start.6) | collective-permute-done | bytes 196640 | tf_op jit(solution)/shard_map/ppermute | solution.py:31
  26.3 3.4 %hidden_units.1 = (bf16[256,1024]{1,0:T(8,128)(2,1)S(1)}, f32[256,1024]{1,0:T(8,128)S(1)}, f32[256,1024]{1,0:T(8,128)S(1)}) custom-call(bf16[32,3072]{1,0:T(8,128)(2,1)S(1)} %get-tuple-element.48.refs_0_.refs_4_, bf16[32,3072]{1,0:T(8,128)(2,1)S(1)} %collective-permute-done.refs_1_, bf16[32,3072]{1,0:T(8,128)(2,1)S(1)} %collective-permute-done.1.refs_2_, ...), custom_call_target="tpu_custom_call" | custom-call | flops 3221225472 | bytes 12582912 | tf_op jit(solution)/shard_map/hidden_units/pallas_call | solution.py:125
  31.9 1.8 %slot_terms.1 = (bf16[32,3072]{1,0:T(8,128)(2,1)S(1)}, bf16[32,3072]{1,0:T(8,128)(2,1)S(1)}, bf16[32,3072]{1,0:T(8,128)(2,1)S(1)}, bf16[32,3072]{1,0:T(8,128)(2,...) custom-call(bf16[256,1024]{1,0:T(8,128)(2,1)S(1)} %get-tuple-element, ...), custom_call_target="tpu_custom_call" | custom-call | flops 1610612736 | bytes 6291456 | tf_op jit(solution)/shard_map/slot_terms/pallas_call | solution.py:153
  33.7 2.2 %collective-permute-start.10 = (bf16[32,3072]{1,0:T(8,128)(2,1)S(1)}, bf16[32,3072]{1,0:T(8,128)(2,1)S(1)}, u32[]{:S(2)}, u32[]{:S(2)}) collective-permute-start(bf16[32,3072]{1,0:T(8,128)(2,1)S(1)} %get-tuple-element.61), channel_id=1, source_target_pairs={{0,48},{4,20},{8,56},{12,28},{1,49},{5,21},{9,57},{13,29},{2,50},{... | collective-permute-start | bytes 589832 | tf_op jit(solution)/shard_map/ppermute | solution.py:31
  36.0 2.1 %collective-permute-start.14 = (bf16[32,3072]{1,0:T(8,128)(2,1)S(1)}, bf16[32,3072]{1,0:T(8,128)(2,1)S(1)}, u32[]{:S(2)}, u32[]{:S(2)}) collective-permute-start(bf16[32,3072]{1,0:T(8,128)(2,1)S(1)} %get-tuple-element.66), channel_id=1, source_target_pairs={{0,8},{4,15},{8,0},{12,5},{1,9},{5,12},{9,1},{13,6},{2,10},{6,13},... | collective-permute-start | bytes 589832 | tf_op jit(solution)/shard_map/ppermute | solution.py:31
  39.5 2.1 %collective-permute-done.12 = bf16[32,3072]{1,0:T(8,128)(2,1)S(1)} collective-permute-done((bf16[32,3072]{1,0:T(8,128)(2,1)S(1)}, bf16[32,3072]{1,0:T(8,128)(2,1)S(1)}, u32[]{:S(2)}, u32[]{:S(2)}) %collective-permute-start.12) | collective-permute-done | bytes 196640 | tf_op jit(solution)/shard_map/ppermute | solution.py:31
  43.7 2.1 %collective-permute-done.15 = bf16[32,3072]{1,0:T(8,128)(2,1)S(1)} collective-permute-done((bf16[32,3072]{1,0:T(8,128)(2,1)S(1)}, bf16[32,3072]{1,0:T(8,128)(2,1)S(1)}, u32[]{:S(2)}, u32[]{:S(2)}) %collective-permute-start.15) | collective-permute-done | bytes 196640 | tf_op jit(solution)/shard_map/ppermute | solution.py:31
  45.9 1.6 %collective-permute-start.16 = (bf16[32,3072]{1,0:T(8,128)(2,1)S(1)}, bf16[32,3072]{1,0:T(8,128)(2,1)S(1)}, u32[]{:S(2)}, u32[]{:S(2)}) collective-permute-start(bf16[32,3072]{1,0:T(8,128)(2,1)S(1)} %add_convert_fusion.3), channel_id=1, source_target_pairs={{0,16},{4,52},{8,24},{12,60},{1,17},{5,53},{9,25},{13,61},{2,18},{... | collective-permute-start | bytes 589832 | tf_op jit(solution)/shard_map/ppermute | solution.py:31
  47.9 5.0 %collective-permute-done.16.refs_3_ = bf16[32,3072]{1,0:T(8,128)(2,1)S(1)} collective-permute-done((bf16[32,3072]{1,0:T(8,128)(2,1)S(1)}, bf16[32,3072]{1,0:T(8,128)(2,1)S(1)}, u32[]{:S(2)}, u32[]{:S(2)}) %collective-permute-start.16) | collective-permute-done | bytes 196640 | tf_op jit(solution)/shard_map/ppermute | solution.py:31
  53.6 2.0 %collective-permute-start.17 = (bf16[32,3200]{1,0:T(8,128)(2,1)S(1)}, bf16[32,3200]{1,0:T(8,128)(2,1)S(1)}, u32[]{:S(2)}, u32[]{:S(2)}) collective-permute-start(bf16[32,3200]{1,0:T(8,128)(2,1)S(1)} %get-tuple-element.73.refs_4_.refs_0_), channel_id=1, source_target_pairs={{0,16},{4,52},{8,24},{12,60},{1,17},{5,53},{9,25},{13,61},{2,18},{... | collective-permute-start | bytes 614408 | tf_op jit(solution)/shard_map/ppermute | solution.py:31
  56.9 3.8 %collective-permute-done.17.refs_5_.refs_1_ = bf16[32,3200]{1,0:T(8,128)(2,1)S(1)} collective-permute-done((bf16[32,3200]{1,0:T(8,128)(2,1)S(1)}, bf16[32,3200]{1,0:T(8,128)(2,1)S(1)}, u32[]{:S(2)}, u32[]{:S(2)}) %collective-permute-start.17) | collective-permute-done | bytes 204832 | tf_op jit(solution)/shard_map/ppermute | solution.py:31
  61.5 1.9 %collective-permute-start.21 = (bf16[32,3200]{1,0:T(8,128)(2,1)S(1)}, bf16[32,3200]{1,0:T(8,128)(2,1)S(1)}, u32[]{:S(2)}, u32[]{:S(2)}) collective-permute-start(bf16[32,3200]{1,0:T(8,128)(2,1)S(1)} %collective-permute-done.17.refs_5_.refs_1_), channel_id=1, source_target_pairs={{0,8},{4,15},{8,0},{12,5},{1,9},{5,12},{9,1},{13,6},{2,10},{6,13},... | collective-permute-start | bytes 614408 | tf_op jit(solution)/shard_map/ppermute | solution.py:31
  63.4 2.3 %collective-permute-start.23 = (bf16[32,3200]{1,0:T(8,128)(2,1)S(1)}, bf16[32,3200]{1,0:T(8,128)(2,1)S(1)}, u32[]{:S(2)}, u32[]{:S(2)}) collective-permute-start(bf16[32,3200]{1,0:T(8,128)(2,1)S(1)} %collective-permute-done.18.refs_6_.refs_2_), channel_id=1, source_target_pairs={{0,56},{4,31},{8,48},{12,21},{1,57},{5,28},{9,49},{13,22},{2,58},{... | collective-permute-start | bytes 614408 | tf_op jit(solution)/shard_map/ppermute | solution.py:31
  65.7 1.7 %collective-permute-start.22 = (bf16[32,3200]{1,0:T(8,128)(2,1)S(1)}, bf16[32,3200]{1,0:T(8,128)(2,1)S(1)}, u32[]{:S(2)}, u32[]{:S(2)}) collective-permute-start(bf16[32,3200]{1,0:T(8,128)(2,1)S(1)} %collective-permute-done.18.refs_6_.refs_2_), channel_id=1, source_target_pairs={{0,8},{4,15},{8,0},{12,5},{1,9},{5,12},{9,1},{13,6},{2,10},{6,13},... | collective-permute-start | bytes 614408 | tf_op jit(solution)/shard_map/ppermute | solution.py:31
  69.6 1.6 %collective-permute-start.25 = (f32[8,3200]{1,0:T(8,128)S(1)}, f32[8,3200]{1,0:T(8,128)S(1)}, u32[]{:S(2)}, u32[]{:S(2)}) collective-permute-start(f32[8,3200]{1,0:T(8,128)S(1)} %add.67), channel_id=1, source_target_pairs={{0,64},{64,0},{128,192},{192,128},{1,65},{65,1},{129,193},{193,129... | collective-permute-start | bytes 307208 | tf_op jit(solution)/shard_map/ppermute | solution.py:415
  71.3 2.4 %collective-permute-done.22.refs_6_ = bf16[32,3200]{1,0:T(8,128)(2,1)S(1)} collective-permute-done((bf16[32,3200]{1,0:T(8,128)(2,1)S(1)}, bf16[32,3200]{1,0:T(8,128)(2,1)S(1)}, u32[]{:S(2)}, u32[]{:S(2)}) %collective-permute-start.22) | collective-permute-done | bytes 204832 | tf_op jit(solution)/shard_map/ppermute | solution.py:31
  73.8 2.1 %hidden_grads.1 = (bf16[256,1024]{1,0:T(8,128)(2,1)S(1)}, bf16[256,1024]{1,0:T(8,128)(2,1)S(1)}) custom-call(bf16[32,3200]{1,0:T(8,128)(2,1)S(1)} %get-tuple-element.73.refs_4_.refs_0_, bf16[32,3200]{1,0:T(8,128)(2,1)S(1)} %collective-permute-done.17.refs_5_.refs_1_, bf16[32,3200]{1,0:T(8,128)(2,1)S(1)} %collective-permute-done.18.refs_6_.refs_2_, ...), custom_call_target="tpu_custom_call" | custom-call | flops 1610612736 | bytes 6291456 | tf_op jit(solution)/shard_map/hidden_grads/pallas_call | solution.py:182
  75.9 3.4 %slot_grads.1 = (bf16[32,3072]{1,0:T(8,128)(2,1)S(1)}, bf16[32,3072]{1,0:T(8,128)(2,1)S(1)}, bf16[32,3072]{1,0:T(8,128)(2,1)S(1)}, bf16[32,3072]{1,0:T(8,128)(2,...) custom-call(bf16[256,1024]{1,0:T(8,128)(2,1)S(1)} %get-tuple-element, ...), custom_call_target="tpu_custom_call" | custom-call | flops 3221225472 | bytes 12582912 | tf_op jit(solution)/shard_map/slot_grads/pallas_call | solution.py:214
  79.3 2.6 %collective-permute-start.26 = (bf16[32,3072]{1,0:T(8,128)(2,1)S(1)}, bf16[32,3072]{1,0:T(8,128)(2,1)S(1)}, u32[]{:S(2)}, u32[]{:S(2)}) collective-permute-start(bf16[32,3072]{1,0:T(8,128)(2,1)S(1)} %get-tuple-element.84), channel_id=1, source_target_pairs={{0,48},{4,20},{8,56},{12,28},{1,49},{5,21},{9,57},{13,29},{2,50},{... | collective-permute-start | bytes 589832 | tf_op jit(solution)/shard_map/ppermute | solution.py:31
  82.3 1.7 %collective-permute-start.30 = (bf16[32,3072]{1,0:T(8,128)(2,1)S(1)}, bf16[32,3072]{1,0:T(8,128)(2,1)S(1)}, u32[]{:S(2)}, u32[]{:S(2)}) collective-permute-start(bf16[32,3072]{1,0:T(8,128)(2,1)S(1)} %get-tuple-element.89), channel_id=1, source_target_pairs={{0,8},{4,15},{8,0},{12,5},{1,9},{5,12},{9,1},{13,6},{2,10},{6,13},... | collective-permute-start | bytes 589832 | tf_op jit(solution)/shard_map/ppermute | solution.py:31
  85.5 2.1 %collective-permute-done.28 = bf16[32,3072]{1,0:T(8,128)(2,1)S(1)} collective-permute-done((bf16[32,3072]{1,0:T(8,128)(2,1)S(1)}, bf16[32,3072]{1,0:T(8,128)(2,1)S(1)}, u32[]{:S(2)}, u32[]{:S(2)}) %collective-permute-start.28) | collective-permute-done | bytes 196640 | tf_op jit(solution)/shard_map/ppermute | solution.py:31
  87.7 1.6 %collective-permute-start.29 = (bf16[32,3072]{1,0:T(8,128)(2,1)S(1)}, bf16[32,3072]{1,0:T(8,128)(2,1)S(1)}, u32[]{:S(2)}, u32[]{:S(2)}) collective-permute-start(bf16[32,3072]{1,0:T(8,128)(2,1)S(1)} %add_convert_fusion.2), channel_id=1, source_target_pairs={{0,48},{4,20},{8,56},{12,28},{1,49},{5,21},{9,57},{13,29},{2,50},{... | collective-permute-start | bytes 589832 | tf_op jit(solution)/shard_map/ppermute | solution.py:31
  89.7 2.0 %collective-permute-done.31 = bf16[32,3072]{1,0:T(8,128)(2,1)S(1)} collective-permute-done((bf16[32,3072]{1,0:T(8,128)(2,1)S(1)}, bf16[32,3072]{1,0:T(8,128)(2,1)S(1)}, u32[]{:S(2)}, u32[]{:S(2)}) %collective-permute-start.31) | collective-permute-done | bytes 196640 | tf_op jit(solution)/shard_map/ppermute | solution.py:31
  91.8 1.7 %collective-permute-start.32 = (bf16[32,3072]{1,0:T(8,128)(2,1)S(1)}, bf16[32,3072]{1,0:T(8,128)(2,1)S(1)}, u32[]{:S(2)}, u32[]{:S(2)}) collective-permute-start(bf16[32,3072]{1,0:T(8,128)(2,1)S(1)} %add_convert_fusion.1), channel_id=1, source_target_pairs={{0,16},{4,52},{8,24},{12,60},{1,17},{5,53},{9,25},{13,61},{2,18},{... | collective-permute-start | bytes 589832 | tf_op jit(solution)/shard_map/ppermute | solution.py:31
  93.9 6.3 %collective-permute-done.33 = f32[8,3200]{1,0:T(8,128)S(1)} collective-permute-done((f32[8,3200]{1,0:T(8,128)S(1)}, f32[8,3200]{1,0:T(8,128)S(1)}, u32[]{:S(2)}, u32[]{:S(2)}) %collective-permute-start.33) | collective-permute-done | bytes 102432 | tf_op jit(solution)/shard_map/ppermute | solution.py:419
  101.6 3.3 %collective-permute-done.34 = f32[8,3200]{1,0:T(8,128)S(1)} collective-permute-done((f32[8,3200]{1,0:T(8,128)S(1)}, f32[8,3200]{1,0:T(8,128)S(1)}, u32[]{:S(2)}, u32[]{:S(2)}) %collective-permute-start.34) | collective-permute-done | bytes 102432 | tf_op jit(solution)/shard_map/ppermute | solution.py:31
  (95 shorter events, 24.4 us)
Async XLA Ops:
  2.8 14.3 %collective-permute-start.2 = (bf16[3072,512]{1,0:T(8,128)(2,1)}, bf16[3072,512]{1,0:T(8,128)(2,1)S(1)}, u32[]{:S(2)}, u32[]{:S(2)}) collective-permute-start(bf16[3072,512]{1,0:T(8,128)(2,1)} %gate), channel_id=1, source_target_pairs={{0,4},{4,0},{8,12},{12,8},{1,5},{5,1},{9,13},{13,9},{2,6},{6,2},{1... | collective-permute-start | bytes 9437192 | tf_op jit(solution)/shard_map/ppermute | solution.py:31
  2.9 14.2 %collective-permute-start.3 = (bf16[3072,512]{1,0:T(8,128)(2,1)}, bf16[3072,512]{1,0:T(8,128)(2,1)S(1)}, u32[]{:S(2)}, u32[]{:S(2)}) collective-permute-start(bf16[3072,512]{1,0:T(8,128)(2,1)} %up.1), channel_id=1, source_target_pairs={{0,4},{4,0},{8,12},{12,8},{1,5},{5,1},{9,13},{13,9},{2,6},{6,2},{1... | collective-permute-start | bytes 9437192 | tf_op jit(solution)/shard_map/ppermute | solution.py:31
  3.4 8.9 %collective-permute-start.1 = (bf16[32,3072]{1,0:T(8,128)(2,1)S(1)}, bf16[32,3072]{1,0:T(8,128)(2,1)S(1)}, u32[]{:S(2)}, u32[]{:S(2)}) collective-permute-start(bf16[32,3072]{1,0:T(8,128)(2,1)S(1)} %get-tuple-element.48.refs_0_.refs_4_), channel_id=1, source_target_pairs={{0,48},{4,20},{8,56},{12,28},{1,49},{5,21},{9,57},{13,29},{2,50},{... | collective-permute-start | bytes 589832 | tf_op jit(solution)/shard_map/ppermute | solution.py:31
  6.2 9.7 %collective-permute-start = (bf16[32,3072]{1,0:T(8,128)(2,1)S(1)}, bf16[32,3072]{1,0:T(8,128)(2,1)S(1)}, u32[]{:S(2)}, u32[]{:S(2)}) collective-permute-start(bf16[32,3072]{1,0:T(8,128)(2,1)S(1)} %get-tuple-element.48.refs_0_.refs_4_), channel_id=1, source_target_pairs={{0,16},{4,52},{8,24},{12,60},{1,17},{5,53},{9,25},{13,61},{2,18},{... | collective-permute-start | bytes 589832 | tf_op jit(solution)/shard_map/ppermute | solution.py:31
  6.2 11.7 %collective-permute-start.5 = (bf16[32,3072]{1,0:T(8,128)(2,1)S(1)}, bf16[32,3072]{1,0:T(8,128)(2,1)S(1)}, u32[]{:S(2)}, u32[]{:S(2)}) collective-permute-start(bf16[32,3072]{1,0:T(8,128)(2,1)S(1)} %get-tuple-element.48.refs_0_.refs_4_), channel_id=1, source_target_pairs={{0,8},{4,15},{8,0},{12,5},{1,9},{5,12},{9,1},{13,6},{2,10},{6,13},... | collective-permute-start | bytes 589832 | tf_op jit(solution)/shard_map/ppermute | solution.py:31
  12.3 6.7 %collective-permute-start.8 = (bf16[32,3072]{1,0:T(8,128)(2,1)S(1)}, bf16[32,3072]{1,0:T(8,128)(2,1)S(1)}, u32[]{:S(2)}, u32[]{:S(2)}) collective-permute-start(bf16[32,3072]{1,0:T(8,128)(2,1)S(1)} %collective-permute-done.1.refs_2_), channel_id=1, source_target_pairs={{0,56},{4,31},{8,48},{12,21},{1,57},{5,28},{9,49},{13,22},{2,58},{... | collective-permute-start | bytes 589832 | tf_op jit(solution)/shard_map/ppermute | solution.py:31
  15.9 7.0 %collective-permute-start.7 = (bf16[32,3072]{1,0:T(8,128)(2,1)S(1)}, bf16[32,3072]{1,0:T(8,128)(2,1)S(1)}, u32[]{:S(2)}, u32[]{:S(2)}) collective-permute-start(bf16[32,3072]{1,0:T(8,128)(2,1)S(1)} %collective-permute-done.1.refs_2_), channel_id=1, source_target_pairs={{0,8},{4,15},{8,0},{12,5},{1,9},{5,12},{9,1},{13,6},{2,10},{6,13},... | collective-permute-start | bytes 589832 | tf_op jit(solution)/shard_map/ppermute | solution.py:31
  17.1 7.8 %collective-permute-start.6 = (bf16[32,3072]{1,0:T(8,128)(2,1)S(1)}, bf16[32,3072]{1,0:T(8,128)(2,1)S(1)}, u32[]{:S(2)}, u32[]{:S(2)}) collective-permute-start(bf16[32,3072]{1,0:T(8,128)(2,1)S(1)} %collective-permute-done.refs_1_), channel_id=1, source_target_pairs={{0,8},{4,15},{8,0},{12,5},{1,9},{5,12},{9,1},{13,6},{2,10},{6,13},... | collective-permute-start | bytes 589832 | tf_op jit(solution)/shard_map/ppermute | solution.py:31
  17.9 8.3 %collective-permute-start.4 = (bf16[32,3072]{1,0:T(8,128)(2,1)S(1)}, bf16[32,3072]{1,0:T(8,128)(2,1)S(1)}, u32[]{:S(2)}, u32[]{:S(2)}) collective-permute-start(bf16[32,3072]{1,0:T(8,128)(2,1)S(1)} %collective-permute-done.refs_1_), channel_id=1, source_target_pairs={{0,16},{4,52},{8,24},{12,60},{1,17},{5,53},{9,25},{13,61},{2,18},{... | collective-permute-start | bytes 589832 | tf_op jit(solution)/shard_map/ppermute | solution.py:31
  33.7 5.7 %collective-permute-start.10 = (bf16[32,3072]{1,0:T(8,128)(2,1)S(1)}, bf16[32,3072]{1,0:T(8,128)(2,1)S(1)}, u32[]{:S(2)}, u32[]{:S(2)}) collective-permute-start(bf16[32,3072]{1,0:T(8,128)(2,1)S(1)} %get-tuple-element.61), channel_id=1, source_target_pairs={{0,48},{4,20},{8,56},{12,28},{1,49},{5,21},{9,57},{13,29},{2,50},{... | collective-permute-start | bytes 589832 | tf_op jit(solution)/shard_map/ppermute | solution.py:31
  35.9 5.7 %collective-permute-start.12 = (bf16[32,3072]{1,0:T(8,128)(2,1)S(1)}, bf16[32,3072]{1,0:T(8,128)(2,1)S(1)}, u32[]{:S(2)}, u32[]{:S(2)}) collective-permute-start(bf16[32,3072]{1,0:T(8,128)(2,1)S(1)} %get-tuple-element.64), channel_id=1, source_target_pairs={{0,8},{4,15},{8,0},{12,5},{1,9},{5,12},{9,1},{13,6},{2,10},{6,13},... | collective-permute-start | bytes 589832 | tf_op jit(solution)/shard_map/ppermute | solution.py:31
  36.0 7.7 %collective-permute-start.14 = (bf16[32,3072]{1,0:T(8,128)(2,1)S(1)}, bf16[32,3072]{1,0:T(8,128)(2,1)S(1)}, u32[]{:S(2)}, u32[]{:S(2)}) collective-permute-start(bf16[32,3072]{1,0:T(8,128)(2,1)S(1)} %get-tuple-element.66), channel_id=1, source_target_pairs={{0,8},{4,15},{8,0},{12,5},{1,9},{5,12},{9,1},{13,6},{2,10},{6,13},... | collective-permute-start | bytes 589832 | tf_op jit(solution)/shard_map/ppermute | solution.py:31
  38.0 7.8 %collective-permute-start.15 = (bf16[32,3072]{1,0:T(8,128)(2,1)S(1)}, bf16[32,3072]{1,0:T(8,128)(2,1)S(1)}, u32[]{:S(2)}, u32[]{:S(2)}) collective-permute-start(bf16[32,3072]{1,0:T(8,128)(2,1)S(1)} %get-tuple-element.67), channel_id=1, source_target_pairs={{0,24},{4,63},{8,16},{12,53},{1,25},{5,60},{9,17},{13,54},{2,26},{... | collective-permute-start | bytes 589832 | tf_op jit(solution)/shard_map/ppermute | solution.py:31
  39.5 8.4 %collective-permute-start.11 = (bf16[32,3072]{1,0:T(8,128)(2,1)S(1)}, bf16[32,3072]{1,0:T(8,128)(2,1)S(1)}, u32[]{:S(2)}, u32[]{:S(2)}) collective-permute-start(bf16[32,3072]{1,0:T(8,128)(2,1)S(1)} %get-tuple-element.62), channel_id=1, source_target_pairs={{0,8},{4,15},{8,0},{12,5},{1,9},{5,12},{9,1},{13,6},{2,10},{6,13},... | collective-permute-start | bytes 589832 | tf_op jit(solution)/shard_map/ppermute | solution.py:31
  41.7 6.2 %collective-permute-start.13 = (bf16[32,3072]{1,0:T(8,128)(2,1)S(1)}, bf16[32,3072]{1,0:T(8,128)(2,1)S(1)}, u32[]{:S(2)}, u32[]{:S(2)}) collective-permute-start(bf16[32,3072]{1,0:T(8,128)(2,1)S(1)} %add_convert_fusion.4), channel_id=1, source_target_pairs={{0,48},{4,20},{8,56},{12,28},{1,49},{5,21},{9,57},{13,29},{2,50},{... | collective-permute-start | bytes 589832 | tf_op jit(solution)/shard_map/ppermute | solution.py:31
  45.9 7.0 %collective-permute-start.16 = (bf16[32,3072]{1,0:T(8,128)(2,1)S(1)}, bf16[32,3072]{1,0:T(8,128)(2,1)S(1)}, u32[]{:S(2)}, u32[]{:S(2)}) collective-permute-start(bf16[32,3072]{1,0:T(8,128)(2,1)S(1)} %add_convert_fusion.3), channel_id=1, source_target_pairs={{0,16},{4,52},{8,24},{12,60},{1,17},{5,53},{9,25},{13,61},{2,18},{... | collective-permute-start | bytes 589832 | tf_op jit(solution)/shard_map/ppermute | solution.py:31
  53.6 9.9 %collective-permute-start.18 = (bf16[32,3200]{1,0:T(8,128)(2,1)S(1)}, bf16[32,3200]{1,0:T(8,128)(2,1)S(1)}, u32[]{:S(2)}, u32[]{:S(2)}) collective-permute-start(bf16[32,3200]{1,0:T(8,128)(2,1)S(1)} %get-tuple-element.73.refs_4_.refs_0_), channel_id=1, source_target_pairs={{0,48},{4,20},{8,56},{12,28},{1,49},{5,21},{9,57},{13,29},{2,50},{... | collective-permute-start | bytes 614408 | tf_op jit(solution)/shard_map/ppermute | solution.py:31
  53.6 7.0 %collective-permute-start.17 = (bf16[32,3200]{1,0:T(8,128)(2,1)S(1)}, bf16[32,3200]{1,0:T(8,128)(2,1)S(1)}, u32[]{:S(2)}, u32[]{:S(2)}) collective-permute-start(bf16[32,3200]{1,0:T(8,128)(2,1)S(1)} %get-tuple-element.73.refs_4_.refs_0_), channel_id=1, source_target_pairs={{0,16},{4,52},{8,24},{12,60},{1,17},{5,53},{9,25},{13,61},{2,18},{... | collective-permute-start | bytes 614408 | tf_op jit(solution)/shard_map/ppermute | solution.py:31
  60.7 7.0 %collective-permute-start.19 = (bf16[32,3200]{1,0:T(8,128)(2,1)S(1)}, bf16[32,3200]{1,0:T(8,128)(2,1)S(1)}, u32[]{:S(2)}, u32[]{:S(2)}) collective-permute-start(bf16[32,3200]{1,0:T(8,128)(2,1)S(1)} %collective-permute-done.17.refs_5_.refs_1_), channel_id=1, source_target_pairs={{0,16},{4,52},{8,24},{12,60},{1,17},{5,53},{9,25},{13,61},{2,18},{... | collective-permute-start | bytes 614408 | tf_op jit(solution)/shard_map/ppermute | solution.py:31
  61.4 9.7 %collective-permute-start.20 = (bf16[32,3200]{1,0:T(8,128)(2,1)S(1)}, bf16[32,3200]{1,0:T(8,128)(2,1)S(1)}, u32[]{:S(2)}, u32[]{:S(2)}) collective-permute-start(bf16[32,3200]{1,0:T(8,128)(2,1)S(1)} %get-tuple-element.73.refs_4_.refs_0_), channel_id=1, source_target_pairs={{0,8},{4,15},{8,0},{12,5},{1,9},{5,12},{9,1},{13,6},{2,10},{6,13},... | collective-permute-start | bytes 614408 | tf_op jit(solution)/shard_map/ppermute | solution.py:31
  61.5 9.7 %collective-permute-start.21 = (bf16[32,3200]{1,0:T(8,128)(2,1)S(1)}, bf16[32,3200]{1,0:T(8,128)(2,1)S(1)}, u32[]{:S(2)}, u32[]{:S(2)}) collective-permute-start(bf16[32,3200]{1,0:T(8,128)(2,1)S(1)} %collective-permute-done.17.refs_5_.refs_1_), channel_id=1, source_target_pairs={{0,8},{4,15},{8,0},{12,5},{1,9},{5,12},{9,1},{13,6},{2,10},{6,13},... | collective-permute-start | bytes 614408 | tf_op jit(solution)/shard_map/ppermute | solution.py:31
  63.4 7.9 %collective-permute-start.23 = (bf16[32,3200]{1,0:T(8,128)(2,1)S(1)}, bf16[32,3200]{1,0:T(8,128)(2,1)S(1)}, u32[]{:S(2)}, u32[]{:S(2)}) collective-permute-start(bf16[32,3200]{1,0:T(8,128)(2,1)S(1)} %collective-permute-done.18.refs_6_.refs_2_), channel_id=1, source_target_pairs={{0,56},{4,31},{8,48},{12,21},{1,57},{5,28},{9,49},{13,22},{2,58},{... | collective-permute-start | bytes 614408 | tf_op jit(solution)/shard_map/ppermute | solution.py:31
  65.7 8.0 %collective-permute-start.22 = (bf16[32,3200]{1,0:T(8,128)(2,1)S(1)}, bf16[32,3200]{1,0:T(8,128)(2,1)S(1)}, u32[]{:S(2)}, u32[]{:S(2)}) collective-permute-start(bf16[32,3200]{1,0:T(8,128)(2,1)S(1)} %collective-permute-done.18.refs_6_.refs_2_), channel_id=1, source_target_pairs={{0,8},{4,15},{8,0},{12,5},{1,9},{5,12},{9,1},{13,6},{2,10},{6,13},... | collective-permute-start | bytes 614408 | tf_op jit(solution)/shard_map/ppermute | solution.py:31
  69.6 6.3 %collective-permute-start.25 = (f32[8,3200]{1,0:T(8,128)S(1)}, f32[8,3200]{1,0:T(8,128)S(1)}, u32[]{:S(2)}, u32[]{:S(2)}) collective-permute-start(f32[8,3200]{1,0:T(8,128)S(1)} %add.67), channel_id=1, source_target_pairs={{0,64},{64,0},{128,192},{192,128},{1,65},{65,1},{129,193},{193,129... | collective-permute-start | bytes 307208 | tf_op jit(solution)/shard_map/ppermute | solution.py:415
  79.3 5.8 %collective-permute-start.26 = (bf16[32,3072]{1,0:T(8,128)(2,1)S(1)}, bf16[32,3072]{1,0:T(8,128)(2,1)S(1)}, u32[]{:S(2)}, u32[]{:S(2)}) collective-permute-start(bf16[32,3072]{1,0:T(8,128)(2,1)S(1)} %get-tuple-element.84), channel_id=1, source_target_pairs={{0,48},{4,20},{8,56},{12,28},{1,49},{5,21},{9,57},{13,29},{2,50},{... | collective-permute-start | bytes 589832 | tf_op jit(solution)/shard_map/ppermute | solution.py:31
  81.9 5.7 %collective-permute-start.28 = (bf16[32,3072]{1,0:T(8,128)(2,1)S(1)}, bf16[32,3072]{1,0:T(8,128)(2,1)S(1)}, u32[]{:S(2)}, u32[]{:S(2)}) collective-permute-start(bf16[32,3072]{1,0:T(8,128)(2,1)S(1)} %get-tuple-element.87), channel_id=1, source_target_pairs={{0,8},{4,15},{8,0},{12,5},{1,9},{5,12},{9,1},{13,6},{2,10},{6,13},... | collective-permute-start | bytes 589832 | tf_op jit(solution)/shard_map/ppermute | solution.py:31
  82.3 7.4 %collective-permute-start.30 = (bf16[32,3072]{1,0:T(8,128)(2,1)S(1)}, bf16[32,3072]{1,0:T(8,128)(2,1)S(1)}, u32[]{:S(2)}, u32[]{:S(2)}) collective-permute-start(bf16[32,3072]{1,0:T(8,128)(2,1)S(1)} %get-tuple-element.89), channel_id=1, source_target_pairs={{0,8},{4,15},{8,0},{12,5},{1,9},{5,12},{9,1},{13,6},{2,10},{6,13},... | collective-permute-start | bytes 589832 | tf_op jit(solution)/shard_map/ppermute | solution.py:31
  84.0 7.8 %collective-permute-start.31 = (bf16[32,3072]{1,0:T(8,128)(2,1)S(1)}, bf16[32,3072]{1,0:T(8,128)(2,1)S(1)}, u32[]{:S(2)}, u32[]{:S(2)}) collective-permute-start(bf16[32,3072]{1,0:T(8,128)(2,1)S(1)} %get-tuple-element.90), channel_id=1, source_target_pairs={{0,24},{4,63},{8,16},{12,53},{1,25},{5,60},{9,17},{13,54},{2,26},{... | collective-permute-start | bytes 589832 | tf_op jit(solution)/shard_map/ppermute | solution.py:31
  85.1 15.1 %collective-permute-start.27 = (bf16[32,3072]{1,0:T(8,128)(2,1)S(1)}, bf16[32,3072]{1,0:T(8,128)(2,1)S(1)}, u32[]{:S(2)}, u32[]{:S(2)}) collective-permute-start(bf16[32,3072]{1,0:T(8,128)(2,1)S(1)} %get-tuple-element.85), channel_id=1, source_target_pairs={{0,8},{4,15},{8,0},{12,5},{1,9},{5,12},{9,1},{13,6},{2,10},{6,13},... | collective-permute-start | bytes 589832 | tf_op jit(solution)/shard_map/ppermute | solution.py:31
  87.7 12.6 %collective-permute-start.29 = (bf16[32,3072]{1,0:T(8,128)(2,1)S(1)}, bf16[32,3072]{1,0:T(8,128)(2,1)S(1)}, u32[]{:S(2)}, u32[]{:S(2)}) collective-permute-start(bf16[32,3072]{1,0:T(8,128)(2,1)S(1)} %add_convert_fusion.2), channel_id=1, source_target_pairs={{0,48},{4,20},{8,56},{12,28},{1,49},{5,21},{9,57},{13,29},{2,50},{... | collective-permute-start | bytes 589832 | tf_op jit(solution)/shard_map/ppermute | solution.py:31
  91.8 8.5 %collective-permute-start.32 = (bf16[32,3072]{1,0:T(8,128)(2,1)S(1)}, bf16[32,3072]{1,0:T(8,128)(2,1)S(1)}, u32[]{:S(2)}, u32[]{:S(2)}) collective-permute-start(bf16[32,3072]{1,0:T(8,128)(2,1)S(1)} %add_convert_fusion.1), channel_id=1, source_target_pairs={{0,16},{4,52},{8,24},{12,60},{1,17},{5,53},{9,25},{13,61},{2,18},{... | collective-permute-start | bytes 589832 | tf_op jit(solution)/shard_map/ppermute | solution.py:31
  93.5 6.6 %collective-permute-start.33 = (f32[8,3200]{1,0:T(8,128)S(1)}, f32[8,3200]{1,0:T(8,128)S(1)}, u32[]{:S(2)}, u32[]{:S(2)}) collective-permute-start(f32[8,3200]{1,0:T(8,128)S(1)} %add.68), channel_id=1, source_target_pairs={{0,128},{64,192},{128,0},{192,64},{1,129},{65,193},{129,1},{193,65... | collective-permute-start | bytes 307208 | tf_op jit(solution)/shard_map/ppermute | solution.py:419
  (13 other events, 50.1 us)
